TPU v7x, 128 devices: a whole 4x4x4 slice. The times are simulated.
128 devices in a mesh: dp: 32 (over x_lo, y, z), tensor: 4 (over x_hi, core).
Axes of the slice: x: 4 (x_hi: 2, x_lo: 2; x = x_hi * 2 + x_lo), y: 4, z: 4, core: 2. Of those that a mesh axis runs over, the one named last changes fastest.
Arguments:
- tokens_in: bfloat16 [150528, 384], P('dp'), may hold values from -6 to 6
- attn_gain: bfloat16 [384], replicated, may hold values from 0.5 to 1.5
- attn_shift: bfloat16 [384], replicated, may hold values from -1.25 to 1.25
- qkv_weight: bfloat16 [3, 384, 384], P(None, None, 'tensor'), may hold values from -0.3125 to 0.3125
- qv_bias: bfloat16 [2, 384], P(None, 'tensor'), may hold values from -1.25 to 1.25
- rel_table: bfloat16 [169, 12], P(None, 'tensor'), may hold values from -6 to 6
- proj_weight: bfloat16 [384, 384], P('tensor'), may hold values from -0.875 to 0.875
- proj_bias: bfloat16 [384], replicated, may hold values from -1.25 to 1.25
- moe_gain: bfloat16 [384], replicated, may hold values from 0.5 to 1.5
- moe_shift: bfloat16 [384], replicated, may hold values from -1.25 to 1.25
- router_weight: bfloat16 [384, 8], replicated, may hold values from -0.21875 to 0.21875
- expert_in: bfloat16 [8, 384, 1536], P(None, None, 'tensor'), may hold values from -0.3125 to 0.3125
- expert_in_bias: bfloat16 [8, 1536], P(None, 'tensor'), may hold values from -0.625 to 0.625
- expert_out: bfloat16 [8, 1536, 384], P(None, 'tensor'), may hold values from -1.25 to 1.25
- expert_out_bias: bfloat16 [8, 384], replicated, may hold values from -3 to 3
- expert_ids: int32 [150528, 1], P('dp'), may hold values from 0 to 7; in each aligned block of 4704 rows (0 to 4703, 4704 to 9407, ...) at most 735 rows name the same one
- cotangent: bfloat16 [150528, 384], P('dp'), may hold values from -6 to 6
Outputs:
- block_out: bfloat16 [150528, 384], P('dp')
- input_grad: float32 [150528, 384], P('dp')
- grad_attn_gain: float32 [384], replicated
- grad_attn_shift: float32 [384], replicated
- grad_qkv_weight: float32 [3, 384, 384], P(None, None, 'tensor')
- grad_qv_bias: float32 [2, 384], P(None, 'tensor')
- grad_rel_table: float32 [169, 12], P(None, 'tensor')
- grad_proj_weight: float32 [384, 384], P('tensor')
- grad_proj_bias: float32 [384], replicated
- grad_moe_gain: float32 [384], replicated
- grad_moe_shift: float32 [384], replicated
- grad_router: float32 [384, 8], replicated
- grad_expert_in: float32 [8, 384, 1536], P(None, None, 'tensor')
- grad_expert_in_bias: float32 [8, 1536], P(None, 'tensor')
- grad_expert_out: float32 [8, 1536, 384], P(None, 'tensor')
- grad_expert_out_bias: float32 [8, 384], replicated
Inputs may be any that keep to these rules, and one draw needn't show every extreme that they name: `expert_ids`: in each aligned block of 4704 rows (the tokens of one index of dp) no expert is named by more than 735 rows, and in some block one expert is named by exactly 735 rows.
All inputs are finite; a program needn't handle non-finite values.
Results may differ from a plain program's by a relative error of at most 0.012.
The roundings to bfloat16 on the way count: a program that leaves them out, or rounds other values in their place, can miss the bound.
Values sent between devices are 32-bit elements; how exact they have to be, the bound alone decides.
No kernel may reach another device: no remote copies, remote signals or barrier semaphores. Data moves between devices by JAX's collectives and lax.ppermute only.
A program may use at most 256 MiB of HBM per device.

v0:
```python
import math

import jax
import jax.numpy as jnp
from jax import lax
from jax.sharding import PartitionSpec as P

HEAD_DIM = 32
EXPERTS = 8
SIDE = 14
WINDOW = 7
IMAGE = 196


HIGHEST_MODE = lax.Precision.HIGHEST
MASK_FILL = -1e30


def region(coordinate):
    return (coordinate >= SIDE - WINDOW).astype(jnp.int32) + (
        coordinate >= SIDE - WINDOW // 2
    ).astype(jnp.int32)


def window_layout():
    cell_ids = jnp.arange(SIDE * SIDE, dtype=jnp.int32)
    offset = WINDOW // 2
    row_pos = (cell_ids // SIDE - offset) % SIDE
    col_pos = (cell_ids % SIDE - offset) % SIDE
    labels = (
        (row_pos // WINDOW * SIDE + col_pos // WINDOW) * 9 + region(row_pos) * 3 + region(col_pos)
    )
    allowed = labels[:, None] == labels[None, :]
    return (allowed, row_pos % WINDOW, col_pos % WINDOW)


def bias_tables():
    allowed, inner_row, inner_col = window_layout()
    spot_ids = jnp.arange(WINDOW * WINDOW, dtype=jnp.int32)
    spot_row = spot_ids // WINDOW
    spot_col = spot_ids % WINDOW
    pair_index = (
        (spot_row[:, None] - spot_row[None, :] + WINDOW - 1) * (2 * WINDOW - 1)
        + spot_col[:, None]
        - spot_col[None, :]
        + WINDOW
        - 1
    ).reshape(-1)
    lookup = (
        pair_index[:, None] == jnp.arange((2 * WINDOW - 1) ** 2, dtype=jnp.int32)[None, :]
    ).astype(jnp.float32)
    placing = ((inner_row * WINDOW + inner_col)[:, None] == spot_ids[None, :]).astype(jnp.float32)
    return (allowed, lookup, placing)


def norm_forward(values, gain_vec, shift_vec):
    centre = values - jnp.mean(values, axis=-1, keepdims=True)
    spread = jnp.mean(centre * centre, axis=-1, keepdims=True)
    inverse = lax.rsqrt(spread + 1e-05)
    unit_rows = centre * inverse
    return (unit_rows * gain_vec + shift_vec, unit_rows, inverse)


def norm_backward(upstream, unit_rows, inverse, gain_vec):
    scaled = upstream * gain_vec
    centred = (
        scaled
        - jnp.mean(scaled, axis=-1, keepdims=True)
        - unit_rows * jnp.mean(scaled * unit_rows, axis=-1, keepdims=True)
    )
    return (centred * inverse, jnp.sum(upstream * unit_rows, axis=0), jnp.sum(upstream, axis=0))


def gelu_parts(values):
    cdf_value = 0.5 * (1.0 + jax.scipy.special.erf(values * (1.0 / math.sqrt(2.0))))
    density = jnp.exp(-0.5 * values * values) * (1.0 / math.sqrt(2.0 * math.pi))
    return (values * cdf_value, cdf_value + values * density)


def shards(
    tokens_in,
    attn_gain,
    attn_shift,
    qkv_weight,
    qv_bias,
    rel_table,
    proj_weight,
    proj_bias,
    moe_gain,
    moe_shift,
    router_weight,
    expert_in,
    expert_in_bias,
    expert_out,
    expert_out_bias,
    expert_ids,
    cotangent,
):
    count_tok, features = tokens_in.shape
    images = count_tok // IMAGE
    local_heads = qv_bias.shape[1] // HEAD_DIM
    head_shape = (images, IMAGE, local_heads, HEAD_DIM)
    capacity = (5 * count_tok + 31) // 32
    score_scale = HEAD_DIM ** (-0.5)
    allowed, lookup, placing = bias_tables()
    window_bias = jnp.dot(
        lookup.astype(jnp.bfloat16), rel_table, preferred_element_type=jnp.float32
    ).reshape(WINDOW * WINDOW, WINDOW * WINDOW, local_heads)
    full_bias = jnp.einsum("ip,pqh,jq->hij", placing, window_bias, placing, precision=HIGHEST_MODE)
    tokens_wide = tokens_in.astype(jnp.float32)
    attn_gain_f = attn_gain.astype(jnp.float32)
    attn_in, attn_unit, attn_inverse = norm_forward(
        tokens_wide, attn_gain_f, attn_shift.astype(jnp.float32)
    )
    attn_low = attn_in.astype(jnp.bfloat16)
    projected = jnp.einsum("td,kdf->ktf", attn_low, qkv_weight, preferred_element_type=jnp.float32)
    bias_rows = jnp.stack([qv_bias[0], jnp.zeros_like(qv_bias[0]), qv_bias[1]]).astype(jnp.float32)
    qkv_low = (projected + bias_rows[:, None, :]).astype(jnp.bfloat16)
    query_heads = qkv_low[0].reshape(head_shape)
    key_heads = qkv_low[1].reshape(head_shape)
    value_heads = qkv_low[2].reshape(head_shape)

    def attention_scores():
        products = jnp.einsum(
            "bihd,bjhd->bhij", query_heads, key_heads, preferred_element_type=jnp.float32
        )
        return jnp.where(allowed, products * score_scale + full_bias[None], MASK_FILL)

    scores = attention_scores()
    row_max = jnp.max(scores, axis=-1, keepdims=True)
    powers = jnp.exp(scores - row_max)
    row_total = jnp.sum(powers, axis=-1, keepdims=True)
    attention = powers / row_total
    log_total = row_max + jnp.log(row_total)
    mixed_low = (
        jnp.einsum(
            "bhij,bjhd->bihd",
            attention.astype(jnp.bfloat16),
            value_heads,
            preferred_element_type=jnp.float32,
        )
        .astype(jnp.bfloat16)
        .reshape(count_tok, -1)
    )
    attn_part = jnp.dot(mixed_low, proj_weight, preferred_element_type=jnp.float32)
    attn_out = lax.psum(attn_part, "tensor") + proj_bias.astype(jnp.float32)
    hidden_one = tokens_wide + attn_out
    moe_gain_f = moe_gain.astype(jnp.float32)
    moe_in, moe_unit, moe_inverse = norm_forward(
        hidden_one, moe_gain_f, moe_shift.astype(jnp.float32)
    )
    second_low = moe_in.astype(jnp.bfloat16)
    second_wide = second_low.astype(jnp.float32)
    router_wide = router_weight.astype(jnp.float32)
    logits = jnp.dot(second_low, router_weight, preferred_element_type=jnp.float32)
    logit_max = jnp.max(logits, axis=-1, keepdims=True)
    logit_pow = jnp.exp(logits - logit_max)
    router_probs = logit_pow / jnp.sum(logit_pow, axis=-1, keepdims=True)
    chosen = expert_ids == jnp.arange(EXPERTS, dtype=jnp.int32)[None, :]
    chosen_wide = chosen.astype(jnp.float32)
    chosen_low = chosen.astype(jnp.bfloat16)
    gate_value = jnp.sum(jnp.where(chosen, router_probs, 0.0), axis=-1, keepdims=True)
    rank_run = jnp.cumsum(chosen.astype(jnp.int32), axis=0, dtype=jnp.int32) - 1
    slot_ids = jnp.sum(jnp.where(chosen, rank_run, 0), axis=-1, dtype=jnp.int32)
    position = expert_ids[:, 0] * capacity + slot_ids
    sources = (
        jnp.full((EXPERTS * capacity,), count_tok, jnp.int32)
        .at[position]
        .set(jnp.arange(count_tok, dtype=jnp.int32))
    )
    zero_row = jnp.zeros((1, features), jnp.bfloat16)
    buffer = jnp.concatenate([second_low, zero_row], axis=0)[sources].reshape(
        EXPERTS, capacity, features
    )
    preact = (
        jnp.einsum("ecd,edf->ecf", buffer, expert_in, preferred_element_type=jnp.float32)
        + expert_in_bias.astype(jnp.float32)[:, None, :]
    )
    activated, gelu_slope = gelu_parts(preact)
    act_low = activated.astype(jnp.bfloat16)
    expert_part = jnp.einsum(
        "ecf,efd->ecd", act_low, expert_out, preferred_element_type=jnp.float32
    )
    token_part = expert_part.reshape(EXPERTS * capacity, features)[position]
    out_bias_tok = jnp.dot(chosen_low, expert_out_bias, preferred_element_type=jnp.float32)
    expert_tok = lax.psum(token_part, "tensor") + out_bias_tok
    block_out = (hidden_one + gate_value * expert_tok).astype(jnp.bfloat16)
    upstream = cotangent.astype(jnp.float32)
    grad_gate = jnp.sum(upstream * expert_tok, axis=-1, keepdims=True)
    grad_tok = (gate_value * upstream).astype(jnp.bfloat16)
    grad_out_bias = jnp.dot(chosen_low.T, grad_tok, preferred_element_type=jnp.float32)
    grad_buffer = jnp.concatenate([grad_tok, zero_row], axis=0)[sources].reshape(
        EXPERTS, capacity, features
    )
    grad_out = jnp.einsum("ecf,ecd->efd", act_low, grad_buffer, preferred_element_type=jnp.float32)
    grad_act = jnp.einsum(
        "ecd,efd->ecf", grad_buffer, expert_out, preferred_element_type=jnp.float32
    )
    grad_pre = (grad_act * gelu_slope).astype(jnp.bfloat16)
    grad_in_bias = jnp.sum(grad_pre.astype(jnp.float32), axis=1)
    grad_in = jnp.einsum("ecd,ecf->edf", buffer, grad_pre, preferred_element_type=jnp.float32)
    grad_second_buf = jnp.einsum(
        "ecf,edf->ecd", grad_pre, expert_in, preferred_element_type=jnp.float32
    )
    grad_second_part = grad_second_buf.reshape(EXPERTS * capacity, features)[position]
    grad_logit = grad_gate * gate_value * (chosen_wide - router_probs)
    grad_router = jnp.dot(second_wide.T, grad_logit, precision=HIGHEST_MODE)
    grad_second = lax.psum(grad_second_part, "tensor") + jnp.dot(
        grad_logit, router_wide.T, precision=HIGHEST_MODE
    )
    moe_norm_grad, grad_moe_gain, grad_moe_shift = norm_backward(
        grad_second, moe_unit, moe_inverse, moe_gain_f
    )
    grad_hidden = upstream + moe_norm_grad
    grad_attn_low = grad_hidden.astype(jnp.bfloat16)
    grad_proj_bias = jnp.sum(grad_attn_low.astype(jnp.float32), axis=0)
    grad_proj = jnp.dot(mixed_low.T, grad_attn_low, preferred_element_type=jnp.float32)
    grad_mixed = jnp.dot(grad_attn_low, proj_weight.T, preferred_element_type=jnp.float32).astype(
        jnp.bfloat16
    )
    grad_heads = grad_mixed.reshape(head_shape)
    recomputed = jnp.exp(attention_scores() - log_total)
    grad_prob = jnp.einsum(
        "bihd,bjhd->bhij", grad_heads, value_heads, preferred_element_type=jnp.float32
    )
    grad_value = jnp.einsum(
        "bhij,bihd->bjhd",
        recomputed.astype(jnp.bfloat16),
        grad_heads,
        preferred_element_type=jnp.float32,
    ).astype(jnp.bfloat16)
    grad_score = recomputed * (grad_prob - jnp.sum(recomputed * grad_prob, axis=-1, keepdims=True))
    grad_pair = jnp.sum(grad_score, axis=0)
    grad_window = jnp.einsum(
        "ip,hij,jq->pqh", placing, grad_pair, placing, precision=HIGHEST_MODE
    ).reshape(WINDOW * WINDOW * WINDOW * WINDOW, local_heads)
    grad_table = jnp.dot(lookup.T, grad_window, precision=HIGHEST_MODE)
    grad_products = (grad_score * score_scale).astype(jnp.bfloat16)
    grad_query = jnp.einsum(
        "bhij,bjhd->bihd", grad_products, key_heads, preferred_element_type=jnp.float32
    ).astype(jnp.bfloat16)
    grad_key = jnp.einsum(
        "bhij,bihd->bjhd", grad_products, query_heads, preferred_element_type=jnp.float32
    ).astype(jnp.bfloat16)
    grad_qkv = jnp.stack(
        [
            grad_query.reshape(count_tok, -1),
            grad_key.reshape(count_tok, -1),
            grad_value.reshape(count_tok, -1),
        ]
    )
    grad_qkv_weight = jnp.einsum(
        "td,ktf->kdf", attn_low, grad_qkv, preferred_element_type=jnp.float32
    )
    grad_qkv_wide = grad_qkv.astype(jnp.float32)
    grad_qv_bias = jnp.stack([jnp.sum(grad_qkv_wide[0], axis=0), jnp.sum(grad_qkv_wide[2], axis=0)])
    grad_attn_part = jnp.einsum(
        "ktf,kdf->td", grad_qkv, qkv_weight, preferred_element_type=jnp.float32
    )
    grad_attn_in = lax.psum(grad_attn_part, "tensor")
    input_norm_grad, grad_attn_gain, grad_attn_shift = norm_backward(
        grad_attn_in, attn_unit, attn_inverse, attn_gain_f
    )
    input_grad = grad_hidden + input_norm_grad
    summed = lax.psum(
        (
            grad_attn_gain,
            grad_attn_shift,
            grad_qkv_weight,
            grad_qv_bias,
            grad_table,
            grad_proj,
            grad_proj_bias,
            grad_moe_gain,
            grad_moe_shift,
            grad_router,
            grad_in,
            grad_in_bias,
            grad_out,
            grad_out_bias,
        ),
        "dp",
    )
    return (
        block_out,
        input_grad,
        summed[0],
        summed[1],
        summed[2],
        summed[3],
        summed[4],
        summed[5],
        summed[6],
        summed[7],
        summed[8],
        summed[9],
        summed[10],
        summed[11],
        summed[12],
        summed[13],
    )


def solution(mesh):
    placed = (
        P("dp", None),
        P(),
        P(),
        P(None, None, "tensor"),
        P(None, "tensor"),
        P(None, "tensor"),
        P("tensor", None),
        P(),
        P(),
        P(),
        P(),
        P(None, None, "tensor"),
        P(None, "tensor"),
        P(None, "tensor", None),
        P(),
        P("dp", None),
        P("dp", None),
    )
    return jax.shard_map(
        shards,
        mesh=mesh,
        in_specs=placed,
        out_specs=(
            P("dp", None),
            P("dp", None),
            P(),
            P(),
            P(None, None, "tensor"),
            P(None, "tensor"),
            P(None, "tensor"),
            P("tensor", None),
            P(),
            P(),
            P(),
            P(),
            P(None, None, "tensor"),
            P(None, "tensor"),
            P(None, "tensor", None),
            P(),
        ),
        check_vma=False,
    )
```

profile of v0, /device:TPU:0, one launch (start us, length us, event | category | flops | bytes accessed | tf_op | source)
XLA Modules:
  0.0 1227.4 jit_solution(987940902200239365)
XLA Ops:
  9.6 2.7 convert_reduce_fusion
  12.3 3.8 fusion.25
  20.0 4.7 fusion.104
  26.7 3.0 reshape_squeeze.9
  29.7 3.2 reshape_squeeze.11
  32.9 4.5 reshape_squeeze.10
  37.4 10.8 fusion.109
  48.3 8.7 fusion
  57.0 7.9 fusion.37
  64.9 1.7 copy.70
  66.6 2.6 reshape.367
  69.3 4.2 fusion.111
  73.8 2.3 reduce-window.6
  77.0 22.9 %scatter_custom_fusion = s32[5880]{0:T(1024)S(1)} fusion(s32[4704]{0:T(1024)S(1)} %fusion.82, s32[4704]{0:T(1024)S(1)} %iota.47, s32[]{:T(128)} %constant.116.clone.1), kind=kCustom, calls=%fused_computation.135 | custom fusion | bytes 23524 | tf_op jit(solution)/shard_map/scatter | solution.py:169
  100.0 118.3 %all-reduce.11.cloned.1.call-done = f32[4704,384]{1,0:T(8,128)} async-done(((f32[4704,384]{1,0:T(8,128)}), f32[4704,384]{1,0:T(8,128)}) %all-reduce.11.cloned.1.call-update) | async-done | bytes 7225360 | tf_op jit(solution)/shard_map/psum | solution.py:146
  218.3 5.1 fusion.106
  225.1 2.8 add_convert_fusion.1
  227.9 2.2 concatenate.10
  232.5 2.0 fusion.26
  234.5 1.8 copy-done.8
  236.3 2.1 concatenate.11
  238.5 18.4 %gather_fusion.2 = bf16[5880,384]{1,0:T(8,128)(2,1)} fusion(bf16[4705,384]{1,0:T(8,128)(2,1)} %concatenate.11, s32[6144]{0:T(1024)S(1)} %pad_clamp_fusion), kind=kCustom, calls=%fused_computation.2 | custom fusion | bytes 9055200 | tf_op jit(solution)/shard_map/gather | solution.py:192
  256.8 5.7 reshape.372
  262.5 18.4 %gather_fusion = bf16[5880,384]{1,0:T(8,128)(2,1)} fusion(bf16[4705,384]{1,0:T(8,128)(2,1)} %concatenate.10, s32[6144]{0:T(1024)S(1)} %pad_clamp_fusion), kind=kCustom, calls=%fused_computation | custom fusion | bytes 9055200 | tf_op jit(solution)/shard_map/gather | solution.py:172
  280.9 5.7 reshape.370
  286.6 7.3 multiply_convert_fusion.1
  293.9 2.1 copy-done.9
  296.0 5.5 fusion.112
  301.4 8.1 reshape.371
  309.5 8.6 convert_reduce_fusion.1
  318.0 2.1 copy-done.10
  320.1 5.3 fusion.113
  325.4 8.2 reshape.373
  333.5 17.5 %gather_fusion.1 = f32[4704,384]{1,0:T(8,128)} fusion(f32[5880,384]{1,0:T(8,128)} %reshape.371, s32[5120]{0:T(1024)S(1)} %pad_clamp_fusion.1), kind=kCustom, calls=%fused_computation.1 | custom fusion | bytes 14469504 | tf_op jit(solution)/shard_map/gather | solution.py:184
  351.1 17.6 %gather_fusion.3 = f32[4704,384]{1,0:T(8,128)} fusion(f32[5880,384]{1,0:T(8,128)} %reshape.373, s32[5120]{0:T(1024)S(1)} %pad_clamp_fusion.1), kind=kCustom, calls=%fused_computation.3 | custom fusion | bytes 14469504 | tf_op jit(solution)/shard_map/gather | solution.py:205
  369.6 257.5 %all-reduce.17.cloned.1.call-done = (f32[4704,384]{1,0:T(8,128)}, f32[4704,384]{1,0:T(8,128)}) async-done(((f32[4704,384]{1,0:T(8,128)}, f32[4704,384]{1,0:T(8,128)}), (f32[4704,384]{1,0:T(8,128)}, f32[4704,384]{1,0:T(8,128)})) %all-reduce.17.cloned.1.call-update) | async-done | bytes 14450704 | tf_op jit(solution)/shard_map/psum | solution.py:186
  627.1 6.1 fusion.27
  633.2 11.6 multiply_reduce_fusion.1
  644.9 5.9 convert_reduce_fusion.2
  650.8 3.0 copy-done.3
  655.1 2.0 reshape.374
  657.1 8.7 fusion.38
  665.8 11.0 multiply_reduce_fusion
  676.8 9.4 fusion.28
  686.1 3.3 fusion.42
  692.4 3.0 stack_reshape.11
  697.1 3.0 stack_reshape.9
  706.0 5.4 convolution_bitcast_fusion
  711.7 8.9 fusion.114
  720.6 9.1 fusion.115
  732.6 2.5 fusion.46
  735.2 2.7 fusion.60
  737.9 4.6 convert_element_type.199
  743.3 2.4 slice_reduce_fusion.1
  746.6 3.6 fusion.63
  750.2 103.1 %all-reduce.13.cloned.1.call-done = f32[4704,384]{1,0:T(8,128)} async-done(((f32[4704,384]{1,0:T(8,128)}), f32[4704,384]{1,0:T(8,128)}) %all-reduce.13.cloned.1.call-update) | async-done | bytes 7225360 | tf_op jit(solution)/shard_map/psum | solution.py:260
  853.3 7.7 fusion.24
  861.1 157.7 %all-reduce.3 = (f32[384]{0:T(512)}, f32[384]{0:T(512)}, f32[2,96]{1,0:T(2,128)}, f32[169,3]{0,1:T(4,128)}, f32[384]{0:T(512)}, /*index=5*/f32[384]{0:T(512)}, f...) all-reduce(f32[384]{0:T(512)S(1)} %get-tuple-element.18, ...), channel_id=1, replica_groups=mesh['dp'=32,'tensor'=4] {'dp'}, use_global_device_ids=true, to_apply=%region_24.25 | all-reduce | flops 11835 | bytes 94680 | tf_op jit(solution)/shard_map/psum | solution.py:265
  1018.8 12.0 fusion.23
  1030.8 178.7 %all-reduce.15.cloned.1.call-done = (f32[3,384,96]{1,2,0:T(8,128)}, f32[96,384]{1,0:T(8,128)}, f32[8,384,384]{2,1,0:T(8,128)}, f32[8,384,384]{2,1,0:T(8,128)}) async-done(((f32[3,384,96]{1,2,0:T(8,128)}, f32[96,384]{1,0:T(8,128)}, f32[8,384,384]{2,1,0:T(8,128)}, f32[8,384,384]{2,1,0:T(8,128)}), (f32[3,384,96]{1,2,0:T(8,128)}, f32[96,384]{1,0:T(8,128)}, f32[8,384,384]{2,1,0:T(8,128)}, ...) | async-done | bytes 10027024 | tf_op jit(solution)/shard_map/psum | solution.py:265
  1209.6 2.0 copy.128
  1211.5 1.7 copy.129
  1213.3 4.9 copy.130
  1218.2 2.2 copy.131
  (192 shorter events, 30.9 us)
Async XLA Ops:
  7.2 279.4 %copy-start = (bf16[8,384,384]{2,1,0:T(8,128)(2,1)S(1)}, bf16[8,384,384]{2,1,0:T(8,128)(2,1)}, u32[]{:S(2)}) copy-start(bf16[8,384,384]{2,1,0:T(8,128)(2,1)} %param.28) | copy-start | bytes 7077892
  7.2 9.7 copy-start.49
  7.2 12.8 %copy-start.30 = (bf16[3,384,96]{1,2,0:T(8,128)(2,1)S(1)}, bf16[3,384,96]{1,2,0:T(8,128)(2,1)}, u32[]{:S(2)}) copy-start(bf16[3,384,96]{1,2,0:T(8,128)(2,1)} %param.20) | copy-start | bytes 663556
  7.2 211.0 %all-reduce.11.cloned.1.call-start = ((), (), s32[]{:S(2)}) async-start(), calls=%async_computation | async-start | bytes 14450688 | tf_op jit(solution)/shard_map/psum | solution.py:146
  7.3 17.5 %copy-start.38 = (s32[196]{0:T(256)}, s32[196]{0:T(256)S(1)}, u32[]{:S(2)}) copy-start(s32[196]{0:T(256)S(1)} %fusion.97) | copy-start | bytes 2356
  8.9 15.9 %copy-start.36 = (f32[384]{0:T(512)}, f32[384]{0:T(512)S(1)}, u32[]{:S(2)}) copy-start(f32[384]{0:T(512)S(1)} %convert_element_type.163) | copy-start | bytes 4612
  9.6 15.2 %copy-start.44 = (f32[384]{0:T(512)}, f32[384]{0:T(512)S(1)}, u32[]{:S(2)}) copy-start(f32[384]{0:T(512)S(1)} %convert_element_type.164) | copy-start | bytes 4612
  12.3 12.5 %copy-start.26 = (f32[4704]{0:T(1024)}, f32[4704]{0:T(1024)S(1)}, u32[]{:S(2)}) copy-start(f32[4704]{0:T(1024)S(1)} %broadcast_multiply_fusion.5) | copy-start | bytes 56452
  16.1 8.7 copy-start.32
  16.3 0.6 copy-start.40
  32.9 15.4 %copy-start.15 = (bf16[24,196,3,32]{1,0,3,2:T(8,128)(2,1)}, bf16[24,196,3,32]{1,0,3,2:T(8,128)(2,1)S(1)}, u32[]{:S(2)}) copy-start(bf16[24,196,3,32]{1,0,3,2:T(8,128)(2,1)S(1)} %reshape_squeeze.11) | copy-start | bytes 2709508
  48.2 8.8 copy-start.24
  48.3 8.8 copy-start.21
  57.0 12.2 copy-start.28
  69.2 4.3 copy-start.13
  69.3 4.3 copy-start.46
  69.3 4.3 copy-start.47
  69.3 4.3 copy-start.48
  69.3 4.3 copy-start.43
  69.3 4.3 copy-start.34
  73.5 553.6 %all-reduce.17.cloned.1.call-start = ((), (), s32[]{:S(2)}) async-start(), calls=%async_computation.3 | async-start | bytes 28901376 | tf_op jit(solution)/shard_map/psum | solution.py:186
  223.4 4.5 copy-start.2
  225.0 5.0 copy-start.35
  227.9 6.7 copy-start.4
  227.9 4.6 copy-start.6
  234.5 1.8 copy-start.8
  286.6 9.4 copy-start.17
  293.9 2.1 copy-start.9
  318.0 2.1 copy-start.10
  368.6 0.9 copy-start.25
  368.6 258.4 %copy-start.42 = (bf16[8,384]{1,0:T(8,128)(2,1)S(1)}, bf16[8,384]{1,0:T(8,128)(2,1)}, u32[]{:S(2)}) copy-start(bf16[8,384]{1,0:T(8,128)(2,1)} %param.31) | copy-start | bytes 18436
  368.7 484.7 %all-reduce.13.cloned.1.call-start = ((), (), s32[]{:S(2)}) async-start(), calls=%async_computation.1 | async-start | bytes 14450688 | tf_op jit(solution)/shard_map/psum | solution.py:260
  627.1 17.8 %slice-start.4 = ((s8[7225344]{0:T(1024)(128)(4,1)}), s8[4194304]{0:T(1024)(128)(4,1)S(1)}, s32[]{:S(2)}) async-start(s8[7225344]{0:T(1024)(128)(4,1)} %bitcast.110), calls=%async_computation.8 | async-start | bytes 8388608
  633.2 11.7 slice-start.5
  633.2 11.7 copy-start.7
  644.9 8.9 copy-start.29
  650.8 3.0 copy-start.3
  657.0 8.7 copy-start.22
  657.0 19.7 %slice-start = ((s8[14745600]{0:T(1024)(128)(4,1)}), s8[4194304]{0:T(1024)(128)(4,1)S(1)}, s32[]{:S(2)}) async-start(s8[14745600]{0:T(1024)(128)(4,1)} %bitcast.108), calls=%async_computation.4 | async-start | bytes 8388608
  657.1 19.7 %slice-start.1 = ((s8[14745600]{0:T(1024)(128)(4,1)}), s8[4194304]{0:T(1024)(128)(4,1)S(1)}, s32[]{:S(2)}) async-start(s8[14745600]{0:T(1024)(128)(4,1)} %bitcast.108), calls=%async_computation.5 | async-start | bytes 8388608
  665.7 11.0 slice-start.2
  665.8 11.0 slice-start.3
  676.8 9.4 copy-start.20
  686.1 3.3 copy-start.16
  689.5 1.3 copy-start.18
  690.7 9.4 copy-start.19
  695.4 10.6 copy-start.31
  704.5 1.5 copy-start.11
  711.4 498.1 %all-reduce.15.cloned.1.call-start = ((), (), s32[]{:S(2)}) async-start(), calls=%async_computation.2 | async-start | bytes 20054016 | tf_op jit(solution)/shard_map/psum | solution.py:265
  711.7 18.0 %slice-start.6 = ((s8[7225344]{0:T(1024)(128)(4,1)}), s8[4194304]{0:T(1024)(128)(4,1)S(1)}, s32[]{:S(2)}) async-start(s8[7225344]{0:T(1024)(128)(4,1)} %bitcast.112), calls=%async_computation.10 | async-start | bytes 8388608
  720.6 9.1 slice-start.7
  720.6 9.1 copy-start.14
  729.7 2.1 copy-start.5
  729.7 2.9 copy-start.12
  729.7 2.9 copy-start.27
  729.7 2.9 copy-start.33
  729.8 2.9 copy-start.37
  729.8 2.9 copy-start.45
  735.2 7.3 copy-start.23
  735.2 7.3 copy-start.39
  737.9 7.8 copy-start.41
  1209.6 8.6 slice-start.8
  1211.5 8.9 copy-start.1
  1213.3 4.9 slice-start.9
Sparse Core Ops, SparseCore 0:
  73.6 144.5 all-reduce.10
  368.8 258.2 all-reduce.16
  711.6 141.7 all-reduce.12
  857.4 352.1 all-reduce.14
where the time goes:
time: 1240 us; the launch traced here: 1230 us
  waiting for transfers between devices  658 us (53%)
  local copies, waits for them, and re-layouts  186 us (15%)
  blocking collectives  158 us (13%)
  matrix products  135 us (11%)
  other arithmetic  74.7 us (6%)
  between operations  15.2 us (1%)
    psum x1, waiting for transfers between devices, shards(): expert_tok = lax.psum(token_part, 'tensor') + out_bias_tok  257 us
    psum x1, waiting for transfers between devices, shards(): lax.psum((grad_attn_gain, grad_attn_shift, grad_qkv_weight, grad_qv_bias,...  179 us
    psum x1, blocking collectives, shards(): lax.psum((grad_attn_gain, grad_attn_shift, grad_qkv_weight, grad_qv_bias,...  158 us
    psum x1, waiting for transfers between devices, shards(): attn_out = lax.psum(attn_part, 'tensor') + proj_bias.astype(jnp.float32)  118 us
    psum x1, waiting for transfers between devices, shards(): grad_attn_in = lax.psum(grad_attn_part, 'tensor')  103 us
    unnamed x127, local copies, waits for them, and re-layouts  27 us
  transfers between devices with their start and end apart: 4, of which 4 were waited for; matrix products, arithmetic and copies ran while one was open for 7% of the time, Pallas kernels for 0%

commit v1 on v0

v1 whole, which is shorter than its diff:
```python
import functools
import math

import jax
import jax.numpy as jnp
import numpy as np
from jax import lax
from jax.experimental import pallas as pl
from jax.experimental.pallas import tpu as pltpu
from jax.sharding import PartitionSpec as P

F32 = jnp.float32
LOW = jnp.bfloat16
D = 384
HEADS = 12
EXPERTS = 8
SIDE = 14
WINDOW = 7
IMAGE = 196
HALF = 2352
BLOCK = 784
BLOCKS = 3
PADDED = 256
SLICE = 208
TILE = 168
TILES = 28
HALF_TILES = 14
GROUPS = 28
SORTED = 224
SLOTS = 960
CHUNK = 240
STORE = EXPERTS * SLOTS + 8
MASK_FILL = -1e30
SCALE = 32 ** (-0.5)
VMEM = 60 * 1024 * 1024


def layout_consts():
    cell = np.arange(IMAGE)
    row = (cell // SIDE - WINDOW // 2) % SIDE
    col = (cell % SIDE - WINDOW // 2) % SIDE
    slot = (row // WINDOW * 2 + col // WINDOW) * 64 + row % WINDOW * WINDOW + col % WINDOW
    place = np.zeros((4, PADDED, SLICE), np.float32)
    for k in range(4):
        place[k, slot, 4 * k + cell] = 1.0
    part = lambda v: (v >= SIDE - WINDOW) * 1 + (v >= SIDE - WINDOW // 2) * 1
    label = np.full((PADDED,), -1)
    label[slot] = part(row) * 3 + part(col)
    label = label.reshape(4, 64)
    real = np.arange(64) < WINDOW * WINDOW
    meet = (label[:, :, None] == label[:, None, :]) | ~real[None, :, None]
    fill = np.where(meet & real[None, None, :], 0.0, MASK_FILL).astype(np.float32)
    fill = np.tile(fill, (1, 1, 4))
    spot = np.arange(49)
    entry = (spot[:, None] // 7 - spot[None, :] // 7 + 6) * 13 + spot[:, None] % 7 - spot[None, :] % 7 + 6
    lookup = np.zeros((64, 64, 169), np.float32)
    lookup[spot[:, None], spot[None, :], entry] = 1.0
    heads = (np.arange(256)[:, None] // 64 == np.arange(128)[None, :] // 32).astype(np.float32)
    segment = (np.arange(256)[:, None] // 64 == np.arange(256)[None, :] // 64).astype(np.float32)
    return place, fill, lookup.reshape(4096, 169), heads, segment


def nn(a, b):
    return lax.dot_general(a, b, (((1,), (0,)), ((), ())), preferred_element_type=F32)


def nt(a, b):
    return lax.dot_general(a, b, (((1,), (1,)), ((), ())), preferred_element_type=F32)


def tn(a, b):
    return lax.dot_general(a, b, (((0,), (0,)), ((), ())), preferred_element_type=F32)


def norm_parts(values):
    centre = values - jnp.mean(values, axis=-1, keepdims=True)
    inverse = lax.rsqrt(jnp.mean(centre * centre, axis=-1, keepdims=True) + 1e-5)
    return centre * inverse, inverse


def norm_back(upstream, unit, inverse, gain):
    scaled = upstream * gain
    return inverse * (
        scaled
        - jnp.mean(scaled, axis=-1, keepdims=True)
        - unit * jnp.mean(scaled * unit, axis=-1, keepdims=True)
    )


def column_sum(values):
    return jnp.sum(values, axis=0, keepdims=True)


def router_softmax(second, router):
    logits = nn(second, router)
    lane = lax.broadcasted_iota(jnp.int32, logits.shape, 1)
    logits = jnp.where(lane < EXPERTS, logits, MASK_FILL)
    power = jnp.exp(logits - jnp.max(logits, axis=-1, keepdims=True))
    return power / jnp.sum(power, axis=-1, keepdims=True), lane


def expand(part, heads):
    return jnp.concatenate([part] * 4, axis=0) * heads


def attention_kernel(
    core, x_ref, ids_ref, attn_gain, attn_shift, wqkv_wide, bqkv, bias, place, place_t, heads, segment,
    wproj_wide, bproj, moe_gain, moe_shift, router, out_bias,
    hidden_ref, base_ref, second_ref, gate_ref, mixed_ref, qkv_ref, prob_ref,
    low_scr, raster_scr, wqkv, wproj,
):
    @pl.when(pl.program_id(0) == 0)
    def _():
        wqkv[...] = wqkv_wide[...].T.astype(LOW)
        wproj[...] = wproj_wide[...].astype(LOW)

    x = x_ref[...].astype(F32)
    unit, _ = norm_parts(x)
    low_scr[...] = (unit * attn_gain[...] + attn_shift[...]).astype(LOW)
    raster_scr[...] = jnp.zeros_like(raster_scr)
    lane = lax.broadcasted_iota(jnp.int32, (64, 128), 1)
    left = lane < 64

    def image(k, carry):
        start = pl.multiple_of(k * 192, 64)
        rows = nn(place[k], low_scr[pl.ds(start, SLICE), :]).astype(LOW)
        qkv = (nn(rows, wqkv[...]) + bqkv[...]).astype(LOW)
        qkv_ref[pl.ds(pl.multiple_of(k * PADDED, PADDED), PADDED), :] = qkv
        outs = []
        for w in range(4):
            row = slice(w * 64, w * 64 + 64)
            parts = []
            for g in range(3):
                q = qkv[row, g * 128 : g * 128 + 128]
                kx = expand(qkv[row, D + g * 128 : D + g * 128 + 128], heads[...])
                vx = expand(qkv[row, 2 * D + g * 128 : 2 * D + g * 128 + 128], heads[...])
                scores = nt(q, kx) * SCALE + bias[w * 3 + g]
                power = []
                for c in range(2):
                    piece = scores[:, c * 128 : c * 128 + 128]
                    first = jnp.max(jnp.where(left, piece, 2 * MASK_FILL), axis=-1, keepdims=True)
                    other = jnp.max(jnp.where(left, 2 * MASK_FILL, piece), axis=-1, keepdims=True)
                    power.append(jnp.exp(piece - jnp.where(left, first, other)))
                power = jnp.concatenate(power, axis=1)
                total = nn(power.astype(LOW), segment[...])
                prob = (power / total).astype(LOW)
                spot = pl.multiple_of(((k * 4 + w) * 3 + g) * 64, 64)
                prob_ref[pl.ds(spot, 64), :] = prob
                parts.append(nn(prob, vx).astype(LOW))
            outs.append(jnp.concatenate(parts, axis=1))
        mixed = jnp.concatenate(outs, axis=0)
        raster_scr[pl.ds(start, SLICE), :] += nn(place_t[k], mixed)
        return carry

    lax.fori_loop(0, 4, image, 0)
    mixed = raster_scr[...].astype(LOW)
    mixed_ref[...] = mixed
    hidden = x + (nn(mixed, wproj[...]) + bproj[...])
    hidden_ref[...] = hidden
    unit, _ = norm_parts(hidden)
    second = (unit * moe_gain[...] + moe_shift[...]).astype(LOW)
    second_ref[...] = second.astype(F32)
    probs, lanes = router_softmax(second, router[...])
    chosen = lanes == ids_ref[...]
    gate = jnp.sum(jnp.where(chosen, probs, 0.0), axis=-1, keepdims=True)
    gate_ref[...] = gate
    base_ref[...] = hidden + gate * nn(chosen.astype(F32).astype(LOW), out_bias[...])


def whole(shape):
    return pl.BlockSpec(shape, lambda *_: (0,) * len(shape))


def attention_forward(core, x, ids, consts, weights, bias):
    place, place_t, heads, segment = consts
    at_block = lambda width: pl.BlockSpec((BLOCK, width), lambda i, s: (s[0] * BLOCKS + i, 0))
    rows = lambda height, width: pl.BlockSpec((height, width), lambda i, s: (i, 0))
    fixed = [weights[n] for n in ("attn_gain", "attn_shift", "wqkv", "bqkv")]
    tail = [weights[n] for n in ("wproj", "bproj", "moe_gain", "moe_shift", "router", "out_bias_pad")]
    operands = fixed + [bias, place, place_t, heads, segment] + tail
    return pl.pallas_call(
        attention_kernel,
        grid_spec=pltpu.PrefetchScalarGridSpec(
            num_scalar_prefetch=1,
            grid=(BLOCKS,),
            in_specs=[at_block(D), at_block(1)] + [whole(v.shape) for v in operands],
            out_specs=[
                rows(BLOCK, D),
                rows(BLOCK, D),
                rows(BLOCK, D),
                rows(BLOCK, 1),
                rows(BLOCK, D),
                rows(4 * PADDED, 3 * D),
                rows(48 * 64, 256),
            ],
            scratch_shapes=[
                pltpu.VMEM((BLOCK, D), LOW),
                pltpu.VMEM((BLOCK, D), F32),
                pltpu.VMEM((D, 3 * D), LOW),
                pltpu.VMEM((D, D), LOW),
            ],
        ),
        out_shape=[
            jax.ShapeDtypeStruct((HALF, D), F32),
            jax.ShapeDtypeStruct((HALF, D), F32),
            jax.ShapeDtypeStruct((HALF, D), F32),
            jax.ShapeDtypeStruct((HALF, 1), F32),
            jax.ShapeDtypeStruct((HALF, D), LOW),
            jax.ShapeDtypeStruct((BLOCKS * 4 * PADDED, 3 * D), LOW),
            jax.ShapeDtypeStruct((BLOCKS * 48 * 64, 256), LOW),
        ],
        compiler_params=pltpu.CompilerParams(vmem_limit_bytes=VMEM),
        cost_estimate=pl.CostEstimate(flops=8_000_000_000, bytes_accessed=40_000_000, transcendentals=4_000_000),
        name="attention_forward",
    )(core, x, ids, *operands)


def gelu_parts(values):
    size = jnp.abs(values)
    decay = jnp.exp(-0.5 * values * values)
    t = 1.0 / (1.0 + (0.3275911 / math.sqrt(2.0)) * size)
    poly = t * (0.254829592 + t * (-0.284496736 + t * (1.421413741 + t * (-1.453152027 + t * 1.061405429))))
    half = 0.5 * poly * decay
    cdf = jnp.where(values >= 0.0, 1.0 - half, half)
    return values * cdf, cdf + values * decay * (1.0 / math.sqrt(2.0 * math.pi))


def experts_kernel(
    core, dest, chunks,
    own_ref, other_ref, g_ref, ids_ref, pos_row, pos_col, router, w_in, b_in, w_out,
    grad_in, grad_out, in_bias, out_bias, gs_theirs, ep_theirs, gg_theirs, gs_mine, ep_mine, gg_mine,
    store,
):
    step = pl.program_id(0)

    @pl.when(step == 0)
    def _():
        def clear(j, carry):
            store[pl.ds(pl.multiple_of(j * 248, 8), 248), :] = jnp.zeros((248, 2 * D), F32)
            return carry

        lax.fori_loop(0, STORE // 248, clear, 0)

    def tile_of():
        undo = step >= TILES + EXPERTS
        j = jnp.where(undo, step - TILES - EXPERTS, step)
        flip = jnp.where(undo, 1 - core[0], core[0])
        half = jnp.where(j < HALF_TILES, flip, 1 - flip)
        return half * HALF_TILES + j % HALF_TILES

    @pl.when(step < TILES)
    def _():
        tile = tile_of()
        second = jnp.where(step < HALF_TILES, own_ref[...], other_ref[...]).astype(LOW)
        probs, lanes = router_softmax(second, router[...])
        gate = jnp.sum(jnp.where(lanes == ids_ref[...], probs, 0.0), axis=-1, keepdims=True)
        grad = (gate * g_ref[...].astype(F32)).astype(LOW)
        spot = lax.broadcasted_iota(jnp.int32, (SORTED, TILE), 0)
        pick = (spot == pos_row[0]).astype(F32).astype(LOW)
        moved = nn(pick, jnp.concatenate([second, grad], axis=1))
        for j in range(GROUPS):
            at = pl.multiple_of(dest[tile * GROUPS + j] * 8, 8)
            store[pl.ds(at, 8), :] = moved[j * 8 : j * 8 + 8, :]

    @pl.when((step >= TILES) & (step < TILES + EXPERTS))
    def _():
        e = step - TILES
        grad_in[...] = jnp.zeros_like(grad_in)
        grad_out[...] = jnp.zeros_like(grad_out)

        def chunk(c, sums):
            at = pl.ds(pl.multiple_of(e * SLOTS + c * CHUNK, 16), CHUNK)
            buffer = store[at, :D].astype(LOW)
            grad = store[at, D:].astype(LOW)
            act, slope = gelu_parts(nn(buffer, w_in[0]) + b_in[pl.ds(e, 1), :].astype(F32))
            act = act.astype(LOW)
            grad_pre = (nt(grad, w_out[0]) * slope).astype(LOW)
            store[at, :D] = nt(grad_pre, w_in[0])
            store[at, D:] = nn(act, w_out[0])
            grad_in[...] += tn(buffer, grad_pre)
            grad_out[...] += tn(act, grad)
            return sums[0] + column_sum(grad_pre.astype(F32)), sums[1] + column_sum(grad.astype(F32))

        zero = jnp.zeros((1, D), F32)
        sums = lax.fori_loop(0, chunks[e], chunk, (zero, zero))
        in_bias[pl.ds(e, 1), :] = sums[0]
        out_bias[pl.ds(e, 1), :] = sums[1]

    def collect():
        tile = tile_of()
        rows = [store[pl.ds(pl.multiple_of(dest[tile * GROUPS + j] * 8, 8), 8), :] for j in range(GROUPS)]
        rows = jnp.concatenate(rows, axis=0).astype(LOW)
        spot = lax.broadcasted_iota(jnp.int32, (TILE, SORTED), 1)
        pick = (spot == pos_col[...]).astype(F32).astype(LOW)
        back = nn(pick, rows)
        gate_grad = jnp.sum(g_ref[...].astype(F32) * back[:, D:], axis=-1, keepdims=True)
        return back[:, :D], back[:, D:], gate_grad

    @pl.when((step >= TILES + EXPERTS) & (step < TILES + EXPERTS + HALF_TILES))
    def _():
        gs_theirs[...], ep_theirs[...], gg_theirs[...] = collect()

    @pl.when(step >= TILES + EXPERTS + HALF_TILES)
    def _():
        gs_mine[...], ep_mine[...], gg_mine[...] = collect()


def experts(core, dest, chunks, own, other, g, ids, pos_row, pos_col, router, w_in, b_in, w_out):
    steps = TILES + EXPERTS + TILES
    last = HALF_TILES - 1

    def tile(i, c, *_):
        undo = i >= TILES + EXPERTS
        j = jnp.where(undo, i - TILES - EXPERTS, jnp.minimum(i, TILES - 1))
        flip = jnp.where(undo, 1 - c[0], c[0])
        half = jnp.where(j < HALF_TILES, flip, 1 - flip)
        return half * HALF_TILES + j % HALF_TILES

    def run(begin):
        return lambda i, *_: (jnp.clip(i - begin, 0, last), 0)

    expert = lambda i, *_: (jnp.clip(i - TILES, 0, EXPERTS - 1), 0, 0)
    flat = lambda i, *_: (jnp.clip(i - TILES, 0, EXPERTS - 1), 0)
    by_tile = lambda width: pl.BlockSpec((TILE, width), lambda i, *s: (tile(i, *s), 0))
    undo = TILES + EXPERTS
    half = lambda width: jax.ShapeDtypeStruct((HALF, width), F32)
    out_half = lambda begin: [pl.BlockSpec((TILE, w), run(begin)) for w in (D, D, 1)]
    return pl.pallas_call(
        experts_kernel,
        grid_spec=pltpu.PrefetchScalarGridSpec(
            num_scalar_prefetch=3,
            grid=(steps,),
            in_specs=[
                pl.BlockSpec((TILE, D), run(0)),
                pl.BlockSpec((TILE, D), run(HALF_TILES)),
                by_tile(D),
                by_tile(1),
                pl.BlockSpec((1, 1, TILE), lambda i, *s: (tile(i, *s), 0, 0)),
                by_tile(1),
                whole((D, 128)),
                pl.BlockSpec((1, D, D), expert),
                whole((EXPERTS, D)),
                pl.BlockSpec((1, D, D), expert),
            ],
            out_specs=[
                pl.BlockSpec((D, D), flat),
                pl.BlockSpec((D, D), flat),
                whole((EXPERTS, D)),
                whole((EXPERTS, D)),
            ]
            + out_half(undo)
            + out_half(undo + HALF_TILES),
            scratch_shapes=[pltpu.VMEM((STORE, 2 * D), F32)],
        ),
        out_shape=[
            jax.ShapeDtypeStruct((EXPERTS * D, D), F32),
            jax.ShapeDtypeStruct((EXPERTS * D, D), F32),
            jax.ShapeDtypeStruct((EXPERTS, D), F32),
            jax.ShapeDtypeStruct((EXPERTS, D), F32),
        ]
        + [half(D), half(D), half(1)] * 2,
        compiler_params=pltpu.CompilerParams(vmem_limit_bytes=VMEM),
        cost_estimate=pl.CostEstimate(flops=25_000_000_000, bytes_accessed=60_000_000, transcendentals=6_000_000),
        name="experts",
    )(core, dest, chunks, own, other, g, ids, pos_row, pos_col, router, w_in, b_in, w_out)


def sort_plan(ids):
    named = ids.reshape(TILES, TILE)
    kinds = jnp.arange(EXPERTS, dtype=jnp.int32)
    chosen = (named[:, :, None] == kinds).astype(F32)
    before = jnp.asarray(np.tril(np.ones((TILE, TILE), np.float32), -1))
    rank = jnp.einsum("ij,tje->tie", before, chosen)
    count = jnp.sum(chosen, axis=1).astype(jnp.int32)
    groups = (count + 7) // 8
    ahead = jnp.asarray(np.tril(np.ones((EXPERTS, EXPERTS), np.int32), -1))
    first = jnp.sum(groups[:, None, :] * ahead[None], axis=-1)
    spot = jnp.sum(chosen * (rank + 8.0 * first[:, None, :].astype(F32)), axis=-1).astype(jnp.int32)
    earlier = jnp.asarray(np.tril(np.ones((TILES, TILES), np.int32), -1))
    offset = jnp.sum(earlier[:, :, None] * groups[None], axis=1)
    j = jnp.arange(GROUPS, dtype=jnp.int32)[None, :, None]
    inside = (j >= first[:, None, :]) & (j < (first + groups)[:, None, :])
    target = kinds * (SLOTS // 8) + offset[:, None, :] + j - first[:, None, :]
    dest = jnp.sum(jnp.where(inside, target, 0), axis=-1)
    dest = jnp.where(jnp.any(inside, axis=-1), dest, EXPERTS * SLOTS // 8).astype(jnp.int32)
    used = jnp.sum(groups, axis=0) * 8
    chunks = (used + CHUNK - 1) // CHUNK
    return spot, dest.reshape(-1), chunks.astype(jnp.int32)


def backward_kernel(
    first, core, gs_a, gs_b, gg_ref, hidden_ref, g_ref, x_ref, ids_ref, mixed_ref, qkv_ref, prob_ref,
    attn_gain, attn_shift, wqkv, place, place_t, heads, segment, wproj, moe_gain, moe_shift, router, out_bias_t,
    *refs,
):
    if first:
        input_grad, grad_wqkv, grad_wproj, small, table, raster_scr, mixed_scr = refs
        grad_wqkv[...] = jnp.zeros_like(grad_wqkv)
        grad_wproj[...] = jnp.zeros_like(grad_wproj)
        small[...] = jnp.zeros_like(small)
        table[...] = jnp.zeros_like(table)
    else:
        before, (input_grad, grad_wqkv, grad_wproj, small, table, raster_scr, mixed_scr) = refs[:4], refs[4:]
        for was, now in zip(before, (grad_wqkv, grad_wproj, small, table)):
            now[...] = was[...]

    g_low = g_ref[...]
    g = g_low.astype(F32)
    unit, inverse = norm_parts(hidden_ref[...])
    second = (unit * moe_gain[...] + moe_shift[...]).astype(LOW)
    probs, lanes = router_softmax(second, router[...])
    chosen = lanes == ids_ref[...]
    gate = jnp.sum(jnp.where(chosen, probs, 0.0), axis=-1, keepdims=True)
    with_bias = jnp.sum(jnp.where(chosen, nn(g_low, out_bias_t[...]), 0.0), axis=-1, keepdims=True)
    grad_gate = gg_ref[...] + with_bias
    grad_logit = grad_gate * gate * (chosen.astype(F32) - probs)
    logit_high = grad_logit.astype(LOW)
    logit_rest = (grad_logit - logit_high.astype(F32)).astype(LOW)
    grad_router = tn(logit_high, second) + tn(logit_rest, second)
    grad_second = gs_a[...] + gs_b[...] + nt(logit_high, router[...]) + nt(logit_rest, router[...])
    small[3:4, :] += column_sum(grad_second * unit)
    small[4:5, :] += column_sum(grad_second)
    small[8:16, :] += grad_router[:EXPERTS, :]
    grad_hidden = g + norm_back(grad_second, unit, inverse, moe_gain[...])
    grad_low = grad_hidden.astype(LOW)
    small[2:3, :] += column_sum(grad_low.astype(F32))
    grad_wproj[...] += tn(mixed_ref[...], grad_low)
    mixed_scr[...] = nt(grad_low, wproj[...].astype(LOW)).astype(LOW)
    raster_scr[...] = jnp.zeros_like(raster_scr)

    def image(k, carry):
        start = pl.multiple_of(k * 192, 64)
        grad_mixed = nn(place[k], mixed_scr[pl.ds(start, SLICE), :]).astype(LOW)
        outs = []
        for w in range(4):
            row = slice(w * 64, w * 64 + 64)
            at = pl.ds(pl.multiple_of(k * PADDED + w * 64, 64), 64)
            parts = [[], [], []]
            for c in range(3):
                q = qkv_ref[at, c * 128 : c * 128 + 128]
                kx = expand(qkv_ref[at, D + c * 128 : D + c * 128 + 128], heads[...])
                vx = expand(qkv_ref[at, 2 * D + c * 128 : 2 * D + c * 128 + 128], heads[...])
                prob_low = prob_ref[pl.ds(pl.multiple_of(((k * 4 + w) * 3 + c) * 64, 64), 64), :]
                prob = prob_low.astype(F32)
                upstream = grad_mixed[row, c * 128 : c * 128 + 128]
                grad_prob = nt(upstream, vx)
                weighted = nn((prob * grad_prob).astype(LOW), segment[...])
                grad_score = prob * (grad_prob - weighted)
                table[c * 64 : c * 64 + 64, :] += grad_score
                low = (grad_score * SCALE).astype(LOW)
                parts[0].append(nn(low, kx).astype(LOW))
                for slot, left, right in ((1, low, q), (2, prob_low, upstream)):
                    full = tn(left, right)
                    kept = [full[h * 64 : h * 64 + 64] * heads[h * 64 : h * 64 + 64, :].astype(F32) for h in range(4)]
                    parts[slot].append((kept[0] + kept[1] + kept[2] + kept[3]).astype(LOW))
            outs.append(jnp.concatenate(parts[0] + parts[1] + parts[2], axis=1))
        grads = jnp.concatenate(outs, axis=0)
        raster_scr[pl.ds(start, SLICE), :] += nn(place_t[k], grads)
        return carry

    lax.fori_loop(0, 4, image, 0)
    unit, inverse = norm_parts(x_ref[...].astype(F32))
    attn_low = (unit * attn_gain[...] + attn_shift[...]).astype(LOW)
    raster = raster_scr[...]
    small[5:6, :] += column_sum(raster[:, :D])
    small[6:7, :] += column_sum(raster[:, 2 * D :])
    grads = raster.astype(LOW)
    grad_wqkv[...] += tn(grads, attn_low)
    grad_in = nn(grads, wqkv[...].astype(LOW))
    small[0:1, :] += column_sum(grad_in * unit)
    small[1:2, :] += column_sum(grad_in)
    input_grad[...] = grad_hidden + norm_back(grad_in, unit, inverse, attn_gain[...])


def attention_backward(block, core, gs_a, gs_b, gg, hidden, g, x, ids, mixed, qkv, prob, consts, weights, sums):
    place, place_t, heads, segment = consts
    at_block = lambda width: pl.BlockSpec((BLOCK, width), lambda i, s: (s[0] * BLOCKS + block, 0))
    rows = lambda height, width: pl.BlockSpec((height, width), lambda i, s: (block, 0))
    fixed = [weights[n] for n in ("attn_gain", "attn_shift", "wqkv")] + [place, place_t, heads, segment]
    fixed = fixed + [weights[n] for n in ("wproj", "moe_gain", "moe_shift", "router", "out_bias_t")]
    totals = [(3 * D, D), (D, D), (16, D), (192, 256)]
    before = [] if sums is None else list(sums)
    return pl.pallas_call(
        functools.partial(backward_kernel, sums is None),
        grid_spec=pltpu.PrefetchScalarGridSpec(
            num_scalar_prefetch=1,
            grid=(1,),
            in_specs=[
                whole((BLOCK, D)),
                whole((BLOCK, D)),
                rows(BLOCK, 1),
                rows(BLOCK, D),
                at_block(D),
                at_block(D),
                at_block(1),
                rows(BLOCK, D),
                rows(4 * PADDED, 3 * D),
                rows(48 * 64, 256),
            ]
            + [whole(v.shape) for v in fixed + before],
            out_specs=[whole((BLOCK, D))] + [whole(v) for v in totals],
            scratch_shapes=[pltpu.VMEM((BLOCK, 3 * D), F32), pltpu.VMEM((BLOCK, D), LOW)],
        ),
        out_shape=[jax.ShapeDtypeStruct(v, F32) for v in [(BLOCK, D)] + totals],
        compiler_params=pltpu.CompilerParams(vmem_limit_bytes=VMEM),
        cost_estimate=pl.CostEstimate(flops=20_000_000_000, bytes_accessed=50_000_000, transcendentals=100_000),
        name="attention_backward",
    )(core, gs_a, gs_b, gg, hidden, g, x, ids, mixed, qkv, prob, *fixed, *before)


def position_bias(table, fill, lookup):
    rows = jnp.dot(lookup, table, precision=lax.Precision.HIGHEST)
    rows = rows.T.reshape(3, 4, 64, 64).transpose(0, 2, 1, 3).reshape(1, 3, 64, 256)
    return (rows + fill[:, None]).reshape(12, 64, 256)


def table_gradient(sums, lookup):
    rows = sums.reshape(3, 64, 4, 64).transpose(1, 3, 0, 2).reshape(4096, HEADS)
    return lax.dot_general(lookup, rows, (((0,), (0,)), ((), ())), precision=lax.Precision.HIGHEST)


AXES = ("dp", "tensor")


def device_index(x, y, z, core):
    return (x % 2 * 16 + y % 4 * 4 + z % 4) * 4 + x // 2 % 2 * 2 + core


def pairs(move):
    places = [(x, y, z, c) for x in range(4) for y in range(4) for z in range(4) for c in range(2)]
    return [(device_index(*p), device_index(*move(*p))) for p in places]


CORE_SWAP = pairs(lambda x, y, z, c: (x, y, z, 1 - c))
FAR_SWAP = pairs(lambda x, y, z, c: ((x + 2) % 4, y, z, c))
NEAR_SWAP = pairs(lambda x, y, z, c: (x ^ 1, y, z, c))
TURN = {
    "y": [pairs(lambda x, y, z, c, s=s: (x, y + s, z, c)) for s in range(4)],
    "z": [pairs(lambda x, y, z, c, s=s: (x, y, z + s, c)) for s in range(4)],
}


def send(values, table):
    return lax.ppermute(values, AXES, table)


def after(values, *others):
    return lax.optimization_barrier((values,) + others)[0]


def scatter_sums(parts):
    got = []
    for shift in (1, 3, 2):
        for n, (values, axis, place) in enumerate(parts):
            rows = values.shape[0] // 4
            piece = lax.dynamic_slice_in_dim(values, (place + shift) % 4 * rows, rows, 0)
            if shift == 2:
                piece = after(piece, got[n])
            got.append(send(piece, TURN[axis][shift]))
    sums = []
    for n, (values, axis, place) in enumerate(parts):
        rows = values.shape[0] // 4
        own = lax.dynamic_slice_in_dim(values, place * rows, rows, 0)
        sums.append(own + got[n] + got[n + len(parts)] + got[n + 2 * len(parts)])
    return sums


def gather_rows(parts):
    got = []
    for shift in (1, 3, 2):
        for n, (values, axis, place) in enumerate(parts):
            piece = after(values, got[n]) if shift == 2 else values
            got.append(send(piece, TURN[axis][shift]))
    fulls = []
    for n, (values, axis, place) in enumerate(parts):
        rows = values.shape[0]
        full = jnp.zeros((4 * rows,) + values.shape[1:], values.dtype)
        for shift, piece in ((0, values), (1, got[n]), (3, got[n + len(parts)]), (2, got[n + 2 * len(parts)])):
            full = lax.dynamic_update_slice_in_dim(full, piece, (place - shift) % 4 * rows, 0)
        fulls.append(full)
    return fulls


def assemble_kernel(core, mine, other, out):
    half = pl.program_id(0) // BLOCKS
    out[...] = jnp.where(half == core[0], mine[...], other[...]).astype(out.dtype)


def assemble(core, mine, other, kind):
    def spot(is_mine):
        def index(i, c):
            here = (i // BLOCKS == c[0]) == is_mine
            return (jnp.where(here, i % BLOCKS, jnp.where(i < BLOCKS, 0, BLOCKS - 1)), 0)

        return index

    return pl.pallas_call(
        assemble_kernel,
        grid_spec=pltpu.PrefetchScalarGridSpec(
            num_scalar_prefetch=1,
            grid=(2 * BLOCKS,),
            in_specs=[pl.BlockSpec((BLOCK, D), spot(True)), pl.BlockSpec((BLOCK, D), spot(False))],
            out_specs=pl.BlockSpec((BLOCK, D), lambda i, c: (i, 0)),
        ),
        out_shape=jax.ShapeDtypeStruct((2 * HALF, D), kind),
        cost_estimate=pl.CostEstimate(flops=10_000_000, bytes_accessed=15_000_000, transcendentals=0),
        name="assemble",
    )(core, mine, other)


def gather_weights(far, core, qkv_weight, qv_bias, rel_table, proj_weight):
    few = jnp.concatenate([qv_bias.astype(F32).reshape(-1), rel_table.astype(F32).reshape(-1)])
    few = jnp.pad(few, (0, 8 * D - few.shape[0])).reshape(8, D)
    own = jnp.concatenate(
        [
            qkv_weight.astype(F32).transpose(0, 2, 1).reshape(3 * 96, D),
            proj_weight.astype(F32),
            few,
        ]
    )
    near = send(own, CORE_SWAP)
    over = send(own, FAR_SWAP)
    last = send(over, CORE_SWAP)
    pick = lambda flag, a, b: jnp.where(flag == 1, a, b)
    low = (pick(core, near, own), pick(core, own, near))
    high = (pick(core, last, over), pick(core, over, last))
    shards = [pick(far, high[i], low[i]) for i in (0, 1)] + [pick(far, low[i], high[i]) for i in (0, 1)]
    wqkv = jnp.stack([v[:288].reshape(3, 96, D) for v in shards], axis=1).reshape(3 * D, D)
    wproj = jnp.concatenate([v[288:384] for v in shards])
    few = jnp.stack([v[384:392].reshape(-1) for v in shards])
    bias = few[:, :192].reshape(4, 2, 96).transpose(1, 0, 2).reshape(2, D)
    table = few[:, 192:699].reshape(4, 169, 3).transpose(1, 0, 2).reshape(169, HEADS)
    return wqkv, wproj, bias, table


def shards(
    tokens_in, attn_gain, attn_shift, qkv_weight, qv_bias, rel_table, proj_weight, proj_bias, moe_gain, moe_shift,
    router_weight, expert_in, expert_in_bias, expert_out, expert_out_bias, expert_ids, cotangent,
):
    group, shard = lax.axis_index("dp"), lax.axis_index("tensor")
    at_x, at_y, at_z = group // 16, group // 4 % 4, group % 4
    far, side = shard // 2, shard % 2
    core = side.astype(jnp.int32).reshape(1)
    place, fill, lookup, heads, segment = layout_consts()
    consts = tuple(jnp.asarray(v).astype(LOW) for v in (place, place.transpose(0, 2, 1), heads, segment))
    lookup = jnp.asarray(lookup)
    wide = lambda v: v.astype(F32).reshape(1, -1)

    wqkv, wproj, bias_qv, table = gather_weights(far, side, qkv_weight, qv_bias, rel_table, proj_weight)
    weights = dict(
        attn_gain=wide(attn_gain),
        attn_shift=wide(attn_shift),
        wqkv=wqkv,
        bqkv=jnp.concatenate([bias_qv[0:1], jnp.zeros((1, D), F32), bias_qv[1:2]], axis=1),
        wproj=wproj,
        bproj=wide(proj_bias),
        moe_gain=wide(moe_gain),
        moe_shift=wide(moe_shift),
        router=jnp.pad(router_weight, ((0, 0), (0, 128 - EXPERTS))),
        out_bias_pad=jnp.pad(expert_out_bias, ((0, 128 - EXPERTS), (0, 0))),
        out_bias_t=jnp.pad(expert_out_bias, ((0, 128 - EXPERTS), (0, 0))).T,
    )
    bias = position_bias(table, jnp.asarray(fill), lookup)
    spot, dest, chunks = sort_plan(expert_ids)
    hidden, base, second, gate, mixed, qkv, prob = attention_forward(
        core, tokens_in, expert_ids, consts, weights, bias
    )
    second_other = send(second, CORE_SWAP)
    (grad_in, grad_out, in_bias, out_bias, gs_theirs, ep_theirs, gg_theirs, gs_mine, ep_mine, gg_mine) = experts(
        core, dest, chunks, second, second_other, cotangent, expert_ids,
        spot.reshape(TILES, 1, TILE), spot.reshape(-1, 1), weights["router"],
        expert_in, expert_in_bias.astype(F32), expert_out,
    )

    gs_theirs = send(gs_theirs, CORE_SWAP)
    gg = gg_mine[:, 0] + send(gg_theirs[:, 0], CORE_SWAP)
    gg = (gg + send(gg, FAR_SWAP)).reshape(HALF, 1)
    gs, gs_far = [], []
    for b in range(BLOCKS):
        block = slice(b * BLOCK, (b + 1) * BLOCK)
        gs.append(gs_mine[block] + gs_theirs[block])
        gs_far.append(send(after(gs[b], gs_far[-1]) if b else gs[b], FAR_SWAP))

    ep = ep_mine + send(ep_theirs, CORE_SWAP)
    ep = ep + send(after(ep, gs_far[-1]), FAR_SWAP)
    block_half = base + gate * ep
    block_out = assemble(core, block_half, send(block_half, CORE_SWAP), LOW)

    sum_in, sum_out = scatter_sums([(grad_in, "y", at_y), (grad_out, "z", at_z)])
    sum_in, sum_out = scatter_sums([(sum_in, "z", at_z), (sum_out, "y", at_y)])
    sum_in, sum_out = sum_in + send(sum_in, NEAR_SWAP), sum_out + send(sum_out, NEAR_SWAP)
    sum_in, sum_out = gather_rows([(sum_in, "z", at_z), (sum_out, "y", at_y)])
    sum_in, sum_out = gather_rows([(sum_in, "y", at_y), (sum_out, "z", at_z)])

    sums, grads = None, []
    for b in range(BLOCKS):
        grad, *sums = attention_backward(
            b, core, gs[b], gs_far[b], gg, hidden, cotangent, tokens_in, expert_ids, mixed, qkv, prob,
            consts, weights, sums,
        )
        grads.append(grad)
    others = [send(v, CORE_SWAP) for v in grads]
    input_grad = assemble(core, jnp.concatenate(grads), jnp.concatenate(others), F32)

    grad_wqkv, grad_wproj, small, pair_sums = sums
    rows = jnp.pad(table_gradient(pair_sums, lookup).reshape(-1), (0, 8 * D - 169 * HEADS)).reshape(8, D)
    by_shard = jnp.concatenate([grad_wqkv.reshape(3, 4, 96, D), grad_wproj.reshape(1, 4, 96, D)])

    def pack(index):
        return jnp.concatenate([lax.dynamic_index_in_dim(by_shard, index, 1, False).reshape(D, D), small, rows])

    packed = pack(shard) + send(pack(shard ^ 1), CORE_SWAP)
    packed = jnp.concatenate([packed, in_bias, out_bias, jnp.zeros((88, D), F32)])
    (packed,) = scatter_sums([(packed, "y", at_y)])
    (packed,) = scatter_sums([(packed, "z", at_z)])
    packed = packed + send(packed, NEAR_SWAP)
    (packed,) = gather_rows([(packed, "z", at_z)])
    (packed,) = gather_rows([(packed, "y", at_y)])
    few = packed[D : D + 24]
    grad_table = few[16:24].reshape(-1)[: 169 * HEADS].reshape(169, HEADS)
    return (
        block_out,
        input_grad,
        few[0],
        few[1],
        packed[:288].reshape(3, 96, D).transpose(0, 2, 1),
        lax.dynamic_slice_in_dim(few[5:7], shard * 96, 96, 1),
        lax.dynamic_slice_in_dim(grad_table, shard * 3, 3, 1),
        packed[288:384],
        few[2],
        few[3],
        few[4],
        few[8:16].T,
        sum_in.reshape(EXPERTS, D, D),
        packed[408:416],
        sum_out.reshape(EXPERTS, D, D),
        packed[416:424],
    )


def solution(mesh):
    placed = (
        P("dp", None),
        P(),
        P(),
        P(None, None, "tensor"),
        P(None, "tensor"),
        P(None, "tensor"),
        P("tensor", None),
        P(),
        P(),
        P(),
        P(),
        P(None, None, "tensor"),
        P(None, "tensor"),
        P(None, "tensor", None),
        P(),
        P("dp", None),
        P("dp", None),
    )
    return jax.shard_map(
        shards,
        mesh=mesh,
        in_specs=placed,
        out_specs=(
            P("dp", None),
            P("dp", None),
            P(),
            P(),
            P(None, None, "tensor"),
            P(None, "tensor"),
            P(None, "tensor"),
            P("tensor", None),
            P(),
            P(),
            P(),
            P(),
            P(None, None, "tensor"),
            P(None, "tensor"),
            P(None, "tensor", None),
            P(),
        ),
        check_vma=False,
    )
```

time: 1240 us -> 640 us (0.52)
  waiting for transfers between devices: 658 us -> 175 us
  Pallas kernels: 0 us -> 256 us
  blocking collectives: 158 us -> 0 us
  local copies, waits for them, and re-layouts: 186 us -> 42.7 us
  matrix products: 135 us -> 12.5 us
  starting transfers between devices: 0.38 us -> 98.1 us
  other arithmetic: 74.7 us -> 42.3 us
  between operations: 15.2 us -> 2 us
    psum x4 -> x0, waiting for transfers between devices: 658 us -> none  [the longest x1 257 us: shards(): expert_tok = lax.psum(token_part, 'tensor') + out_bias_tok]
    pallas_call x0 -> x7, Pallas kernels: none -> 256 us  [the longest x3 96.7 us: attention_backward(): pl.pallas_call(functools.partial(backward_kernel, sums is None), grid_spe...]
    ppermute x0 -> x56, waiting for transfers between devices: none -> 175 us  [send(): return lax.ppermute(values, AXES, table)]
    psum x1 -> x0, blocking collectives: 158 us -> none  [shards(): lax.psum((grad_attn_gain, grad_attn_shift, grad_qkv_weight, grad_qv_bias,...]
    dot_general x28 -> x3, matrix products: 131 us -> 12.5 us  [the longest x1 7.23 us: position_bias(): rows = jnp.dot(lookup, table, precision=lax.Precision.HIGHEST)]
    ppermute x0 -> x56, starting transfers between devices: none -> 98.1 us  [send(): return lax.ppermute(values, AXES, table)]
    gather x4 -> x0, local copies, waits for them, and re-layouts: 71.9 us -> none  [the longest x1 18.4 us: shards(): jnp.concatenate([grad_tok, zero_row], axis=0)[sources]]
    reduce_sum x12 -> x5, other arithmetic: 47.6 us -> 0.94 us  [the longest x1 0.55 us: sort_plan(): offset = jnp.sum(earlier[:, :, None] * groups[None], axis=1)]
  transfers between devices with their start and end apart: 4 -> 56, of which waited for: 4 -> 23; matrix products, arithmetic and copies ran while one was open for 7% -> 12% of each run, Pallas kernels for 0% -> 17%
where the time goes in v1:
time: 640 us; the launch traced here: 629 us
  Pallas kernels  256 us (40%)
  waiting for transfers between devices  175 us (27%)
  starting transfers between devices  98.1 us (15%)
  local copies, waits for them, and re-layouts  42.7 us (7%)
  other arithmetic  42.3 us (7%)
  matrix products  12.5 us (2%)
    ppermute x56, waiting for transfers between devices, send(): return lax.ppermute(values, AXES, table)  175 us
    ppermute x56, starting transfers between devices, send(): return lax.ppermute(values, AXES, table)  98.1 us
    pallas_call x3, Pallas kernels, attention_backward(): pl.pallas_call(functools.partial(backward_kernel, sums is None), grid_spe...  96.7 us
    pallas_call x1, Pallas kernels, experts(): pl.pallas_call(experts_kernel, grid_spec=pltpu.PrefetchScalarGridSpec(num...  86 us
    pallas_call x1, Pallas kernels, attention_forward(): pl.pallas_call(attention_kernel, grid_spec=pltpu.PrefetchScalarGridSpec(n...  59.1 us
    pallas_call x2, Pallas kernels, assemble(): pl.pallas_call(assemble_kernel, grid_spec=pltpu.PrefetchScalarGridSpec(nu...  14.6 us
  transfers between devices with their start and end apart: 56, of which 23 were waited for; matrix products, arithmetic and copies ran while one was open for 12% of the time, Pallas kernels for 17%

profile of v1, /device:TPU:0, one launch (start us, length us, event | category | flops | bytes accessed | tf_op | source)
XLA Modules:
  0.0 628.6 jit_solution(5580463228544405769)
XLA Ops:
  3.5 3.2 collective-permute-start
  6.7 13.6 %collective-permute-done = f32[392,384]{1,0:T(8,128)S(1)} collective-permute-done((f32[392,384]{1,0:T(8,128)S(1)}, f32[392,384]{1,0:T(8,128)S(1)}, u32[]{:S(2)}, u32[]{:S(2)}) %collective-permute-start) | collective-permute-done | bytes 602144 | tf_op jit(solution)/shard_map/ppermute | solution.py:544
  20.4 3.0 copy.101.ids_ref
  29.1 7.2 %convolution_bitcast_fusion = f32[3,64,4,64]{3,2,1,0:T(4,128)S(1)} fusion(f32[64,64,169,1]{2,1,0,3:T(8,128)} %constant.292, f32[3,4,169,1]{2,1,0,3:T(4,128)S(1)} %reshape.285), kind=kOutput, calls=%fused_computation.11 | convolution fusion | flops 99680256 | bytes 2973616 | tf_op jit(solution)/shard_map/dot_general | solution.py:512
  40.9 59.1 %attention_forward.1 = (f32[2352,384]{1,0:T(8,128)}, f32[2352,384]{1,0:T(8,128)}, f32[2352,384]{1,0:T(8,128)}, f32[2352,1]{1,0:T(8,128)}, bf16[2352,384]{1,0:T(8...) custom-call(s32[1]{0:T(128)} %bitcast.core, bf16[4704,384]{1,0:T(8,128)(2,1)} %x_ref.7, ...), custom_call_target="tpu_custom_call" | custom-call | flops 8000000000 | bytes 40000000 | tf_op jit(solution)/shard_map/attention_forward/pallas_call | solution.py:181
  101.9 2.2 convert_element_type.92.pos_col
  107.5 86.0 %experts.1 = (f32[3072,384]{1,0:T(8,128)}, f32[3072,384]{1,0:T(8,128)}, f32[8,384]{1,0:T(8,128)}, f32[8,384]{1,0:T(8,128)}, f32[2352,384]{1,0:T(8,128)}, /*index...) custom-call(s32[1]{0:T(128)} %bitcast.core, ...), custom_call_target="tpu_custom_call" | custom-call | flops 24999999488 | bytes 60000000 | tf_op jit(solution)/shard_map/experts/pallas_call | solution.py:328
  193.5 3.9 constant_dynamic-slice_fusion.4
  198.3 3.7 constant_dynamic-slice_fusion.10
  202.1 2.7 collective-permute-start.30
  204.8 2.3 collective-permute-start.44
  207.1 21.0 %collective-permute-done.43 = f32[768,384]{1,0:T(8,128)S(1)} collective-permute-done((f32[768,384]{1,0:T(8,128)}, f32[768,384]{1,0:T(8,128)S(1)}, u32[]{:S(2)}, u32[]{:S(2)}) %collective-permute-start.43) | collective-permute-done | bytes 1179680 | tf_op jit(solution)/shard_map/ppermute | solution.py:544
  229.7 2.3 collective-permute-start.31
  233.6 24.2 %collective-permute-done.44 = f32[768,384]{1,0:T(8,128)S(1)} collective-permute-done((f32[768,384]{1,0:T(8,128)S(1)}, f32[768,384]{1,0:T(8,128)S(1)}, u32[]{:S(2)}, u32[]{:S(2)}) %collective-permute-start.44) | collective-permute-done | bytes 1179680 | tf_op jit(solution)/shard_map/ppermute | solution.py:544
  258.9 2.2 add_add_fusion
  263.6 18.5 %collective-permute-done.31 = f32[768,384]{1,0:T(8,128)} collective-permute-done((f32[768,384]{1,0:T(8,128)}, f32[768,384]{1,0:T(8,128)}, u32[]{:S(2)}, u32[]{:S(2)}) %collective-permute-start.31) | collective-permute-done | bytes 1179680 | tf_op jit(solution)/shard_map/ppermute | solution.py:544
  282.1 2.2 add_add_fusion.1
  284.3 1.8 collective-permute-start.33
  286.1 3.7 collective-permute-start.47
  293.2 6.7 %collective-permute-done.47 = f32[192,384]{1,0:T(8,128)} collective-permute-done((f32[192,384]{1,0:T(8,128)}, f32[192,384]{1,0:T(8,128)}, u32[]{:S(2)}, u32[]{:S(2)}) %collective-permute-start.47) | collective-permute-done | bytes 294944 | tf_op jit(solution)/shard_map/ppermute | solution.py:544
  299.9 1.9 collective-permute-start.35
  304.7 5.0 slice_add_fusion
  309.7 2.7 collective-permute-start.6
  315.5 25.5 %collective-permute-done.36 = f32[192,384]{1,0:T(8,128)} collective-permute-done((f32[192,384]{1,0:T(8,128)S(1)}, f32[192,384]{1,0:T(8,128)}, u32[]{:S(2)}, u32[]{:S(2)}) %collective-permute-start.36) | collective-permute-done | bytes 294944 | tf_op jit(solution)/shard_map/ppermute | solution.py:544
  341.1 1.7 constant_dynamic-update-slice_fusion.15
  342.8 2.6 collective-permute-start.37
  345.4 1.7 reduce.3
  347.2 1.7 reduce.2
  348.9 2.2 collective-permute-start.12
  351.1 3.0 collective-permute-done.12
  354.2 3.7 collective-permute-start.51
  360.0 1.9 collective-permute-start.38
  362.0 8.3 %collective-permute-done.51 = f32[192,384]{1,0:T(8,128)S(1)} collective-permute-done((f32[192,384]{1,0:T(8,128)}, f32[192,384]{1,0:T(8,128)S(1)}, u32[]{:S(2)}, u32[]{:S(2)}) %collective-permute-start.51) | collective-permute-done | bytes 294944 | tf_op jit(solution)/shard_map/ppermute | solution.py:544
  370.3 2.3 collective-permute-start.39
  372.6 5.3 add.484
  378.3 2.3 collective-permute-start.7
  380.7 31.7 %attention_backward.3 = (f32[784,384]{1,0:T(8,128)}, f32[1152,384]{1,0:T(8,128)}, f32[384,384]{1,0:T(8,128)}, f32[16,384]{1,0:T(8,128)}, f32[192,256]{1,0:T(8,128)}) custom-call(s32[1]{0:T(128)} %bitcast.core, f32[784,384]{1,0:T(8,128)} %get-tuple-element.171.gs_a, f32[784,384]{1,0:T(8,128)} %collective-permute-done.6.gs_b, f32[2352,1]{1,0:T(8,128)} %reshape.289.gg_ref, ...), custom_call_target="tpu_custom_call" | custom-call | flops 20000000000 | bytes 50000000 | tf_op jit(solution)/shard_map/attention_backward/pallas_call | solution.py:483
  413.8 32.5 %attention_backward.4 = (f32[784,384]{1,0:T(8,128)}, f32[1152,384]{1,0:T(8,128)}, f32[384,384]{1,0:T(8,128)}, f32[16,384]{1,0:T(8,128)}, f32[192,256]{1,0:T(8,128)}) custom-call(s32[1]{0:T(128)} %bitcast.core, f32[784,384]{1,0:T(8,128)} %get-tuple-element.70.gs_a, f32[784,384]{1,0:T(8,128)} %collective-permute-done.7.gs_b, f32[2352,1]{1,0:T(8,128)} %reshape.289.gg_ref, ...), custom_call_target="tpu_custom_call" | custom-call | flops 20000000000 | bytes 50000000 | tf_op jit(solution)/shard_map/attention_backward/pallas_call | solution.py:483
  446.3 2.8 collective-permute-start.9
  449.2 32.5 %attention_backward.5 = (f32[784,384]{1,0:T(8,128)}, f32[1152,384]{1,0:T(8,128)}, f32[384,384]{1,0:T(8,128)}, f32[16,384]{1,0:T(8,128)}, f32[192,256]{1,0:T(8,128)}) custom-call(s32[1]{0:T(128)} %bitcast.core, f32[784,384]{1,0:T(8,128)} %get-tuple-element.71.gs_a, f32[784,384]{1,0:T(8,128)} %collective-permute-done.8.gs_b, f32[2352,1]{1,0:T(8,128)} %reshape.289.gg_ref, ...), custom_call_target="tpu_custom_call" | custom-call | flops 20000000000 | bytes 50000000 | tf_op jit(solution)/shard_map/attention_backward/pallas_call | solution.py:483
  483.0 5.0 fusion.19
  494.5 1.7 reduce
  496.2 2.9 collective-permute-start.54
  500.0 3.7 collective-permute-start.41
  506.6 18.1 %collective-permute-done.40 = f32[768,384]{1,0:T(8,128)} collective-permute-done((f32[768,384]{1,0:T(8,128)S(1)}, f32[768,384]{1,0:T(8,128)}, u32[]{:S(2)}, u32[]{:S(2)}) %collective-permute-start.40) | collective-permute-done | bytes 1179680 | tf_op jit(solution)/shard_map/ppermute | solution.py:544
  524.7 2.3 collective-permute-start.55
  530.5 24.4 %collective-permute-start.19 = (f32[128,384]{1,0:T(8,128)S(1)}, f32[128,384]{1,0:T(8,128)S(1)}, u32[]{:S(2)}, u32[]{:S(2)}) collective-permute-start(f32[128,384]{1,0:T(8,128)S(1)} %get-tuple-element.96), channel_id=1, source_target_pairs={{0,32},{1,33},{4,36},{5,37},{8,40},{9,41},{12,44},{13,45},{16,48},... | collective-permute-start | bytes 589832 | tf_op jit(solution)/shard_map/ppermute | solution.py:544
  554.9 5.4 multiply_add_fusion.mine
  560.3 2.0 collective-permute-done.18
  564.7 3.8 collective-permute-done.20
  570.8 1.8 collective-permute-done.21
  572.6 3.1 collective-permute-done.22
  575.9 4.0 collective-permute-done.23
  580.5 2.0 pad_maximum_fusion.mine
  582.6 2.8 collective-permute-done.24
  585.4 4.0 collective-permute-done.25
  589.5 5.6 collective-permute-done.26
  595.0 2.6 collective-permute-start.27
  597.7 2.0 pad_maximum_fusion.1.other
  599.7 7.9 %assemble.3 = f32[4704,384]{1,0:T(8,128)} custom-call(s32[1]{0:T(128)} %bitcast.core, f32[2352,384]{1,0:T(8,128)} %pad_maximum_fusion.mine, f32[2352,384]{1,0:T(8,128)} %pad_maximum_fusion.1.other), custom_call_target="tpu_custom_call" | custom-call | flops 10000000 | bytes 15000000 | tf_op jit(solution)/shard_map/assemble/pallas_call | solution.py:597
  607.6 2.4 collective-permute-start.28
  611.6 1.9 collective-permute-done.28
  613.6 3.8 collective-permute-done.29
  621.6 6.8 %assemble.2 = bf16[4704,384]{1,0:T(8,128)(2,1)} custom-call(s32[1]{0:T(128)} %bitcast.core, f32[2352,384]{1,0:T(8,128)} %multiply_add_fusion.mine, f32[2352,384]{1,0:T(8,128)} %collective-permute-done.10.other), custom_call_target="tpu_custom_call" | custom-call | flops 10000000 | bytes 15000000 | tf_op jit(solution)/shard_map/assemble/pallas_call | solution.py:597
  (273 shorter events, 65.7 us)
Async XLA Ops:
  3.5 16.8 %collective-permute-start = (f32[392,384]{1,0:T(8,128)S(1)}, f32[392,384]{1,0:T(8,128)S(1)}, u32[]{:S(2)}, u32[]{:S(2)}) collective-permute-start(f32[392,384]{1,0:T(8,128)S(1)} %maximum_convert_fusion), channel_id=1, source_target_pairs={{0,2},{1,3},{4,6},{5,7},{8,10},{9,11},{12,14},{13,15},{16,18},{17,... | collective-permute-start | bytes 1806344 | tf_op jit(solution)/shard_map/ppermute | solution.py:544
  6.7 21.2 %collective-permute-start.2 = (f32[392,384]{1,0:T(8,128)S(1)}, f32[392,384]{1,0:T(8,128)S(1)}, u32[]{:S(2)}, u32[]{:S(2)}) collective-permute-start(f32[392,384]{1,0:T(8,128)S(1)} %maximum_convert_fusion), channel_id=1, source_target_pairs={{0,1},{1,0},{4,5},{5,4},{8,9},{9,8},{12,13},{13,12},{16,17},{17,16... | collective-permute-start | bytes 1806344 | tf_op jit(solution)/shard_map/ppermute | solution.py:544
  20.3 7.7 %collective-permute-start.1 = (f32[392,384]{1,0:T(8,128)S(1)}, f32[392,384]{1,0:T(8,128)S(1)}, u32[]{:S(2)}, u32[]{:S(2)}) collective-permute-start(f32[392,384]{1,0:T(8,128)S(1)} %collective-permute-done), channel_id=1, source_target_pairs={{0,1},{1,0},{4,5},{5,4},{8,9},{9,8},{12,13},{13,12},{16,17},{17,16... | collective-permute-start | bytes 1806344 | tf_op jit(solution)/shard_map/ppermute | solution.py:544
  40.9 60.1 %copy-start.19 = (s32[4704,1]{0,1:T(1,128)S(1)}, s32[4704,1]{0,1:T(1,128)}, u32[]{:S(2)}) copy-start(s32[4704,1]{0,1:T(1,128)} %param.41) | copy-start | bytes 56452
  40.9 60.5 %copy-start.26 = (s32[8,8]{1,0:T(8,128)S(1)}, s32[8,8]{1,0:T(8,128)}, u32[]{:S(2)}) copy-start(s32[8,8]{1,0:T(8,128)} %constant.276.clone) | copy-start | bytes 772
  40.9 60.7 %copy-start.32 = (bf16[168,168,1]{1,0,2:T(8,128)(2,1)S(1)}, bf16[168,168,1]{1,0,2:T(8,128)(2,1)}, u32[]{:S(2)}) copy-start(bf16[168,168,1]{1,0,2:T(8,128)(2,1)} %constant.388) | copy-start | bytes 169348
  99.9 7.5 %collective-permute-start.3 = (f32[2352,384]{1,0:T(8,128)}, f32[2352,384]{1,0:T(8,128)}, u32[]{:S(2)}, u32[]{:S(2)}) collective-permute-start(f32[2352,384]{1,0:T(8,128)} %get-tuple-element.65.own_ref), channel_id=1, source_target_pairs={{0,1},{1,0},{4,5},{5,4},{8,9},{9,8},{12,13},{13,12},{16,17},{17,16... | collective-permute-start | bytes 10838024 | tf_op jit(solution)/shard_map/ppermute | solution.py:544
  197.4 30.8 %collective-permute-start.43 = (f32[768,384]{1,0:T(8,128)}, f32[768,384]{1,0:T(8,128)S(1)}, u32[]{:S(2)}, u32[]{:S(2)}) collective-permute-start(f32[768,384]{1,0:T(8,128)} %get-tuple-element.176), channel_id=1, source_target_pairs={{0,4},{1,5},{4,8},{5,9},{8,12},{9,13},{12,0},{13,1},{16,20},{17,21... | collective-permute-start | bytes 3538952 | tf_op jit(solution)/shard_map/ppermute | solution.py:544
  198.3 106.3 %collective-permute-start.5 = (f32[2352,384]{1,0:T(8,128)}, f32[2352,384]{1,0:T(8,128)}, u32[]{:S(2)}, u32[]{:S(2)}) collective-permute-start(f32[2352,384]{1,0:T(8,128)} %get-tuple-element.69), channel_id=1, source_target_pairs={{0,1},{1,0},{4,5},{5,4},{8,9},{9,8},{12,13},{13,12},{16,17},{17,16... | collective-permute-start | bytes 10838024 | tf_op jit(solution)/shard_map/ppermute | solution.py:544
  202.1 30.8 %collective-permute-start.30 = (f32[768,384]{1,0:T(8,128)S(1)}, f32[768,384]{1,0:T(8,128)S(1)}, u32[]{:S(2)}, u32[]{:S(2)}) collective-permute-start(f32[768,384]{1,0:T(8,128)S(1)} %get-tuple-element.179), channel_id=1, source_target_pairs={{0,16},{1,17},{4,20},{5,21},{8,24},{9,25},{12,28},{13,29},{16,32},... | collective-permute-start | bytes 3538952 | tf_op jit(solution)/shard_map/ppermute | solution.py:544
  204.8 53.0 %collective-permute-start.44 = (f32[768,384]{1,0:T(8,128)S(1)}, f32[768,384]{1,0:T(8,128)S(1)}, u32[]{:S(2)}, u32[]{:S(2)}) collective-permute-start(f32[768,384]{1,0:T(8,128)S(1)} %copy-done.8), channel_id=1, source_target_pairs={{0,12},{1,13},{4,0},{5,1},{8,4},{9,5},{12,8},{13,9},{16,28},{17,29... | collective-permute-start | bytes 3538952 | tf_op jit(solution)/shard_map/ppermute | solution.py:544
  228.1 30.8 %collective-permute-start.45 = (f32[768,384]{1,0:T(8,128)}, f32[768,384]{1,0:T(8,128)}, u32[]{:S(2)}, u32[]{:S(2)}) collective-permute-start(f32[768,384]{1,0:T(8,128)} %get-tuple-element.106), channel_id=1, source_target_pairs={{0,8},{1,9},{4,12},{5,13},{8,0},{9,1},{12,4},{13,5},{16,24},{17,25... | collective-permute-start | bytes 3538952 | tf_op jit(solution)/shard_map/ppermute | solution.py:544
  229.7 52.3 %collective-permute-start.31 = (f32[768,384]{1,0:T(8,128)}, f32[768,384]{1,0:T(8,128)}, u32[]{:S(2)}, u32[]{:S(2)}) collective-permute-start(f32[768,384]{1,0:T(8,128)} %get-tuple-element.177), channel_id=1, source_target_pairs={{0,48},{1,49},{4,52},{5,53},{8,56},{9,57},{12,60},{13,61},{16,0},{... | collective-permute-start | bytes 3538952 | tf_op jit(solution)/shard_map/ppermute | solution.py:544
  232.9 49.2 %collective-permute-start.32 = (f32[768,384]{1,0:T(8,128)}, f32[768,384]{1,0:T(8,128)}, u32[]{:S(2)}, u32[]{:S(2)}) collective-permute-start(f32[768,384]{1,0:T(8,128)} %get-tuple-element.101), channel_id=1, source_target_pairs={{0,32},{1,33},{4,36},{5,37},{8,40},{9,41},{12,44},{13,45},{16,48},... | collective-permute-start | bytes 3538952 | tf_op jit(solution)/shard_map/ppermute | solution.py:544
  257.9 114.7 %collective-permute-start.4 = (f32[2352,384]{1,0:T(8,128)}, f32[2352,384]{1,0:T(8,128)}, u32[]{:S(2)}, u32[]{:S(2)}) collective-permute-start(f32[2352,384]{1,0:T(8,128)} %get-tuple-element.67), channel_id=1, source_target_pairs={{0,1},{1,0},{4,5},{5,4},{8,9},{9,8},{12,13},{13,12},{16,17},{17,16... | collective-permute-start | bytes 10838024 | tf_op jit(solution)/shard_map/ppermute | solution.py:544
  262.0 27.9 %collective-permute-start.46 = (f32[192,384]{1,0:T(8,128)S(1)}, f32[192,384]{1,0:T(8,128)S(1)}, u32[]{:S(2)}, u32[]{:S(2)}) collective-permute-start(f32[192,384]{1,0:T(8,128)S(1)} %get-tuple-element.188), channel_id=1, source_target_pairs={{0,16},{1,17},{4,20},{5,21},{8,24},{9,25},{12,28},{13,29},{16,32},... | collective-permute-start | bytes 884744 | tf_op jit(solution)/shard_map/ppermute | solution.py:544
  284.3 8.0 %collective-permute-start.33 = (f32[192,384]{1,0:T(8,128)S(1)}, f32[192,384]{1,0:T(8,128)S(1)}, u32[]{:S(2)}, u32[]{:S(2)}) collective-permute-start(f32[192,384]{1,0:T(8,128)S(1)} %get-tuple-element.191), channel_id=1, source_target_pairs={{0,4},{1,5},{4,8},{5,9},{8,12},{9,13},{12,0},{13,1},{16,20},{17,21... | collective-permute-start | bytes 884744 | tf_op jit(solution)/shard_map/ppermute | solution.py:544
  286.1 13.8 %collective-permute-start.47 = (f32[192,384]{1,0:T(8,128)}, f32[192,384]{1,0:T(8,128)}, u32[]{:S(2)}, u32[]{:S(2)}) collective-permute-start(f32[192,384]{1,0:T(8,128)} %get-tuple-element.186), channel_id=1, source_target_pairs={{0,48},{1,49},{4,52},{5,53},{8,56},{9,57},{12,60},{13,61},{16,0},{... | collective-permute-start | bytes 884744 | tf_op jit(solution)/shard_map/ppermute | solution.py:544
  290.5 11.3 %collective-permute-start.48 = (f32[192,384]{1,0:T(8,128)}, f32[192,384]{1,0:T(8,128)}, u32[]{:S(2)}, u32[]{:S(2)}) collective-permute-start(f32[192,384]{1,0:T(8,128)} %get-tuple-element.107), channel_id=1, source_target_pairs={{0,32},{1,33},{4,36},{5,37},{8,40},{9,41},{12,44},{13,45},{16,48},... | collective-permute-start | bytes 884744 | tf_op jit(solution)/shard_map/ppermute | solution.py:544
  292.3 9.5 %copy-start.13 = (f32[192,384]{1,0:T(8,128)}, f32[192,384]{1,0:T(8,128)S(1)}, u32[]{:S(2)}) copy-start(f32[192,384]{1,0:T(8,128)S(1)} %collective-permute-done.33) | copy-start | bytes 884740
  292.3 20.1 %collective-permute-start.34 = (f32[192,384]{1,0:T(8,128)S(1)}, f32[192,384]{1,0:T(8,128)S(1)}, u32[]{:S(2)}, u32[]{:S(2)}) collective-permute-start(f32[192,384]{1,0:T(8,128)S(1)} %get-tuple-element.189), channel_id=1, source_target_pairs={{0,12},{1,13},{4,0},{5,1},{8,4},{9,5},{12,8},{13,9},{16,28},{17,29... | collective-permute-start | bytes 884744 | tf_op jit(solution)/shard_map/ppermute | solution.py:544
  299.9 12.5 %collective-permute-start.35 = (f32[192,384]{1,0:T(8,128)S(1)}, f32[192,384]{1,0:T(8,128)S(1)}, u32[]{:S(2)}, u32[]{:S(2)}) collective-permute-start(f32[192,384]{1,0:T(8,128)S(1)} %get-tuple-element.102), channel_id=1, source_target_pairs={{0,8},{1,9},{4,12},{5,13},{8,0},{9,1},{12,4},{13,5},{16,24},{17,25... | collective-permute-start | bytes 884744 | tf_op jit(solution)/shard_map/ppermute | solution.py:544
  303.1 10.0 %collective-permute-start.49 = (f32[192,384]{1,0:T(8,128)S(1)}, f32[192,384]{1,0:T(8,128)S(1)}, u32[]{:S(2)}, u32[]{:S(2)}) collective-permute-start(f32[192,384]{1,0:T(8,128)S(1)} %add_add_fusion.2), channel_id=1, source_target_pairs={{0,64},{1,65},{4,68},{5,69},{8,72},{9,73},{12,76},{13,77},{16,80},... | collective-permute-start | bytes 884744 | tf_op jit(solution)/shard_map/ppermute | solution.py:544
  309.7 68.6 %collective-permute-start.6 = (f32[784,384]{1,0:T(8,128)}, f32[784,384]{1,0:T(8,128)}, u32[]{:S(2)}, u32[]{:S(2)}) collective-permute-start(f32[784,384]{1,0:T(8,128)} %get-tuple-element.171.gs_a), channel_id=1, source_target_pairs={{0,2},{1,3},{4,6},{5,7},{8,10},{9,11},{12,14},{13,15},{16,18},{17,... | collective-permute-start | bytes 3612680 | tf_op jit(solution)/shard_map/ppermute | solution.py:544
  312.5 28.5 %collective-permute-start.36 = (f32[192,384]{1,0:T(8,128)S(1)}, f32[192,384]{1,0:T(8,128)}, u32[]{:S(2)}, u32[]{:S(2)}) collective-permute-start(f32[192,384]{1,0:T(8,128)S(1)} %add_add_fusion.3), channel_id=1, source_target_pairs={{0,64},{1,65},{4,68},{5,69},{8,72},{9,73},{12,76},{13,77},{16,80},... | collective-permute-start | bytes 884744 | tf_op jit(solution)/shard_map/ppermute | solution.py:544
  313.9 46.1 %collective-permute-start.50 = (f32[192,384]{1,0:T(8,128)}, f32[192,384]{1,0:T(8,128)S(1)}, u32[]{:S(2)}, u32[]{:S(2)}) collective-permute-start(f32[192,384]{1,0:T(8,128)} %get-tuple-element.108), channel_id=1, source_target_pairs={{0,16},{1,17},{4,20},{5,21},{8,24},{9,25},{12,28},{13,29},{16,32},... | collective-permute-start | bytes 884744 | tf_op jit(solution)/shard_map/ppermute | solution.py:544
  342.8 17.2 %collective-permute-start.37 = (f32[192,384]{1,0:T(8,128)}, f32[192,384]{1,0:T(8,128)S(1)}, u32[]{:S(2)}, u32[]{:S(2)}) collective-permute-start(f32[192,384]{1,0:T(8,128)} %get-tuple-element.103), channel_id=1, source_target_pairs={{0,4},{1,5},{4,8},{5,9},{8,12},{9,13},{12,0},{13,1},{16,20},{17,21... | collective-permute-start | bytes 884744 | tf_op jit(solution)/shard_map/ppermute | solution.py:544
  345.4 12.5 %copy-start.10 = (bf16[8,384]{0,1:T(8,128)(2,1)S(1)}, bf16[8,384]{0,1:T(8,128)(2,1)}, u32[]{:S(2)}) copy-start(bf16[8,384]{0,1:T(8,128)(2,1)} %copy-done.9) | copy-start | bytes 18436
  347.1 1.8 collective-permute-start.11
  348.9 5.3 collective-permute-start.12
  354.2 16.1 %collective-permute-start.51 = (f32[192,384]{1,0:T(8,128)}, f32[192,384]{1,0:T(8,128)S(1)}, u32[]{:S(2)}, u32[]{:S(2)}) collective-permute-start(f32[192,384]{1,0:T(8,128)} %get-tuple-element.108), channel_id=1, source_target_pairs={{0,48},{1,49},{4,52},{5,53},{8,56},{9,57},{12,60},{13,61},{16,0},{... | collective-permute-start | bytes 884744 | tf_op jit(solution)/shard_map/ppermute | solution.py:544
  360.0 17.9 %collective-permute-start.52 = (f32[192,384]{1,0:T(8,128)}, f32[192,384]{1,0:T(8,128)S(1)}, u32[]{:S(2)}, u32[]{:S(2)}) collective-permute-start(f32[192,384]{1,0:T(8,128)} %get-tuple-element.108), channel_id=1, source_target_pairs={{0,32},{1,33},{4,36},{5,37},{8,40},{9,41},{12,44},{13,45},{16,48},... | collective-permute-start | bytes 884744 | tf_op jit(solution)/shard_map/ppermute | solution.py:544
  360.0 131.9 %collective-permute-start.38 = (f32[192,384]{1,0:T(8,128)}, f32[192,384]{1,0:T(8,128)}, u32[]{:S(2)}, u32[]{:S(2)}) collective-permute-start(f32[192,384]{1,0:T(8,128)} %get-tuple-element.103), channel_id=1, source_target_pairs={{0,12},{1,13},{4,0},{5,1},{8,4},{9,5},{12,8},{13,9},{16,28},{17,29... | collective-permute-start | bytes 884744 | tf_op jit(solution)/shard_map/ppermute | solution.py:544
  370.3 122.7 %collective-permute-start.39 = (f32[192,384]{1,0:T(8,128)}, f32[192,384]{1,0:T(8,128)}, u32[]{:S(2)}, u32[]{:S(2)}) collective-permute-start(f32[192,384]{1,0:T(8,128)} %get-tuple-element.103), channel_id=1, source_target_pairs={{0,8},{1,9},{4,12},{5,13},{8,0},{9,1},{12,4},{13,5},{16,24},{17,25... | collective-permute-start | bytes 884744 | tf_op jit(solution)/shard_map/ppermute | solution.py:544
  377.9 127.1 %collective-permute-start.53 = (f32[768,384]{1,0:T(8,128)S(1)}, f32[768,384]{1,0:T(8,128)}, u32[]{:S(2)}, u32[]{:S(2)}) collective-permute-start(f32[768,384]{1,0:T(8,128)S(1)} %constant_dynamic-update-slice_fusion.4), channel_id=1, source_target_pairs={{0,4},{1,5},{4,8},{5,9},{8,12},{9,13},{12,0},{13,1},{16,20},{17,21... | collective-permute-start | bytes 3538952 | tf_op jit(solution)/shard_map/ppermute | solution.py:544
  378.3 34.0 %collective-permute-start.7 = (f32[784,384]{1,0:T(8,128)}, f32[784,384]{1,0:T(8,128)}, u32[]{:S(2)}, u32[]{:S(2)}) collective-permute-start(f32[784,384]{1,0:T(8,128)} %get-tuple-element.70.gs_a), channel_id=1, source_target_pairs={{0,2},{1,3},{4,6},{5,7},{8,10},{9,11},{12,14},{13,15},{16,18},{17,... | collective-permute-start | bytes 3612680 | tf_op jit(solution)/shard_map/ppermute | solution.py:544
  412.4 34.0 %collective-permute-start.8 = (f32[784,384]{1,0:T(8,128)}, f32[784,384]{1,0:T(8,128)}, u32[]{:S(2)}, u32[]{:S(2)}) collective-permute-start(f32[784,384]{1,0:T(8,128)} %get-tuple-element.71.gs_a), channel_id=1, source_target_pairs={{0,2},{1,3},{4,6},{5,7},{8,10},{9,11},{12,14},{13,15},{16,18},{17,... | collective-permute-start | bytes 3612680 | tf_op jit(solution)/shard_map/ppermute | solution.py:544
  446.3 84.2 %collective-permute-start.9 = (f32[2352,384]{1,0:T(8,128)}, f32[2352,384]{1,0:T(8,128)}, u32[]{:S(2)}, u32[]{:S(2)}) collective-permute-start(f32[2352,384]{1,0:T(8,128)} %add.484), channel_id=1, source_target_pairs={{0,2},{1,3},{4,6},{5,7},{8,10},{9,11},{12,14},{13,15},{16,18},{17,... | collective-permute-start | bytes 10838024 | tf_op jit(solution)/shard_map/ppermute | solution.py:544
  492.0 8.0 %collective-permute-start.16 = (f32[408,384]{1,0:T(8,128)}, f32[408,384]{1,0:T(8,128)}, u32[]{:S(2)}, u32[]{:S(2)}) collective-permute-start(f32[408,384]{1,0:T(8,128)} %pad_maximum_fusion.3), channel_id=1, source_target_pairs={{0,1},{1,0},{4,5},{5,4},{8,9},{9,8},{12,13},{13,12},{16,17},{17,16... | collective-permute-start | bytes 1880072 | tf_op jit(solution)/shard_map/ppermute | solution.py:544
  494.0 30.8 %collective-permute-start.40 = (f32[768,384]{1,0:T(8,128)S(1)}, f32[768,384]{1,0:T(8,128)}, u32[]{:S(2)}, u32[]{:S(2)}) collective-permute-start(f32[768,384]{1,0:T(8,128)S(1)} %constant_dynamic-update-slice_fusion.12), channel_id=1, source_target_pairs={{0,16},{1,17},{4,20},{5,21},{8,24},{9,25},{12,28},{13,29},{16,32},... | collective-permute-start | bytes 3538952 | tf_op jit(solution)/shard_map/ppermute | solution.py:544
  496.2 33.1 %collective-permute-start.54 = (f32[768,384]{1,0:T(8,128)S(1)}, f32[768,384]{1,0:T(8,128)S(1)}, u32[]{:S(2)}, u32[]{:S(2)}) collective-permute-start(f32[768,384]{1,0:T(8,128)S(1)} %constant_dynamic-update-slice_fusion.4), channel_id=1, source_target_pairs={{0,12},{1,13},{4,0},{5,1},{8,4},{9,5},{12,8},{13,9},{16,28},{17,29... | collective-permute-start | bytes 3538952 | tf_op jit(solution)/shard_map/ppermute | solution.py:544
  500.0 63.2 %collective-permute-start.41 = (f32[768,384]{1,0:T(8,128)S(1)}, f32[768,384]{1,0:T(8,128)S(1)}, u32[]{:S(2)}, u32[]{:S(2)}) collective-permute-start(f32[768,384]{1,0:T(8,128)S(1)} %constant_dynamic-update-slice_fusion.12), channel_id=1, source_target_pairs={{0,48},{1,49},{4,52},{5,53},{8,56},{9,57},{12,60},{13,61},{16,0},{... | collective-permute-start | bytes 3538952 | tf_op jit(solution)/shard_map/ppermute | solution.py:544
  505.0 23.6 %collective-permute-start.17 = (f32[128,384]{1,0:T(8,128)S(1)}, f32[128,384]{1,0:T(8,128)S(1)}, u32[]{:S(2)}, u32[]{:S(2)}) collective-permute-start(f32[128,384]{1,0:T(8,128)S(1)} %get-tuple-element.198), channel_id=1, source_target_pairs={{0,16},{1,17},{4,20},{5,21},{8,24},{9,25},{12,28},{13,29},{16,32},... | collective-permute-start | bytes 589832 | tf_op jit(solution)/shard_map/ppermute | solution.py:544
  505.1 49.8 %copy-start.2 = (f32[2352,384]{1,0:T(8,128)S(1)}, f32[2352,384]{1,0:T(8,128)}, u32[]{:S(2)}) copy-start(f32[2352,384]{1,0:T(8,128)} %get-tuple-element.63) | copy-start | bytes 10838020
  524.7 45.4 %collective-permute-start.55 = (f32[768,384]{1,0:T(8,128)S(1)}, f32[768,384]{1,0:T(8,128)S(1)}, u32[]{:S(2)}, u32[]{:S(2)}) collective-permute-start(f32[768,384]{1,0:T(8,128)S(1)} %constant_dynamic-update-slice_fusion.4), channel_id=1, source_target_pairs={{0,8},{1,9},{4,12},{5,13},{8,0},{9,1},{12,4},{13,5},{16,24},{17,25... | collective-permute-start | bytes 3538952 | tf_op jit(solution)/shard_map/ppermute | solution.py:544
  528.6 47.1 %collective-permute-start.42 = (f32[768,384]{1,0:T(8,128)S(1)}, f32[768,384]{1,0:T(8,128)S(1)}, u32[]{:S(2)}, u32[]{:S(2)}) collective-permute-start(f32[768,384]{1,0:T(8,128)S(1)} %constant_dynamic-update-slice_fusion.12), channel_id=1, source_target_pairs={{0,32},{1,33},{4,36},{5,37},{8,40},{9,41},{12,44},{13,45},{16,48},... | collective-permute-start | bytes 3538952 | tf_op jit(solution)/shard_map/ppermute | solution.py:544
  529.4 33.0 %collective-permute-start.18 = (f32[128,384]{1,0:T(8,128)S(1)}, f32[128,384]{1,0:T(8,128)S(1)}, u32[]{:S(2)}, u32[]{:S(2)}) collective-permute-start(f32[128,384]{1,0:T(8,128)S(1)} %get-tuple-element.196), channel_id=1, source_target_pairs={{0,48},{1,49},{4,52},{5,53},{8,56},{9,57},{12,60},{13,61},{16,0},{... | collective-permute-start | bytes 589832 | tf_op jit(solution)/shard_map/ppermute | solution.py:544
  530.5 31.9 %collective-permute-start.19 = (f32[128,384]{1,0:T(8,128)S(1)}, f32[128,384]{1,0:T(8,128)S(1)}, u32[]{:S(2)}, u32[]{:S(2)}) collective-permute-start(f32[128,384]{1,0:T(8,128)S(1)} %get-tuple-element.96), channel_id=1, source_target_pairs={{0,32},{1,33},{4,36},{5,37},{8,40},{9,41},{12,44},{13,45},{16,48},... | collective-permute-start | bytes 589832 | tf_op jit(solution)/shard_map/ppermute | solution.py:544
  562.3 59.3 %collective-permute-start.10 = (f32[2352,384]{1,0:T(8,128)}, f32[2352,384]{1,0:T(8,128)}, u32[]{:S(2)}, u32[]{:S(2)}) collective-permute-start(f32[2352,384]{1,0:T(8,128)} %multiply_add_fusion.mine), channel_id=1, source_target_pairs={{0,1},{1,0},{4,5},{5,4},{8,9},{9,8},{12,13},{13,12},{16,17},{17,16... | collective-permute-start | bytes 10838024 | tf_op jit(solution)/shard_map/ppermute | solution.py:544
  562.4 35.2 %collective-permute-start.13 = (f32[784,384]{1,0:T(8,128)S(1)}, f32[784,384]{1,0:T(8,128)S(1)}, u32[]{:S(2)}, u32[]{:S(2)}) collective-permute-start(f32[784,384]{1,0:T(8,128)S(1)} %copy-done.4), channel_id=1, source_target_pairs={{0,1},{1,0},{4,5},{5,4},{8,9},{9,8},{12,13},{13,12},{16,17},{17,16... | collective-permute-start | bytes 3612680 | tf_op jit(solution)/shard_map/ppermute | solution.py:544
  563.1 5.4 collective-permute-start.20
  564.6 11.1 %copy-start.6 = (f32[784,384]{1,0:T(8,128)S(1)}, f32[784,384]{1,0:T(8,128)}, u32[]{:S(2)}) copy-start(f32[784,384]{1,0:T(8,128)} %get-tuple-element.89) | copy-start | bytes 3612676
  568.5 4.1 collective-permute-start.21
  570.1 5.6 collective-permute-start.22
  570.8 11.7 %copy-start = (f32[3072,384]{1,0:T(8,128)}, f32[3072,384]{1,0:T(8,128)S(1)}, u32[]{:S(2)}) copy-start(f32[3072,384]{1,0:T(8,128)S(1)} %constant_dynamic-update-slice_fusion) | copy-start | bytes 14155780
  572.6 25.1 %collective-permute-start.14 = (f32[784,384]{1,0:T(8,128)S(1)}, f32[784,384]{1,0:T(8,128)S(1)}, u32[]{:S(2)}, u32[]{:S(2)}) collective-permute-start(f32[784,384]{1,0:T(8,128)S(1)} %copy-done.5), channel_id=1, source_target_pairs={{0,1},{1,0},{4,5},{5,4},{8,9},{9,8},{12,13},{13,12},{16,17},{17,16... | collective-permute-start | bytes 3612680 | tf_op jit(solution)/shard_map/ppermute | solution.py:544
  575.7 22.0 %collective-permute-start.15 = (f32[784,384]{1,0:T(8,128)S(1)}, f32[784,384]{1,0:T(8,128)S(1)}, u32[]{:S(2)}, u32[]{:S(2)}) collective-permute-start(f32[784,384]{1,0:T(8,128)S(1)} %copy-done.6), channel_id=1, source_target_pairs={{0,1},{1,0},{4,5},{5,4},{8,9},{9,8},{12,13},{13,12},{16,17},{17,16... | collective-permute-start | bytes 3612680 | tf_op jit(solution)/shard_map/ppermute | solution.py:544
  575.7 4.2 collective-permute-start.23
  580.0 5.4 collective-permute-start.24
  585.4 4.1 collective-permute-start.25
  589.4 5.6 collective-permute-start.26
  595.0 15.0 %collective-permute-start.27 = (f32[128,384]{1,0:T(8,128)S(1)}, f32[128,384]{1,0:T(8,128)S(1)}, u32[]{:S(2)}, u32[]{:S(2)}) collective-permute-start(f32[128,384]{1,0:T(8,128)S(1)} %constant_dynamic-update-slice_fusion.20), channel_id=1, source_target_pairs={{0,16},{1,17},{4,20},{5,21},{8,24},{9,25},{12,28},{13,29},{16,32},... | collective-permute-start | bytes 589832 | tf_op jit(solution)/shard_map/ppermute | solution.py:544
  607.6 6.0 collective-permute-start.28
  610.1 7.3 %collective-permute-start.29 = (f32[128,384]{1,0:T(8,128)S(1)}, f32[128,384]{1,0:T(8,128)S(1)}, u32[]{:S(2)}, u32[]{:S(2)}) collective-permute-start(f32[128,384]{1,0:T(8,128)S(1)} %constant_dynamic-update-slice_fusion.20), channel_id=1, source_target_pairs={{0,32},{1,33},{4,36},{5,37},{8,40},{9,41},{12,44},{13,45},{16,48},... | collective-permute-start | bytes 589832 | tf_op jit(solution)/shard_map/ppermute | solution.py:544
  (25 other events, 114.1 us)

commit v2 on v1

v2 whole, which is shorter than its diff:
```python
import functools
import math

import jax
import jax.numpy as jnp
import numpy as np
from jax import lax
from jax.experimental import pallas as pl
from jax.experimental.pallas import tpu as pltpu
from jax.sharding import PartitionSpec as P

F32 = jnp.float32
LOW = jnp.bfloat16
D = 384
HEADS = 12
EXPERTS = 8
SIDE = 14
WINDOW = 7
IMAGE = 196
HALF = 2352
BLOCK = 784
BLOCKS = 3
PADDED = 256
SLICE = 208
TILE = 168
TILES = 28
HALF_TILES = 14
GROUPS = 28
SORTED = 224
RUN = 7
STEPS_HALF = HALF_TILES // RUN
DISPATCH = 2 * STEPS_HALF
SLOTS = 960
CHUNK = 240
STORE = EXPERTS * SLOTS + 8
CLEAR = 248
MASK_FILL = -1e30
SCALE = 32 ** (-0.5)
VMEM = 60 * 1024 * 1024


def layout_consts():
    cell = np.arange(IMAGE)
    row = (cell // SIDE - WINDOW // 2) % SIDE
    col = (cell % SIDE - WINDOW // 2) % SIDE
    slot = (row // WINDOW * 2 + col // WINDOW) * 64 + row % WINDOW * WINDOW + col % WINDOW
    place = np.zeros((4, PADDED, SLICE), np.float32)
    for k in range(4):
        place[k, slot, 4 * k + cell] = 1.0
    part = lambda v: (v >= SIDE - WINDOW) * 1 + (v >= SIDE - WINDOW // 2) * 1
    label = np.full((PADDED,), -1)
    label[slot] = part(row) * 3 + part(col)
    label = label.reshape(4, 64)
    real = np.arange(64) < WINDOW * WINDOW
    meet = (label[:, :, None] == label[:, None, :]) | ~real[None, :, None]
    fill = np.where(meet & real[None, None, :], 0.0, MASK_FILL).astype(np.float32)
    fill = np.tile(fill, (1, 1, 4))
    spot = np.arange(49)
    entry = (spot[:, None] // 7 - spot[None, :] // 7 + 6) * 13 + spot[:, None] % 7 - spot[None, :] % 7 + 6
    lookup = np.zeros((64, 64, 169), np.float32)
    lookup[spot[:, None], spot[None, :], entry] = 1.0
    heads = (np.arange(256)[:, None] // 64 == np.arange(128)[None, :] // 32).astype(np.float32)
    segment = (np.arange(256)[:, None] // 64 == np.arange(256)[None, :] // 64).astype(np.float32)
    return place, fill, lookup.reshape(4096, 169), heads, segment


def nn(a, b):
    return lax.dot_general(a, b, (((1,), (0,)), ((), ())), preferred_element_type=F32)


def nt(a, b):
    return lax.dot_general(a, b, (((1,), (1,)), ((), ())), preferred_element_type=F32)


def tn(a, b):
    return lax.dot_general(a, b, (((0,), (0,)), ((), ())), preferred_element_type=F32)


def norm_parts(values):
    centre = values - jnp.mean(values, axis=-1, keepdims=True)
    inverse = lax.rsqrt(jnp.mean(centre * centre, axis=-1, keepdims=True) + 1e-5)
    return centre * inverse, inverse


def norm_back(upstream, unit, inverse, gain):
    scaled = upstream * gain
    return inverse * (
        scaled
        - jnp.mean(scaled, axis=-1, keepdims=True)
        - unit * jnp.mean(scaled * unit, axis=-1, keepdims=True)
    )


def column_sum(values):
    return jnp.sum(values, axis=0, keepdims=True)


def router_softmax(second, router):
    logits = nn(second, router)
    lane = lax.broadcasted_iota(jnp.int32, logits.shape, 1)
    logits = jnp.where(lane < EXPERTS, logits, MASK_FILL)
    power = jnp.exp(logits - jnp.max(logits, axis=-1, keepdims=True))
    return power / jnp.sum(power, axis=-1, keepdims=True), lane


def expand(part, heads):
    return jnp.concatenate([part] * 4, axis=0) * heads


def attention_kernel(
    core, x_ref, ids_ref, attn_gain, attn_shift, wqkv_wide, bqkv, bias, place, place_t, heads, segment,
    wproj_wide, bproj, moe_gain, moe_shift, router, out_bias,
    hidden_ref, base_ref, second_ref, gate_ref, mixed_ref, qkv_ref, prob_ref, window_ref,
    low_scr, raster_scr, wqkv, wproj, power_scr,
):
    @pl.when(pl.program_id(0) == 0)
    def _():
        wqkv[...] = wqkv_wide[...].T.astype(LOW)
        wproj[...] = wproj_wide[...].astype(LOW)

    x = x_ref[...].astype(F32)
    unit, _ = norm_parts(x)
    low_scr[...] = (unit * attn_gain[...] + attn_shift[...]).astype(LOW)
    raster_scr[...] = jnp.zeros_like(raster_scr)
    lane = lax.broadcasted_iota(jnp.int32, (64, 128), 1)
    left = lane < 64

    def project(k, carry):
        start = pl.multiple_of(k * 192, 64)
        rows = nn(place[k], low_scr[pl.ds(start, SLICE), :]).astype(LOW)
        qkv = (nn(rows, wqkv[...]) + bqkv[...]).astype(LOW)
        qkv_ref[pl.ds(pl.multiple_of(k * PADDED, PADDED), PADDED), :] = qkv
        return carry

    def scores_of(k, w, g):
        at = pl.ds(pl.multiple_of(k * PADDED + w * 64, 64), 64)
        q = qkv_ref[at, g * 128 : g * 128 + 128]
        kx = expand(qkv_ref[at, D + g * 128 : D + g * 128 + 128], heads[...])
        return nt(q, kx) * SCALE + bias[w * 3 + g]

    def finish(k):
        spot = pl.multiple_of(k * 768, 64)
        total = nn(power_scr[...], segment[...])
        prob_ref[pl.ds(spot, 768), :] = (power_scr[...].astype(F32) / total).astype(LOW)
        for w in range(4):
            at = pl.ds(pl.multiple_of(k * PADDED + w * 64, 64), 64)
            parts = []
            for g in range(3):
                vx = expand(qkv_ref[at, 2 * D + g * 128 : 2 * D + g * 128 + 128], heads[...])
                prob = prob_ref[pl.ds(pl.multiple_of(spot + (w * 3 + g) * 64, 64), 64), :]
                parts.append(nn(prob, vx).astype(LOW))
            window_ref[at, :] = jnp.concatenate(parts, axis=1)
        mixed = window_ref[pl.ds(pl.multiple_of(k * PADDED, PADDED), PADDED), :]
        raster_scr[pl.ds(pl.multiple_of(k * 192, 64), SLICE), :] += nn(place_t[k], mixed)
        return total

    def image(k, bounds):
        project(k, 0)
        for w in range(4):
            for g in range(3):
                power_scr[(w * 3 + g) * 64 : (w * 3 + g) * 64 + 64, :] = jnp.exp(scores_of(k, w, g)).astype(LOW)
        total = finish(k).reshape(96, 8, 256)
        return jnp.minimum(bounds[0], jnp.min(total, axis=0)), jnp.maximum(bounds[1], jnp.max(total, axis=0))

    def image_shifted(k, carry):
        for w in range(4):
            for g in range(3):
                scores = scores_of(k, w, g)
                power = []
                for c in range(2):
                    piece = scores[:, c * 128 : c * 128 + 128]
                    first = jnp.max(jnp.where(left, piece, 2 * MASK_FILL), axis=-1, keepdims=True)
                    other = jnp.max(jnp.where(left, 2 * MASK_FILL, piece), axis=-1, keepdims=True)
                    power.append(jnp.exp(piece - jnp.where(left, first, other)))
                power_scr[(w * 3 + g) * 64 : (w * 3 + g) * 64 + 64, :] = jnp.concatenate(power, axis=1).astype(LOW)
        finish(k)
        return carry

    least, most = lax.fori_loop(0, 4, image, (jnp.full((8, 256), 1.0, F32), jnp.full((8, 256), 1.0, F32)))
    safe = (jnp.min(least) > 1e-25) & (jnp.max(most) < 1e25)

    @pl.when(jnp.logical_not(safe))
    def _():
        raster_scr[...] = jnp.zeros_like(raster_scr)
        lax.fori_loop(0, 4, image_shifted, 0)

    mixed = raster_scr[...].astype(LOW)
    mixed_ref[...] = mixed
    hidden = x + (nn(mixed, wproj[...]) + bproj[...])
    hidden_ref[...] = hidden
    unit, _ = norm_parts(hidden)
    second = (unit * moe_gain[...] + moe_shift[...]).astype(LOW)
    second_ref[...] = second.astype(F32)
    probs, lanes = router_softmax(second, router[...])
    chosen = lanes == ids_ref[...]
    gate = jnp.sum(jnp.where(chosen, probs, 0.0), axis=-1, keepdims=True)
    gate_ref[...] = gate
    base_ref[...] = hidden + gate * nn(chosen.astype(F32).astype(LOW), out_bias[...])


def whole(shape):
    return pl.BlockSpec(shape, lambda *_: (0,) * len(shape))


def attention_forward(core, x, ids, consts, weights, bias):
    place, place_t, heads, segment, _ = consts
    at_block = lambda width: pl.BlockSpec((BLOCK, width), lambda i, s: (s[0] * BLOCKS + i, 0))
    rows = lambda height, width: pl.BlockSpec((height, width), lambda i, s: (i, 0))
    fixed = [weights[n] for n in ("attn_gain", "attn_shift", "wqkv", "bqkv")]
    tail = [weights[n] for n in ("wproj", "bproj", "moe_gain", "moe_shift", "router", "out_bias_pad")]
    operands = fixed + [bias, place, place_t, heads, segment] + tail
    return pl.pallas_call(
        attention_kernel,
        grid_spec=pltpu.PrefetchScalarGridSpec(
            num_scalar_prefetch=1,
            grid=(BLOCKS,),
            in_specs=[at_block(D), at_block(1)] + [whole(v.shape) for v in operands],
            out_specs=[
                rows(BLOCK, D),
                rows(BLOCK, D),
                rows(BLOCK, D),
                rows(BLOCK, 1),
                rows(BLOCK, D),
                rows(4 * PADDED, 3 * D),
                rows(48 * 64, 256),
                rows(4 * PADDED, D),
            ],
            scratch_shapes=[
                pltpu.VMEM((BLOCK, D), LOW),
                pltpu.VMEM((BLOCK, D), F32),
                pltpu.VMEM((D, 3 * D), LOW),
                pltpu.VMEM((D, D), LOW),
                pltpu.VMEM((768, 256), LOW),
            ],
        ),
        out_shape=[
            jax.ShapeDtypeStruct((HALF, D), F32),
            jax.ShapeDtypeStruct((HALF, D), F32),
            jax.ShapeDtypeStruct((HALF, D), F32),
            jax.ShapeDtypeStruct((HALF, 1), F32),
            jax.ShapeDtypeStruct((HALF, D), LOW),
            jax.ShapeDtypeStruct((BLOCKS * 4 * PADDED, 3 * D), LOW),
            jax.ShapeDtypeStruct((BLOCKS * 48 * 64, 256), LOW),
            jax.ShapeDtypeStruct((BLOCKS * 4 * PADDED, D), LOW),
        ],
        compiler_params=pltpu.CompilerParams(vmem_limit_bytes=VMEM),
        cost_estimate=pl.CostEstimate(flops=1_000_000, bytes_accessed=100_000, transcendentals=0),
        name="attention_forward",
    )(core, x, ids, *operands)


def gelu_parts(values):
    size = jnp.abs(values)
    decay = jnp.exp(-0.5 * values * values)
    t = 1.0 / (1.0 + (0.3275911 / math.sqrt(2.0)) * size)
    poly = t * (0.254829592 + t * (-0.284496736 + t * (1.421413741 + t * (-1.453152027 + t * 1.061405429))))
    half = 0.5 * poly * decay
    cdf = jnp.where(values >= 0.0, 1.0 - half, half)
    return values * cdf, cdf + values * decay * (1.0 / math.sqrt(2.0 * math.pi))


def experts_kernel(
    core, dest, chunks,
    own_ref, other_ref, g_ref, meta_ref, router_t, w_in, b_in, w_out,
    grad_in, grad_out, in_bias, out_bias, act_ref, gs_theirs, gg_theirs, gs_mine, gg_mine,
    store,
):
    step = pl.program_id(0)
    undo = DISPATCH + EXPERTS

    def first_tile(j, flip):
        half = jnp.where(j < STEPS_HALF, flip, 1 - flip)
        return half * HALF_TILES + j % STEPS_HALF * RUN

    @pl.when(step == 0)
    def _():
        def clear(j, carry):
            store[pl.ds(pl.multiple_of(j * CLEAR, 8), CLEAR), :] = jnp.zeros((CLEAR, 2 * D), F32)
            return carry

        lax.fori_loop(0, STORE // CLEAR, clear, 0)

    @pl.when(step < DISPATCH)
    def _():
        begin = first_tile(step, core[0])
        for r in range(RUN):
            second = jnp.where(step < STEPS_HALF, own_ref[r], other_ref[r]).astype(LOW)
            logits = nt(router_t[...], second)
            kind = lax.broadcasted_iota(jnp.int32, logits.shape, 0)
            logits = jnp.where(kind < EXPERTS, logits, MASK_FILL)
            power = jnp.exp(logits - jnp.max(logits, axis=0, keepdims=True))
            chosen = jnp.where(kind == meta_ref[r, 1:2, :], power, 0.0)
            gate = jnp.sum(chosen, axis=0, keepdims=True) / jnp.sum(power, axis=0, keepdims=True)
            high = gate.astype(LOW).astype(F32)
            spot = lax.broadcasted_iota(jnp.int32, (SORTED, TILE), 0)
            here = spot == meta_ref[r, 0:1, :]
            pick = jnp.where(here, 1.0, 0.0).astype(LOW)
            pick_high = jnp.where(here, high, 0.0).astype(LOW)
            pick_rest = jnp.where(here, gate - high, 0.0).astype(LOW)
            moved = jnp.concatenate([nn(pick, second), nn(pick_high, g_ref[r]) + nn(pick_rest, g_ref[r])], axis=1)
            for j in range(GROUPS):
                at = pl.multiple_of(dest[(begin + r) * GROUPS + j] * 8, 8)
                store[pl.ds(at, 8), :] = moved[j * 8 : j * 8 + 8, :]

    @pl.when((step >= DISPATCH) & (step < undo))
    def _():
        e = step - DISPATCH
        grad_in[...] = jnp.zeros_like(grad_in)
        grad_out[...] = jnp.zeros_like(grad_out)
        lane = lax.broadcasted_iota(jnp.int32, (CHUNK, 128), 1)

        def chunk(c, sums):
            at = pl.ds(pl.multiple_of(e * SLOTS + c * CHUNK, 16), CHUNK)
            buffer = store[at, :D].astype(LOW)
            grad = store[at, D:].astype(LOW)
            act, slope = gelu_parts(nn(buffer, w_in[0]) + b_in[pl.ds(e, 1), :].astype(F32))
            act = act.astype(LOW)
            act_ref[pl.ds(pl.multiple_of(c * CHUNK, 16), CHUNK), :] = act
            grad_act = nt(grad, w_out[0])
            gate_grad = jnp.sum(act.astype(F32) * grad_act, axis=-1, keepdims=True)
            high = gate_grad.astype(LOW).astype(F32)
            grad_pre = (grad_act * slope).astype(LOW)
            store[at, :D] = nt(grad_pre, w_in[0])
            store[at, D : D + 128] = jnp.where(lane == 0, high, gate_grad - high)
            grad_in[...] += tn(buffer, grad_pre)
            grad_out[...] += tn(act, grad)
            return sums[0] + column_sum(grad_pre.astype(F32)), sums[1] + column_sum(grad.astype(F32))

        zero = jnp.zeros((1, D), F32)
        sums = lax.fori_loop(0, chunks[e], chunk, (zero, zero))
        in_bias[pl.ds(e, 1), :] = sums[0]
        out_bias[pl.ds(e, 1), :] = sums[1]

    def collect(gs_ref, gg_ref):
        begin = first_tile(step - undo, 1 - core[0])
        ones = jnp.where(lax.broadcasted_iota(jnp.int32, (8, 128), 1) < 2, 1.0, 0.0).astype(LOW)
        for r in range(RUN):
            tile = (begin + r) * GROUPS
            rows = [store[pl.ds(pl.multiple_of(dest[tile + j] * 8, 8), 8), : D + 128] for j in range(GROUPS)]
            rows = jnp.concatenate(rows, axis=0).astype(LOW)
            spot = lax.broadcasted_iota(jnp.int32, (SORTED, TILE), 0)
            pick = jnp.where(spot == meta_ref[r, 0:1, :], 1.0, 0.0).astype(LOW)
            back = tn(pick, rows)
            gs_ref[r] = back[:, :D]
            gg_ref[r] = nt(ones, back[:, D:].astype(LOW))[0:1, :]

    @pl.when((step >= undo) & (step < undo + STEPS_HALF))
    def _():
        collect(gs_theirs, gg_theirs)

    @pl.when(step >= undo + STEPS_HALF)
    def _():
        collect(gs_mine, gg_mine)


def tile_blocks(begin, undo):
    def index(i, c, *_):
        back = i >= undo
        j = jnp.where(back, i - undo, jnp.clip(i - begin, 0, DISPATCH - 1))
        flip = jnp.where(back, 1 - c[0], c[0])
        half = jnp.where(j < STEPS_HALF, flip, 1 - flip)
        return half * STEPS_HALF + j % STEPS_HALF

    return index


def run_from(begin):
    return lambda i, *_: (jnp.clip(i - begin, 0, STEPS_HALF - 1), 0, 0)


def experts(core, dest, chunks, own, other, g, meta, router_t, w_in, b_in, w_out):
    undo = DISPATCH + EXPERTS
    tile = tile_blocks(0, undo)
    expert = lambda i, *_: (jnp.clip(i - DISPATCH, 0, EXPERTS - 1), 0, 0)
    flat = lambda i, *_: (jnp.clip(i - DISPATCH, 0, EXPERTS - 1), 0)
    out_half = lambda begin: [
        pl.BlockSpec((RUN, TILE, D), run_from(begin)),
        pl.BlockSpec((RUN, 1, TILE), run_from(begin)),
    ]
    half = [
        jax.ShapeDtypeStruct((HALF_TILES, TILE, D), F32),
        jax.ShapeDtypeStruct((HALF_TILES, 1, TILE), F32),
    ]
    return pl.pallas_call(
        experts_kernel,
        grid_spec=pltpu.PrefetchScalarGridSpec(
            num_scalar_prefetch=3,
            grid=(undo + DISPATCH,),
            in_specs=[
                pl.BlockSpec((RUN, TILE, D), run_from(0)),
                pl.BlockSpec((RUN, TILE, D), run_from(STEPS_HALF)),
                pl.BlockSpec((RUN, TILE, D), lambda i, *s: (tile(jnp.minimum(i, undo - 1), *s), 0, 0)),
                pl.BlockSpec((RUN, 2, TILE), lambda i, *s: (tile(i, *s), 0, 0)),
                whole((16, D)),
                pl.BlockSpec((1, D, D), expert),
                whole((EXPERTS, D)),
                pl.BlockSpec((1, D, D), expert),
            ],
            out_specs=[
                pl.BlockSpec((D, D), flat),
                pl.BlockSpec((D, D), flat),
                whole((EXPERTS, D)),
                whole((EXPERTS, D)),
                pl.BlockSpec((SLOTS, D), flat),
            ]
            + out_half(undo)
            + out_half(undo + STEPS_HALF),
            scratch_shapes=[pltpu.VMEM((STORE, 2 * D), F32)],
        ),
        out_shape=[
            jax.ShapeDtypeStruct((EXPERTS * D, D), F32),
            jax.ShapeDtypeStruct((EXPERTS * D, D), F32),
            jax.ShapeDtypeStruct((EXPERTS, D), F32),
            jax.ShapeDtypeStruct((EXPERTS, D), F32),
            jax.ShapeDtypeStruct((EXPERTS * SLOTS, D), LOW),
        ]
        + half
        + half,
        compiler_params=pltpu.CompilerParams(vmem_limit_bytes=VMEM),
        cost_estimate=pl.CostEstimate(flops=1_000_000, bytes_accessed=100_000, transcendentals=0),
        name="experts",
    )(core, dest, chunks, own, other, g, meta, router_t, w_in, b_in, w_out)


def output_kernel(core, dest, chunks, act_ref, meta_ref, w_out, ep_theirs, ep_mine, store):
    step = pl.program_id(0)

    @pl.when(step == 0)
    def _():
        store[EXPERTS * SLOTS :, :] = jnp.zeros((8, D), F32)

    @pl.when(step < EXPERTS)
    def _():
        def chunk(c, carry):
            rows = act_ref[pl.ds(pl.multiple_of(c * CHUNK, 16), CHUNK), :]
            store[pl.ds(pl.multiple_of(step * SLOTS + c * CHUNK, 16), CHUNK), :] = nn(rows, w_out[0])
            return carry

        lax.fori_loop(0, chunks[step], chunk, 0)

    def collect(ep_ref):
        j = step - EXPERTS
        half = jnp.where(j < STEPS_HALF, 1 - core[0], core[0])
        begin = half * HALF_TILES + j % STEPS_HALF * RUN
        for r in range(RUN):
            tile = (begin + r) * GROUPS
            rows = [store[pl.ds(pl.multiple_of(dest[tile + j] * 8, 8), 8), :] for j in range(GROUPS)]
            rows = jnp.concatenate(rows, axis=0).astype(LOW)
            spot = lax.broadcasted_iota(jnp.int32, (SORTED, TILE), 0)
            pick = jnp.where(spot == meta_ref[r, 0:1, :], 1.0, 0.0).astype(LOW)
            ep_ref[r] = tn(pick, rows)

    @pl.when((step >= EXPERTS) & (step < EXPERTS + STEPS_HALF))
    def _():
        collect(ep_theirs)

    @pl.when(step >= EXPERTS + STEPS_HALF)
    def _():
        collect(ep_mine)


def experts_output(core, dest, chunks, act, meta, w_out):
    tile = tile_blocks(-DISPATCH, EXPERTS)
    half = jax.ShapeDtypeStruct((HALF_TILES, TILE, D), F32)
    return pl.pallas_call(
        output_kernel,
        grid_spec=pltpu.PrefetchScalarGridSpec(
            num_scalar_prefetch=3,
            grid=(EXPERTS + DISPATCH,),
            in_specs=[
                pl.BlockSpec((SLOTS, D), lambda i, *_: (jnp.minimum(i, EXPERTS - 1), 0)),
                pl.BlockSpec((RUN, 2, TILE), lambda i, *s: (tile(i, *s), 0, 0)),
                pl.BlockSpec((1, D, D), lambda i, *_: (jnp.minimum(i, EXPERTS - 1), 0, 0)),
            ],
            out_specs=[
                pl.BlockSpec((RUN, TILE, D), run_from(EXPERTS)),
                pl.BlockSpec((RUN, TILE, D), run_from(EXPERTS + STEPS_HALF)),
            ],
            scratch_shapes=[pltpu.VMEM((STORE, D), F32)],
        ),
        out_shape=[half, half],
        compiler_params=pltpu.CompilerParams(vmem_limit_bytes=VMEM),
        cost_estimate=pl.CostEstimate(flops=1_000_000, bytes_accessed=100_000, transcendentals=0),
        name="experts_output",
    )(core, dest, chunks, act, meta, w_out)


def sort_plan(ids):
    named = ids.reshape(TILES, TILE)
    kinds = jnp.arange(EXPERTS, dtype=jnp.int32)
    chosen = (named[:, :, None] == kinds).astype(F32)
    before = jnp.asarray(np.tril(np.ones((TILE, TILE), np.float32), -1))
    rank = jnp.einsum("ij,tje->tie", before, chosen)
    count = jnp.sum(chosen, axis=1).astype(jnp.int32)
    groups = (count + 7) // 8
    ahead = jnp.asarray(np.tril(np.ones((EXPERTS, EXPERTS), np.int32), -1))
    first = jnp.sum(groups[:, None, :] * ahead[None], axis=-1)
    spot = jnp.sum(chosen * (rank + 8.0 * first[:, None, :].astype(F32)), axis=-1).astype(jnp.int32)
    earlier = jnp.asarray(np.tril(np.ones((TILES, TILES), np.int32), -1))
    offset = jnp.sum(earlier[:, :, None] * groups[None], axis=1)
    j = jnp.arange(GROUPS, dtype=jnp.int32)[None, :, None]
    inside = (j >= first[:, None, :]) & (j < (first + groups)[:, None, :])
    target = kinds * (SLOTS // 8) + offset[:, None, :] + j - first[:, None, :]
    dest = jnp.sum(jnp.where(inside, target, 0), axis=-1)
    dest = jnp.where(jnp.any(inside, axis=-1), dest, EXPERTS * SLOTS // 8).astype(jnp.int32)
    used = jnp.sum(groups, axis=0) * 8
    chunks = (used + CHUNK - 1) // CHUNK
    return spot, dest.reshape(-1), chunks.astype(jnp.int32)


def backward_kernel(
    first, core, gs_a, gs_b, hidden_ref, g_ref, x_ref, ids_ref, mixed_ref, qkv_ref, prob_ref, window_ref,
    attn_gain, attn_shift, wqkv, place, place_t, heads, spread, wproj, moe_gain, moe_shift, router, out_bias_t,
    *refs,
):
    if first:
        input_grad, grad_wqkv, grad_wproj, small, table, raster_scr, mixed_scr = refs
        grad_wqkv[...] = jnp.zeros_like(grad_wqkv)
        grad_wproj[...] = jnp.zeros_like(grad_wproj)
        small[...] = jnp.zeros_like(small)
        table[...] = jnp.zeros_like(table)
    else:
        before, (input_grad, grad_wqkv, grad_wproj, small, table, raster_scr, mixed_scr) = refs[:4], refs[4:]
        for was, now in zip(before, (grad_wqkv, grad_wproj, small, table)):
            now[...] = was[...]

    g_low = g_ref[...]
    g = g_low.astype(F32)
    unit, inverse = norm_parts(hidden_ref[...])
    second = (unit * moe_gain[...] + moe_shift[...]).astype(LOW)
    probs, lanes = router_softmax(second, router[...])
    chosen = lanes == ids_ref[...]
    gate = jnp.sum(jnp.where(chosen, probs, 0.0), axis=-1, keepdims=True)
    with_bias = jnp.sum(jnp.where(chosen, nn(g_low, out_bias_t[...]), 0.0), axis=-1, keepdims=True)
    sums = gs_a[BLOCK:, :] + gs_b[BLOCK:, :]
    columns = []
    for piece in range(3):
        count = min(D, BLOCK - piece * D)
        same = lax.broadcasted_iota(jnp.int32, (count, D), 0) == lax.broadcasted_iota(jnp.int32, (count, D), 1)
        columns.append(jnp.sum(jnp.where(same, sums[piece : piece + 1, :], 0.0), axis=-1, keepdims=True))
    gated = jnp.concatenate(columns, axis=0)
    grad_logit = (gated + gate * with_bias) * (chosen.astype(F32) - probs)
    logit_high = grad_logit.astype(LOW)
    logit_rest = (grad_logit - logit_high.astype(F32)).astype(LOW)
    grad_router = tn(logit_high, second) + tn(logit_rest, second)
    grad_second = gs_a[:BLOCK, :] + gs_b[:BLOCK, :] + nt(logit_high, router[...]) + nt(logit_rest, router[...])
    small[3:4, :] += column_sum(grad_second * unit)
    small[4:5, :] += column_sum(grad_second)
    small[8:16, :] += grad_router[:EXPERTS, :]
    grad_hidden = g + norm_back(grad_second, unit, inverse, moe_gain[...])
    grad_low = grad_hidden.astype(LOW)
    small[2:3, :] += column_sum(grad_low.astype(F32))
    grad_wproj[...] += tn(mixed_ref[...], grad_low)
    mixed_scr[...] = nt(grad_low, wproj[...].astype(LOW)).astype(LOW)
    raster_scr[...] = jnp.zeros_like(raster_scr)

    def image(k, carry):
        start = pl.multiple_of(k * 192, 64)
        grad_mixed = nn(place[k], mixed_scr[pl.ds(start, SLICE), :])
        dots = (grad_mixed * window_ref[pl.ds(pl.multiple_of(k * PADDED, PADDED), PADDED), :].astype(F32)).astype(LOW)
        grad_mixed = grad_mixed.astype(LOW)
        weighted = [nn(dots[:, c * 128 : c * 128 + 128], spread[...]) for c in range(3)]
        outs = []
        for w in range(4):
            row = slice(w * 64, w * 64 + 64)
            at = pl.ds(pl.multiple_of(k * PADDED + w * 64, 64), 64)
            parts = [[], [], []]
            for c in range(3):
                q = qkv_ref[at, c * 128 : c * 128 + 128]
                kx = expand(qkv_ref[at, D + c * 128 : D + c * 128 + 128], heads[...])
                vx = expand(qkv_ref[at, 2 * D + c * 128 : 2 * D + c * 128 + 128], heads[...])
                prob_low = prob_ref[pl.ds(pl.multiple_of(((k * 4 + w) * 3 + c) * 64, 64), 64), :]
                prob = prob_low.astype(F32)
                upstream = grad_mixed[row, c * 128 : c * 128 + 128]
                grad_prob = nt(upstream, vx)
                grad_score = prob * (grad_prob - weighted[c][row])
                table[c * 64 : c * 64 + 64, :] += grad_score
                low = (grad_score * SCALE).astype(LOW)
                parts[0].append(nn(low, kx).astype(LOW))
                for slot, left, right in ((1, low, q), (2, prob_low, upstream)):
                    full = tn(left, right)
                    kept = [full[h * 64 : h * 64 + 64] * heads[h * 64 : h * 64 + 64, :].astype(F32) for h in range(4)]
                    parts[slot].append((kept[0] + kept[1] + kept[2] + kept[3]).astype(LOW))
            outs.append(jnp.concatenate(parts[0] + parts[1] + parts[2], axis=1))
        grads = jnp.concatenate(outs, axis=0)
        raster_scr[pl.ds(start, SLICE), :] += nn(place_t[k], grads)
        return carry

    lax.fori_loop(0, 4, image, 0)
    unit, inverse = norm_parts(x_ref[...].astype(F32))
    attn_low = (unit * attn_gain[...] + attn_shift[...]).astype(LOW)
    raster = raster_scr[...]
    small[5:6, :] += column_sum(raster[:, :D])
    small[6:7, :] += column_sum(raster[:, 2 * D :])
    grads = raster.astype(LOW)
    grad_wqkv[...] += tn(grads, attn_low)
    grad_in = nn(grads, wqkv[...].astype(LOW))
    small[0:1, :] += column_sum(grad_in * unit)
    small[1:2, :] += column_sum(grad_in)
    input_grad[...] = grad_hidden + norm_back(grad_in, unit, inverse, attn_gain[...])


def attention_backward(block, core, gs_a, gs_b, hidden, g, x, ids, mixed, qkv, prob, window, consts, weights, sums):
    place, place_t, heads, _, spread = consts
    at_block = lambda width: pl.BlockSpec((BLOCK, width), lambda i, s: (s[0] * BLOCKS + block, 0))
    rows = lambda height, width: pl.BlockSpec((height, width), lambda i, s: (block, 0))
    fixed = [weights[n] for n in ("attn_gain", "attn_shift", "wqkv")] + [place, place_t, heads, spread]
    fixed = fixed + [weights[n] for n in ("wproj", "moe_gain", "moe_shift", "router", "out_bias_t")]
    totals = [(3 * D, D), (D, D), (16, D), (192, 256)]
    before = [] if sums is None else list(sums)
    return pl.pallas_call(
        functools.partial(backward_kernel, sums is None),
        grid_spec=pltpu.PrefetchScalarGridSpec(
            num_scalar_prefetch=1,
            grid=(1,),
            in_specs=[
                whole((BLOCK + 8, D)),
                whole((BLOCK + 8, D)),
                rows(BLOCK, D),
                at_block(D),
                at_block(D),
                at_block(1),
                rows(BLOCK, D),
                rows(4 * PADDED, 3 * D),
                rows(48 * 64, 256),
                rows(4 * PADDED, D),
            ]
            + [whole(v.shape) for v in fixed + before],
            out_specs=[whole((BLOCK, D))] + [whole(v) for v in totals],
            scratch_shapes=[pltpu.VMEM((BLOCK, 3 * D), F32), pltpu.VMEM((BLOCK, D), LOW)],
        ),
        out_shape=[jax.ShapeDtypeStruct(v, F32) for v in [(BLOCK, D)] + totals],
        compiler_params=pltpu.CompilerParams(vmem_limit_bytes=VMEM),
        cost_estimate=pl.CostEstimate(flops=1_000_000, bytes_accessed=100_000, transcendentals=0),
        name="attention_backward",
    )(core, gs_a, gs_b, hidden, g, x, ids, mixed, qkv, prob, window, *fixed, *before)


def head_bias(table, lookup):
    rows = lax.dot_general(table.astype(LOW), lookup.astype(LOW), (((0,), (1,)), ((), ())), preferred_element_type=F32)
    return rows.reshape(96, 128)


def position_bias(heads, fill):
    rows = heads.reshape(3, 4, 64, 64).transpose(0, 2, 1, 3).reshape(1, 3, 64, 256)
    return (rows + fill[:, None]).reshape(12, 64, 256)


def table_gradient(sums, lookup):
    rows = sums.reshape(3, 64, 4, 64).transpose(1, 3, 0, 2).reshape(4096, HEADS)
    return lax.dot_general(lookup, rows, (((0,), (0,)), ((), ())), precision=lax.Precision.HIGHEST)


AXES = ("dp", "tensor")


def device_index(x, y, z, core):
    return (x % 2 * 16 + y % 4 * 4 + z % 4) * 4 + x // 2 % 2 * 2 + core


def pairs(move):
    places = [(x, y, z, c) for x in range(4) for y in range(4) for z in range(4) for c in range(2)]
    return [(device_index(*p), device_index(*move(*p))) for p in places]


CORE_SWAP = pairs(lambda x, y, z, c: (x, y, z, 1 - c))
FAR_SWAP = pairs(lambda x, y, z, c: ((x + 2) % 4, y, z, c))
NEAR_SWAP = pairs(lambda x, y, z, c: (x ^ 1, y, z, c))
TURN = {
    "y": [pairs(lambda x, y, z, c, s=s: (x, y + s, z, c)) for s in range(4)],
    "z": [pairs(lambda x, y, z, c, s=s: (x, y, z + s, c)) for s in range(4)],
}


def send(values, table):
    return lax.ppermute(values, AXES, table)


def after(values, *others):
    return lax.optimization_barrier((values,) + others)[0]


def scatter_near(parts):
    return [send(quarter(v, at + shift, dim), TURN[axis][shift]) for shift in (1, 3) for v, axis, at, dim in parts]


def quarter(values, index, dim):
    return lax.dynamic_index_in_dim(values, index % 4, dim, False)


def scatter_across(parts, near):
    return [
        send(after(quarter(v, at + 2, dim), near[n]), TURN[axis][2]) for n, (v, axis, at, dim) in enumerate(parts)
    ]


def scatter_total(parts, near, across):
    return [
        quarter(v, at, dim) + near[n] + near[n + len(parts)] + across[n]
        for n, (v, axis, at, dim) in enumerate(parts)
    ]


def scatter_sums(parts):
    near = [send(quarter(v, at + shift, dim), TURN[axis][shift]) for shift in (1, 3, 2) for v, axis, at, dim in parts]
    sums = scatter_total(parts, near, near[2 * len(parts) :])
    return [v.reshape((4, v.shape[0] // 4) + v.shape[1:]) for v in sums]


def gather_rows(parts):
    got = []
    for shift in (1, 3, 2):
        for n, (values, axis, place) in enumerate(parts):
            piece = after(values, got[n]) if shift == 2 and len(parts) > 1 else values
            got.append(send(piece, TURN[axis][shift]))
    fulls = []
    for n, (values, axis, place) in enumerate(parts):
        rows = values.shape[0]
        full = jnp.zeros((4 * rows,) + values.shape[1:], values.dtype)
        for shift, piece in ((0, values), (1, got[n]), (3, got[n + len(parts)]), (2, got[n + 2 * len(parts)])):
            full = lax.dynamic_update_slice_in_dim(full, piece, (place - shift) % 4 * rows, 0)
        fulls.append(full)
    return fulls


def assemble_kernel(core, mine, other, *refs):
    refs[-1][...] = jnp.where(pl.program_id(0) == 0, mine[...], other[...]).astype(refs[-1].dtype)


def assemble(core, b, mine, other, kind, before):
    def spot(i, c):
        return (jnp.where(i == 0, c[0], 1 - c[0]) * BLOCKS + b, 0)

    kept = [] if before is None else [before]
    return pl.pallas_call(
        assemble_kernel,
        grid_spec=pltpu.PrefetchScalarGridSpec(
            num_scalar_prefetch=1,
            grid=(2,),
            in_specs=[whole((BLOCK, D)), whole((BLOCK, D))] + [pl.BlockSpec(memory_space=pl.ANY)] * len(kept),
            out_specs=pl.BlockSpec((BLOCK, D), spot),
        ),
        out_shape=jax.ShapeDtypeStruct((2 * HALF, D), kind),
        input_output_aliases={3: 0} if kept else {},
        cost_estimate=pl.CostEstimate(flops=1_000_000, bytes_accessed=100_000, transcendentals=0),
        name="assemble",
    )(core, mine, other, *kept)


def gather_shards(far, core, own):
    near = send(own, CORE_SWAP)
    over = send(own, FAR_SWAP)
    last = send(over, CORE_SWAP)
    pick = lambda flag, a, b: jnp.where(flag == 1, a, b)
    low = (pick(core, near, own), pick(core, own, near))
    high = (pick(core, last, over), pick(core, over, last))
    return [pick(far, high[i], low[i]) for i in (0, 1)] + [pick(far, low[i], high[i]) for i in (0, 1)]


def gather_weights(far, core, qkv_weight, qv_bias, rel_table, proj_weight, lookup):
    own = jnp.concatenate(
        [
            qkv_weight.astype(F32).transpose(0, 2, 1).reshape(3 * 96, D),
            proj_weight.astype(F32),
        ]
    )
    shards = gather_shards(far, core, own)
    wqkv = jnp.stack([v[:288].reshape(3, 96, D) for v in shards], axis=1).reshape(3 * D, D)
    wproj = jnp.concatenate([v[288:384] for v in shards])
    few = jnp.pad(qv_bias.astype(F32), ((0, 6), (0, 32)))
    shards = gather_shards(far, core, jnp.concatenate([head_bias(after(rel_table, own), lookup), few]))
    heads = jnp.stack([v[:96].reshape(3, 64, 64) for v in shards]).reshape(HEADS, 64, 64)
    bias = jnp.concatenate([v[96:98, :96] for v in shards], axis=1)
    return wqkv, wproj, bias, heads


def pack_rest(shard, sums, in_bias, out_bias, lookup):
    grad_wqkv, grad_wproj, small, pair_sums = sums
    rows = jnp.pad(table_gradient(pair_sums, lookup).reshape(-1), (0, 8 * D - 169 * HEADS)).reshape(8, D)
    by_shard = jnp.concatenate([grad_wqkv.reshape(3, 4, 96, D), grad_wproj.reshape(1, 4, 96, D)])

    def pack(index):
        return jnp.concatenate([lax.dynamic_index_in_dim(by_shard, index, 1, False).reshape(D, D), small, rows])

    packed = pack(shard) + send(pack(shard ^ 1), CORE_SWAP)
    return jnp.concatenate([packed, in_bias, out_bias, jnp.zeros((88, D), F32)]).reshape(4, 128, D)


def shards(
    tokens_in, attn_gain, attn_shift, qkv_weight, qv_bias, rel_table, proj_weight, proj_bias, moe_gain, moe_shift,
    router_weight, expert_in, expert_in_bias, expert_out, expert_out_bias, expert_ids, cotangent,
):
    group, shard = lax.axis_index("dp"), lax.axis_index("tensor")
    at_x, at_y, at_z = group // 16, group // 4 % 4, group % 4
    far, side = shard // 2, shard % 2
    core = side.astype(jnp.int32).reshape(1)
    place, fill, lookup, heads, segment = layout_consts()
    consts = (place, place.transpose(0, 2, 1), heads, segment, heads.T)
    consts = tuple(jnp.asarray(v).astype(LOW) for v in consts)
    lookup = jnp.asarray(lookup)
    wide = lambda v: v.astype(F32).reshape(1, -1)

    wqkv, wproj, bias_qv, table = gather_weights(
        far, side, qkv_weight, qv_bias, rel_table, proj_weight, lookup
    )
    router = jnp.pad(router_weight, ((0, 0), (0, 128 - EXPERTS)))
    weights = dict(
        attn_gain=wide(attn_gain),
        attn_shift=wide(attn_shift),
        wqkv=wqkv,
        bqkv=jnp.concatenate([bias_qv[0:1], jnp.zeros((1, D), F32), bias_qv[1:2]], axis=1),
        wproj=wproj,
        bproj=wide(proj_bias),
        moe_gain=wide(moe_gain),
        moe_shift=wide(moe_shift),
        router=router,
        out_bias_pad=jnp.pad(expert_out_bias, ((0, 128 - EXPERTS), (0, 0))),
        out_bias_t=jnp.pad(expert_out_bias, ((0, 128 - EXPERTS), (0, 0))).T,
    )
    bias = position_bias(table, jnp.asarray(fill))
    spot, dest, chunks = sort_plan(expert_ids)
    meta = jnp.stack([spot, expert_ids.reshape(TILES, TILE)], axis=1)
    hidden, base, second, gate, mixed, qkv, prob, window = attention_forward(
        core, tokens_in, expert_ids, consts, weights, bias
    )
    second = second.reshape(HALF_TILES, TILE, D)
    grad_in, grad_out, in_bias, out_bias, act, gs_theirs, gg_theirs, gs_mine, gg_mine = experts(
        core, dest, chunks, second, send(second, CORE_SWAP), cotangent.reshape(TILES, TILE, D), meta,
        router[:, :16].T, expert_in, expert_in_bias.astype(F32), expert_out,
    )

    gs_theirs = send(gs_theirs, CORE_SWAP).reshape(HALF, D)
    gs_mine = gs_mine.reshape(HALF, D)
    gg = gg_mine.reshape(HALF) + send(gg_theirs.reshape(HALF), CORE_SWAP)
    gg = jnp.pad(gg.reshape(BLOCKS, BLOCK), ((0, 0), (0, 8 * D - BLOCK))).reshape(BLOCKS, 8, D)
    gs = [
        jnp.concatenate([gs_mine[b * BLOCK : (b + 1) * BLOCK] + gs_theirs[b * BLOCK : (b + 1) * BLOCK], gg[b]])
        for b in range(BLOCKS)
    ]
    gs_far = [send(gs[0], FAR_SWAP)]

    def attend(b, sums):
        return attention_backward(
            b, core, gs[b], gs_far[b], hidden, cotangent, tokens_in, expert_ids, mixed, qkv, prob, window,
            consts, weights, sums,
        )

    sixteen = [[i * 16 + j for j in range(16)] for i in range(2)]
    gather = lambda v: lax.all_gather(v, "dp", axis=0, axis_index_groups=sixteen, tiled=True)
    sum_out = lax.psum_scatter(grad_out, "dp", scatter_dimension=0, axis_index_groups=sixteen, tiled=True)
    cells = grad_in.reshape(4, 4, 2, 96, D)
    first = [(cells[:, :, 0], "y", at_y, 0), (cells[:, :, 1], "z", at_z, 1)]
    near = scatter_near(first)
    ep_theirs, ep_mine = experts_output(core, dest, chunks, after(act, gs[0]), meta, expert_out)
    ep_mine, near = lax.optimization_barrier((ep_mine, near))
    across = scatter_across(first, near)
    gs_far.append(send(gs[1], FAR_SWAP))
    ep_mine, ep_theirs, gs_far[0] = lax.optimization_barrier((ep_mine, ep_theirs, gs_far[0]))
    ep_theirs = send(ep_theirs, CORE_SWAP)
    gs_far.append(send(after(gs[2], gs_far[0]), FAR_SWAP))
    grad_0, *sums = attend(0, None)
    across, gs_far[1], grad_0, ep_theirs = lax.optimization_barrier((across, gs_far[1], grad_0, ep_theirs))
    halves = scatter_total(first, near, across)
    second = [(halves[0], "z", at_z, 0), (halves[1], "y", at_y, 0)]
    near = scatter_near(second)
    grad_1, *sums = attend(1, sums)
    ep = (ep_mine + ep_theirs).reshape(HALF, D)
    ep = [ep[b * BLOCK : (b + 1) * BLOCK] for b in range(BLOCKS)]
    near, sum_out, gs_far[2], grad_1, ep[0] = lax.optimization_barrier((near, sum_out, gs_far[2], grad_1, ep[0]))
    near_out = send(sum_out, NEAR_SWAP)
    across = scatter_across(second, near)
    ep_far = [send(after(ep[0], gs_far[2]), FAR_SWAP)]
    grad_2, *sums = attend(2, sums)
    near_out, across, grad_2, sums, ep_far[0] = lax.optimization_barrier((near_out, across, grad_2, sums, ep_far[0]))
    sum_out = gather(sum_out + near_out)
    sum_in = jnp.concatenate(scatter_total(second, near, across))
    sum_in = gather(sum_in + send(sum_in, NEAR_SWAP))
    ep_far.append(send(after(ep[1], ep_far[0]), FAR_SWAP))
    packed = pack_rest(shard, sums, in_bias, out_bias, lookup)
    (packed,) = scatter_sums([(packed, "y", at_y, 0)])
    (packed,) = scatter_sums([(packed, "z", at_z, 0)])
    packed, ep_far[1] = lax.optimization_barrier((packed.reshape(32, D), ep_far[1]))
    packed = packed + send(packed, NEAR_SWAP)
    ep_far.append(send(after(ep[2], ep_far[1]), FAR_SWAP))

    block_out, input_grad = None, None
    for b, grad in enumerate((grad_0, grad_1, grad_2)):
        block = slice(b * BLOCK, (b + 1) * BLOCK)
        block_half = base[block] + gate[block] * (ep[b] + ep_far[b])
        block_out = assemble(core, b, block_half, send(block_half, CORE_SWAP), LOW, block_out)
        input_grad = assemble(core, b, grad, send(grad, CORE_SWAP), F32, input_grad)

    (packed,) = gather_rows([(packed, "z", at_z)])
    (packed,) = gather_rows([(packed, "y", at_y)])
    few = packed[D : D + 24]
    grad_table = few[16:24].reshape(-1)[: 169 * HEADS].reshape(169, HEADS)
    return (
        block_out,
        input_grad,
        few[0],
        few[1],
        packed[:288].reshape(3, 96, D).transpose(0, 2, 1),
        lax.dynamic_slice_in_dim(few[5:7], shard * 96, 96, 1),
        lax.dynamic_slice_in_dim(grad_table, shard * 3, 3, 1),
        packed[288:384],
        few[2],
        few[3],
        few[4],
        few[8:16].T,
        sum_in.reshape(EXPERTS, D, D),
        packed[408:416],
        sum_out.reshape(EXPERTS, D, D),
        packed[416:424],
    )


def solution(mesh):
    placed = (
        P("dp", None),
        P(),
        P(),
        P(None, None, "tensor"),
        P(None, "tensor"),
        P(None, "tensor"),
        P("tensor", None),
        P(),
        P(),
        P(),
        P(),
        P(None, None, "tensor"),
        P(None, "tensor"),
        P(None, "tensor", None),
        P(),
        P("dp", None),
        P("dp", None),
    )
    return jax.shard_map(
        shards,
        mesh=mesh,
        in_specs=placed,
        out_specs=(
            P("dp", None),
            P("dp", None),
            P(),
            P(),
            P(None, None, "tensor"),
            P(None, "tensor"),
            P(None, "tensor"),
            P("tensor", None),
            P(),
            P(),
            P(),
            P(),
            P(None, None, "tensor"),
            P(None, "tensor"),
            P(None, "tensor", None),
            P(),
        ),
        check_vma=False,
    )
```

time: 640 us -> 458 us (0.72)
  the two profiles are of different devices: /device:TPU:0 before, /device:TPU:10 now
where the time goes in v2:
time: 458 us; the launch traced here: 450 us
  Pallas kernels  202 us (44%)
  waiting for transfers between devices  96.5 us (21%)
  starting transfers between devices  60 us (13%)
  local copies, waits for them, and re-layouts  35.9 us (8%)
  other arithmetic  33.5 us (7%)
  between operations  15.3 us (3%)
  matrix products  6.96 us (2%)
    ppermute x50, waiting for transfers between devices, send(): return lax.ppermute(values, AXES, table)  96.4 us
    pallas_call x3, Pallas kernels, attention_backward(): pl.pallas_call(functools.partial(backward_kernel, sums is None), grid_spe...  80.2 us
    ppermute x50, starting transfers between devices, send(): return lax.ppermute(values, AXES, table)  59.9 us
    pallas_call x1, Pallas kernels, experts(): pl.pallas_call(experts_kernel, grid_spec=pltpu.PrefetchScalarGridSpec(num...  55.3 us
    pallas_call x1, Pallas kernels, attention_forward(): pl.pallas_call(attention_kernel, grid_spec=pltpu.PrefetchScalarGridSpec(n...  32.5 us
    pallas_call x6, Pallas kernels, assemble(): pl.pallas_call(assemble_kernel, grid_spec=pltpu.PrefetchScalarGridSpec(nu...  17.9 us
    pallas_call x1, Pallas kernels, experts_output(): pl.pallas_call(output_kernel, grid_spec=pltpu.PrefetchScalarGridSpec(num_...  15.8 us
    unnamed x85, local copies, waits for them, and re-layouts  14.1 us
  transfers between devices with their start and end apart: 53, of which 21 were waited for; matrix products, arithmetic and copies ran while one was open for 13% of the time, Pallas kernels for 25%

profile of v2, /device:TPU:10, one launch (start us, length us, event | category | flops | bytes accessed | tf_op | source)
XLA Modules:
  0.0 449.9 jit_solution(2090004659379762674)
XLA Ops:
  7.9 1.8 maximum_convert_fusion
  9.8 2.3 fusion.33
  12.2 2.2 collective-permute-start.3
  14.4 3.5 collective-permute-done.3
  17.9 2.1 collective-permute-start
  24.8 2.2 copy.91.ids_ref
  27.5 7.8 %collective-permute-done = f32[384,384]{1,0:T(8,128)S(1)} collective-permute-done((f32[384,384]{1,0:T(8,128)}, f32[384,384]{1,0:T(8,128)S(1)}, u32[]{:S(2)}, u32[]{:S(2)}) %collective-permute-start) | collective-permute-done | bytes 589856 | tf_op jit(solution)/shard_map/ppermute | solution.py:676
  38.1 1.4 copy.87
  40.4 32.5 %attention_forward.1 = (f32[2352,384]{1,0:T(8,128)}, f32[2352,384]{1,0:T(8,128)}, f32[2352,384]{1,0:T(8,128)}, f32[2352,1]{1,0:T(8,128)}, bf16[2352,384]{1,0:T(8...) custom-call(s32[1]{0:T(128)} %bitcast.core, ...), custom_call_target="tpu_custom_call" | custom-call | flops 1000000 | bytes 100000 | tf_op jit(solution)/shard_map/attention_forward/pallas_call | solution.py:212
  80.0 55.3 %experts.1 = (f32[3072,384]{1,0:T(8,128)}, f32[3072,384]{1,0:T(8,128)}, f32[8,384]{1,0:T(8,128)}, f32[8,384]{1,0:T(8,128)}, bf16[7680,384]{1,0:T(8,128)(2,1)}, /...) custom-call(s32[1]{0:T(128)} %bitcast.core, ...), custom_call_target="tpu_custom_call" | custom-call | flops 1000000 | bytes 100000 | tf_op jit(solution)/shard_map/experts/pallas_call | solution.py:384
  137.0 4.7 %collective-permute-done.8 = f32[2352]{0:T(1024)S(1)} collective-permute-done((f32[2352]{0:T(1024)S(1)}, f32[2352]{0:T(1024)S(1)}, u32[]{:S(2)}, u32[]{:S(2)}) %collective-permute-start.8) | collective-permute-done | bytes 9440 | tf_op jit(solution)/shard_map/ppermute | solution.py:676
  142.0 5.1 %slice_add_fusion = (f32[784,384]{1,0:T(8,128)}, f32[784,384]{1,0:T(8,128)}, f32[784,384]{1,0:T(8,128)S(1)}) fusion(f32[2352,384]{1,0:T(8,128)} %bitcast.17, f32[2352,384]{1,0:T(8,128)} %bitcast.139), kind=kLoop, calls=%fused_computation.8 | loop fusion | flops 903168 | bytes 10838016 | tf_op jit(solution)/shard_map/add | solution.py:837
  148.2 2.1 collective-permute-start.13
  152.1 5.1 %collective-permute-start.12 = (f32[4,96,384]{2,1,0:T(8,128)}, f32[4,96,384]{2,1,0:T(8,128)S(1)}, u32[]{:S(2)}, u32[]{:S(2)}) collective-permute-start(f32[4,96,384]{2,1,0:T(8,128)} %get-tuple-element.245), channel_id=1, source_target_pairs={{0,12},{1,13},{4,0},{5,1},{8,4},{9,5},{12,8},{13,9},{16,28},{17,29... | collective-permute-start | bytes 1769480 | tf_op jit(solution)/shard_map/ppermute | solution.py:676
  158.9 1.6 collective-permute-start.9
  160.5 15.8 %experts_output.1 = (f32[14,168,384]{2,1,0:T(8,128)}, f32[14,168,384]{2,1,0:T(8,128)}) custom-call(s32[1]{0:T(128)} %bitcast.core, s32[784]{0:T(1024)} %select_n.329.dest, s32[8]{0:T(128)} %and_select_fusion.chunks, bf16[7680,384]{1,0:T(8,128)(2,1)} %get-tuple-element.101.act_ref, s32[28,2,168]{2,1,0:T(2,128)} %pad_add_fusion.meta_ref, ...), custom_call_target="tpu_custom_call" | custom-call | flops 1000000 | bytes 100000 | tf_op jit(solution)/shard_map/experts_output/pallas_call | solution.py:465
  176.2 2.4 collective-permute-done.12
  178.6 3.4 collective-permute-done.10
  182.0 1.5 collective-permute-done.9
  183.9 2.4 pad_maximum_fusion.2.gs_a
  187.4 2.7 collective-permute-start.15
  191.3 2.4 pad_maximum_fusion.3.gs_a
  193.7 2.4 collective-permute-start.22
  196.8 26.3 %attention_backward.3 = (f32[784,384]{1,0:T(8,128)}, f32[1152,384]{1,0:T(8,128)}, f32[384,384]{1,0:T(8,128)}, f32[16,384]{1,0:T(8,128)}, f32[192,256]{1,0:T(8,128)}) custom-call(s32[1]{0:T(128)} %bitcast.core, f32[792,384]{1,0:T(8,128)} %pad_maximum_fusion.1.gs_a, f32[792,384]{1,0:T(8,128)} %collective-permute-done.13.gs_b, ...), custom_call_target="tpu_custom_call" | custom-call | flops 1000000 | bytes 100000 | tf_op jit(solution)/shard_map/attention_backward/pallas_call | solution.py:611
  223.9 2.6 fusion.7
  227.2 1.4 collective-permute-start.21
  232.4 2.6 add.434
  235.1 1.9 fusion.30
  237.7 27.0 %attention_backward.4 = (f32[784,384]{1,0:T(8,128)}, f32[1152,384]{1,0:T(8,128)}, f32[384,384]{1,0:T(8,128)}, f32[16,384]{1,0:T(8,128)}, f32[192,256]{1,0:T(8,128)}) custom-call(s32[1]{0:T(128)} %bitcast.core, f32[792,384]{1,0:T(8,128)} %pad_maximum_fusion.2.gs_a, f32[792,384]{1,0:T(8,128)} %collective-permute-done.16.gs_b, ...), custom_call_target="tpu_custom_call" | custom-call | flops 1000000 | bytes 100000 | tf_op jit(solution)/shard_map/attention_backward/pallas_call | solution.py:611
  264.7 1.5 collective-permute-start.26
  266.9 2.5 collective-permute-start.25
  269.5 1.7 collective-permute-start.24
  271.1 27.0 %attention_backward.5 = (f32[784,384]{1,0:T(8,128)}, f32[1152,384]{1,0:T(8,128)}, f32[384,384]{1,0:T(8,128)}, f32[16,384]{1,0:T(8,128)}, f32[192,256]{1,0:T(8,128)}) custom-call(s32[1]{0:T(128)} %bitcast.core, f32[792,384]{1,0:T(8,128)} %pad_maximum_fusion.3.gs_a, f32[792,384]{1,0:T(8,128)} %collective-permute-done.22.gs_b, ...), custom_call_target="tpu_custom_call" | custom-call | flops 1000000 | bytes 100000 | tf_op jit(solution)/shard_map/attention_backward/pallas_call | solution.py:611
  300.7 2.0 collective-permute-start.49
  302.7 4.8 %collective-permute-done.49 = f32[192,384]{1,0:T(8,128)S(1)} collective-permute-done((f32[192,384]{1,0:T(8,128)S(1)}, f32[192,384]{1,0:T(8,128)S(1)}, u32[]{:S(2)}, u32[]{:S(2)}) %collective-permute-start.49) | collective-permute-done | bytes 294944 | tf_op jit(solution)/shard_map/ppermute | solution.py:676
  308.7 4.4 fusion.34
  315.6 2.6 collective-permute-start.34
  318.8 3.0 collective-permute-start.30
  322.4 4.5 collective-permute-done.28
  328.1 3.0 collective-permute-done.29
  331.2 1.4 collective-permute-start.31
  332.6 2.7 collective-permute-start.33
  335.7 1.4 collective-permute-done.31
  338.2 2.2 collective-permute-done.32
  340.5 4.8 %collective-permute-done.34 = f32[784,384]{1,0:T(8,128)S(1)} collective-permute-done((f32[784,384]{1,0:T(8,128)S(1)}, f32[784,384]{1,0:T(8,128)S(1)}, u32[]{:S(2)}, u32[]{:S(2)}) %collective-permute-start.34) | collective-permute-done | bytes 1204256 | tf_op jit(solution)/shard_map/ppermute | solution.py:676
  345.3 2.6 collective-permute-start.35
  347.9 2.1 collective-permute-start.42
  350.6 25.9 %collective-permute-done.42 = f32[32,384]{1,0:T(8,128)S(1)} collective-permute-done((f32[32,384]{1,0:T(8,128)S(1)}, f32[32,384]{1,0:T(8,128)S(1)}, u32[]{:S(2)}, u32[]{:S(2)}) %collective-permute-start.42) | collective-permute-done | bytes 49184 | tf_op jit(solution)/shard_map/ppermute | solution.py:676
  377.5 1.7 slice_reduce_fusion
  379.2 3.0 collective-permute-done.43
  382.2 1.6 collective-permute-start.44
  383.8 2.5 collective-permute-done.44
  387.4 4.9 %multiply_add_fusion.1 = (f32[784,384]{1,0:T(8,128)}, f32[784,384]{1,0:T(8,128)S(1)}, f32[784,384]{1,0:T(8,128)}) fusion(f32[784,384]{1,0:T(8,128)S(1)} %copy-done.11, f32[2352,384]{1,0:T(8,128)} %get-tuple-element.93, f32[784]{0:T(1024)S(1)} %get-tuple-element.217, f32[2352,384]{1,0:T(8,128)} %bitcast.133, f32[784,384]{1,0:T(8,128)} %collective-permute-done.35, ...), kind=kLoop, calls=%fused_computation.12 | loop fusion | flops 2709504 | bytes 14460096 | tf_op jit(solution)/shard_map/add | solution.py:889
  393.1 3.2 assemble.9.refs_0_
  396.3 3.2 assemble.10.refs_0_
  399.5 3.3 assemble.11
  402.7 2.0 collective-permute-start.47
  405.7 8.2 %collective-permute-done.47 = f32[128,384]{1,0:T(8,128)S(1)} collective-permute-done((f32[128,384]{1,0:T(8,128)S(1)}, f32[128,384]{1,0:T(8,128)S(1)}, u32[]{:S(2)}, u32[]{:S(2)}) %collective-permute-start.47) | collective-permute-done | bytes 196640 | tf_op jit(solution)/shard_map/ppermute | solution.py:676
  413.9 9.2 %collective-permute-done.48 = f32[128,384]{1,0:T(8,128)S(1)} collective-permute-done((f32[128,384]{1,0:T(8,128)S(1)}, f32[128,384]{1,0:T(8,128)S(1)}, u32[]{:S(2)}, u32[]{:S(2)}) %collective-permute-start.48) | collective-permute-done | bytes 196640 | tf_op jit(solution)/shard_map/ppermute | solution.py:676
  427.4 2.8 assemble.6.refs_0_
  430.2 2.8 assemble.7.refs_0_
  432.9 2.8 assemble.8
  435.7 5.0 %copy.123 = f32[8,384,384]{2,1,0:T(8,128)} copy(f32[8,384,384]{2,1,0:T(8,128)} %bitcast.135) | data formatting | bytes 9437184
  440.7 2.2 copy.124
  (281 shorter events, 51.9 us)
Async XLA Ops:
  7.2 257.5 %reduce-scatter.2.cloned.1.call-start = ((), (), s32[]{:S(2)}) async-start(), calls=%async_computation.1 | async-start | bytes 5013504 | tf_op jit(solution)/shard_map/reduce_scatter | solution.py:850
  9.8 12.8 %copy-start.35 = (bf16[384]{0:T(512)(128)(2,1)S(1)}, bf16[384]{0:T(512)(128)(2,1)}, u32[]{:S(2)}) copy-start(bf16[384]{0:T(512)(128)(2,1)} %param.34) | copy-start | bytes 2308
  9.8 13.3 %copy-start.27 = (bf16[384,8]{0,1:T(8,128)(2,1)S(1)}, bf16[384,8]{0,1:T(8,128)(2,1)}, u32[]{:S(2)}) copy-start(bf16[384,8]{0,1:T(8,128)(2,1)} %param.37) | copy-start | bytes 18436
  9.8 13.5 %copy-start.28 = (bf16[8,384]{1,0:T(8,128)(2,1)S(1)}, bf16[8,384]{1,0:T(8,128)(2,1)}, u32[]{:S(2)}) copy-start(bf16[8,384]{1,0:T(8,128)(2,1)} %param.41) | copy-start | bytes 18436
  9.8 15.0 %copy-start.21 = (s32[4704,1]{0,1:T(1,128)S(1)}, s32[4704,1]{0,1:T(1,128)}, u32[]{:S(2)}) copy-start(s32[4704,1]{0,1:T(1,128)} %param.42) | copy-start | bytes 56452
  12.2 5.7 %collective-permute-start.3 = (f32[104,128]{1,0:T(8,128)S(1)}, f32[104,128]{1,0:T(8,128)S(1)}, u32[]{:S(2)}, u32[]{:S(2)}) collective-permute-start(f32[104,128]{1,0:T(8,128)S(1)} %pad_maximum_fusion.11), channel_id=1, source_target_pairs={{0,2},{1,3},{4,6},{5,7},{8,10},{9,11},{12,14},{13,15},{16,18},{17,... | collective-permute-start | bytes 159752 | tf_op jit(solution)/shard_map/ppermute | solution.py:676
  14.4 12.6 %collective-permute-start.5 = (f32[104,128]{1,0:T(8,128)S(1)}, f32[104,128]{1,0:T(8,128)S(1)}, u32[]{:S(2)}, u32[]{:S(2)}) collective-permute-start(f32[104,128]{1,0:T(8,128)S(1)} %pad_maximum_fusion.11), channel_id=1, source_target_pairs={{0,1},{1,0},{4,5},{5,4},{8,9},{9,8},{12,13},{13,12},{16,17},{17,16... | collective-permute-start | bytes 159752 | tf_op jit(solution)/shard_map/ppermute | solution.py:676
  17.9 9.1 %collective-permute-start.4 = (f32[104,128]{1,0:T(8,128)S(1)}, f32[104,128]{1,0:T(8,128)S(1)}, u32[]{:S(2)}, u32[]{:S(2)}) collective-permute-start(f32[104,128]{1,0:T(8,128)S(1)} %collective-permute-done.3), channel_id=1, source_target_pairs={{0,1},{1,0},{4,5},{5,4},{8,9},{9,8},{12,13},{13,12},{16,17},{17,16... | collective-permute-start | bytes 159752 | tf_op jit(solution)/shard_map/ppermute | solution.py:676
  17.9 17.5 %collective-permute-start = (f32[384,384]{1,0:T(8,128)}, f32[384,384]{1,0:T(8,128)S(1)}, u32[]{:S(2)}, u32[]{:S(2)}) collective-permute-start(f32[384,384]{1,0:T(8,128)} %maximum_convert_fusion), channel_id=1, source_target_pairs={{0,2},{1,3},{4,6},{5,7},{8,10},{9,11},{12,14},{13,15},{16,18},{17,... | collective-permute-start | bytes 1769480 | tf_op jit(solution)/shard_map/ppermute | solution.py:676
  20.0 17.5 %collective-permute-start.2 = (f32[384,384]{1,0:T(8,128)}, f32[384,384]{1,0:T(8,128)S(1)}, u32[]{:S(2)}, u32[]{:S(2)}) collective-permute-start(f32[384,384]{1,0:T(8,128)} %maximum_convert_fusion), channel_id=1, source_target_pairs={{0,1},{1,0},{4,5},{5,4},{8,9},{9,8},{12,13},{13,12},{16,17},{17,16... | collective-permute-start | bytes 1769480 | tf_op jit(solution)/shard_map/ppermute | solution.py:676
  35.3 2.2 collective-permute-start.1
  40.4 33.6 %copy-start.29 = (bf16[8,384]{1,0:T(8,128)(2,1)S(1)}, bf16[8,384]{1,0:T(8,128)(2,1)}, u32[]{:S(2)}) copy-start(bf16[8,384]{1,0:T(8,128)(2,1)} %param.39) | copy-start | bytes 18436
  40.4 34.4 %copy-start.30 = (s32[8,8]{1,0:T(8,128)S(1)}, s32[8,8]{1,0:T(8,128)}, u32[]{:S(2)}) copy-start(s32[8,8]{1,0:T(8,128)} %constant.315.clone) | copy-start | bytes 772
  40.4 34.7 %copy-start.36 = (bf16[168,168,1]{1,0,2:T(8,128)(2,1)S(1)}, bf16[168,168,1]{1,0,2:T(8,128)(2,1)}, u32[]{:S(2)}) copy-start(bf16[168,168,1]{1,0,2:T(8,128)(2,1)} %constant.475) | copy-start | bytes 169348
  40.4 35.0 %copy-start.22 = (s32[28,28]{1,0:T(8,128)S(1)}, s32[28,28]{1,0:T(8,128)}, u32[]{:S(2)}) copy-start(s32[28,28]{1,0:T(8,128)} %constant.316.clone) | copy-start | bytes 9412
  72.9 7.1 %collective-permute-start.6 = (f32[14,168,384]{2,1,0:T(8,128)}, f32[14,168,384]{2,1,0:T(8,128)}, u32[]{:S(2)}, u32[]{:S(2)}) collective-permute-start(f32[14,168,384]{2,1,0:T(8,128)} %bitcast.140), channel_id=1, source_target_pairs={{0,1},{1,0},{4,5},{5,4},{8,9},{9,8},{12,13},{13,12},{16,17},{17,16... | collective-permute-start | bytes 10838024 | tf_op jit(solution)/shard_map/ppermute | solution.py:676
  135.3 6.8 %collective-permute-start.7 = (f32[14,168,384]{2,1,0:T(8,128)}, f32[14,168,384]{2,1,0:T(8,128)}, u32[]{:S(2)}, u32[]{:S(2)}) collective-permute-start(f32[14,168,384]{2,1,0:T(8,128)} %get-tuple-element.98), channel_id=1, source_target_pairs={{0,1},{1,0},{4,5},{5,4},{8,9},{9,8},{12,13},{13,12},{16,17},{17,16... | collective-permute-start | bytes 10838024 | tf_op jit(solution)/shard_map/ppermute | solution.py:676
  135.8 300.0 %all-gather.5.cloned.1.call-start = ((), (), s32[]{:S(2)}) async-start(), calls=%async_computation.3 | async-start | bytes 5013504 | tf_op jit(solution)/shard_map/all_gather | solution.py:849
  136.6 5.1 %collective-permute-start.8 = (f32[2352]{0:T(1024)S(1)}, f32[2352]{0:T(1024)S(1)}, u32[]{:S(2)}, u32[]{:S(2)}) collective-permute-start(f32[2352]{0:T(1024)S(1)} %reshape.279), channel_id=1, source_target_pairs={{0,1},{1,0},{4,5},{5,4},{8,9},{9,8},{12,13},{13,12},{16,17},{17,16... | collective-permute-start | bytes 28232 | tf_op jit(solution)/shard_map/ppermute | solution.py:676
  148.2 35.3 %collective-permute-start.13 = (f32[792,384]{1,0:T(8,128)}, f32[792,384]{1,0:T(8,128)}, u32[]{:S(2)}, u32[]{:S(2)}) collective-permute-start(f32[792,384]{1,0:T(8,128)} %pad_maximum_fusion.1.gs_a), channel_id=1, source_target_pairs={{0,2},{1,3},{4,6},{5,7},{8,10},{9,11},{12,14},{13,15},{16,18},{17,... | collective-permute-start | bytes 3649544 | tf_op jit(solution)/shard_map/ppermute | solution.py:676
  152.1 26.5 %collective-permute-start.12 = (f32[4,96,384]{2,1,0:T(8,128)}, f32[4,96,384]{2,1,0:T(8,128)S(1)}, u32[]{:S(2)}, u32[]{:S(2)}) collective-permute-start(f32[4,96,384]{2,1,0:T(8,128)} %get-tuple-element.245), channel_id=1, source_target_pairs={{0,12},{1,13},{4,0},{5,1},{8,4},{9,5},{12,8},{13,9},{16,28},{17,29... | collective-permute-start | bytes 1769480 | tf_op jit(solution)/shard_map/ppermute | solution.py:676
  157.2 24.8 %collective-permute-start.10 = (f32[4,96,384]{2,1,0:T(8,128)}, f32[4,96,384]{2,1,0:T(8,128)}, u32[]{:S(2)}, u32[]{:S(2)}) collective-permute-start(f32[4,96,384]{2,1,0:T(8,128)} %get-tuple-element.246), channel_id=1, source_target_pairs={{0,4},{1,5},{4,8},{5,9},{8,12},{9,13},{12,0},{13,1},{16,20},{17,21... | collective-permute-start | bytes 1769480 | tf_op jit(solution)/shard_map/ppermute | solution.py:676
  158.5 23.6 %collective-permute-start.11 = (f32[4,96,384]{2,1,0:T(8,128)}, f32[4,96,384]{2,1,0:T(8,128)}, u32[]{:S(2)}, u32[]{:S(2)}) collective-permute-start(f32[4,96,384]{2,1,0:T(8,128)} %get-tuple-element.248), channel_id=1, source_target_pairs={{0,48},{1,49},{4,52},{5,53},{8,56},{9,57},{12,60},{13,61},{16,0},{... | collective-permute-start | bytes 1769480 | tf_op jit(solution)/shard_map/ppermute | solution.py:676
  158.9 24.6 %collective-permute-start.9 = (f32[4,96,384]{2,1,0:T(8,128)}, f32[4,96,384]{2,1,0:T(8,128)}, u32[]{:S(2)}, u32[]{:S(2)}) collective-permute-start(f32[4,96,384]{2,1,0:T(8,128)} %get-tuple-element.249), channel_id=1, source_target_pairs={{0,16},{1,17},{4,20},{5,21},{8,24},{9,25},{12,28},{13,29},{16,32},... | collective-permute-start | bytes 1769480 | tf_op jit(solution)/shard_map/ppermute | solution.py:676
  183.5 39.6 %collective-permute-start.17 = (f32[14,168,384]{2,1,0:T(8,128)}, f32[14,168,384]{2,1,0:T(8,128)}, u32[]{:S(2)}, u32[]{:S(2)}) collective-permute-start(f32[14,168,384]{2,1,0:T(8,128)} %get-tuple-element.118), channel_id=1, source_target_pairs={{0,1},{1,0},{4,5},{5,4},{8,9},{9,8},{12,13},{13,12},{16,17},{17,16... | collective-permute-start | bytes 10838024 | tf_op jit(solution)/shard_map/ppermute | solution.py:676
  186.3 36.7 %collective-permute-start.16 = (f32[792,384]{1,0:T(8,128)}, f32[792,384]{1,0:T(8,128)}, u32[]{:S(2)}, u32[]{:S(2)}) collective-permute-start(f32[792,384]{1,0:T(8,128)} %pad_maximum_fusion.2.gs_a), channel_id=1, source_target_pairs={{0,2},{1,3},{4,6},{5,7},{8,10},{9,11},{12,14},{13,15},{16,18},{17,... | collective-permute-start | bytes 3649544 | tf_op jit(solution)/shard_map/ppermute | solution.py:676
  187.4 35.7 %collective-permute-start.15 = (f32[4,96,384]{2,1,0:T(8,128)}, f32[4,96,384]{2,1,0:T(8,128)S(1)}, u32[]{:S(2)}, u32[]{:S(2)}) collective-permute-start(f32[4,96,384]{2,1,0:T(8,128)} %get-tuple-element.110), channel_id=1, source_target_pairs={{0,8},{1,9},{4,12},{5,13},{8,0},{9,1},{12,4},{13,5},{16,24},{17,25... | collective-permute-start | bytes 1769480 | tf_op jit(solution)/shard_map/ppermute | solution.py:676
  190.0 33.0 %collective-permute-start.14 = (f32[4,96,384]{2,1,0:T(8,128)}, f32[4,96,384]{2,1,0:T(8,128)}, u32[]{:S(2)}, u32[]{:S(2)}) collective-permute-start(f32[4,96,384]{2,1,0:T(8,128)} %get-tuple-element.108), channel_id=1, source_target_pairs={{0,32},{1,33},{4,36},{5,37},{8,40},{9,41},{12,44},{13,45},{16,48},... | collective-permute-start | bytes 1769480 | tf_op jit(solution)/shard_map/ppermute | solution.py:676
  193.7 70.9 %collective-permute-start.22 = (f32[792,384]{1,0:T(8,128)}, f32[792,384]{1,0:T(8,128)}, u32[]{:S(2)}, u32[]{:S(2)}) collective-permute-start(f32[792,384]{1,0:T(8,128)} %pad_maximum_fusion.3.gs_a), channel_id=1, source_target_pairs={{0,2},{1,3},{4,6},{5,7},{8,10},{9,11},{12,14},{13,15},{16,18},{17,... | collective-permute-start | bytes 3649544 | tf_op jit(solution)/shard_map/ppermute | solution.py:676
  227.2 37.5 %collective-permute-start.21 = (f32[96,384]{1,0:T(8,128)S(1)}, f32[96,384]{1,0:T(8,128)S(1)}, u32[]{:S(2)}, u32[]{:S(2)}) collective-permute-start(f32[96,384]{1,0:T(8,128)S(1)} %get-tuple-element.262), channel_id=1, source_target_pairs={{0,48},{1,49},{4,52},{5,53},{8,56},{9,57},{12,60},{13,61},{16,0},{... | collective-permute-start | bytes 442376 | tf_op jit(solution)/shard_map/ppermute | solution.py:676
  228.6 36.1 %collective-permute-start.19 = (f32[96,384]{1,0:T(8,128)S(1)}, f32[96,384]{1,0:T(8,128)S(1)}, u32[]{:S(2)}, u32[]{:S(2)}) collective-permute-start(f32[96,384]{1,0:T(8,128)S(1)} %get-tuple-element.263), channel_id=1, source_target_pairs={{0,16},{1,17},{4,20},{5,21},{8,24},{9,25},{12,28},{13,29},{16,32},... | collective-permute-start | bytes 442376 | tf_op jit(solution)/shard_map/ppermute | solution.py:676
  230.3 34.4 %collective-permute-start.20 = (f32[96,384]{1,0:T(8,128)S(1)}, f32[96,384]{1,0:T(8,128)S(1)}, u32[]{:S(2)}, u32[]{:S(2)}) collective-permute-start(f32[96,384]{1,0:T(8,128)S(1)} %get-tuple-element.265), channel_id=1, source_target_pairs={{0,12},{1,13},{4,0},{5,1},{8,4},{9,5},{12,8},{13,9},{16,28},{17,29... | collective-permute-start | bytes 442376 | tf_op jit(solution)/shard_map/ppermute | solution.py:676
  231.4 33.3 %collective-permute-start.18 = (f32[96,384]{1,0:T(8,128)S(1)}, f32[96,384]{1,0:T(8,128)S(1)}, u32[]{:S(2)}, u32[]{:S(2)}) collective-permute-start(f32[96,384]{1,0:T(8,128)S(1)} %get-tuple-element.266), channel_id=1, source_target_pairs={{0,4},{1,5},{4,8},{5,9},{8,12},{9,13},{12,0},{13,1},{16,20},{17,21... | collective-permute-start | bytes 442376 | tf_op jit(solution)/shard_map/ppermute | solution.py:676
  264.7 33.5 %collective-permute-start.26 = (f32[784,384]{1,0:T(8,128)S(1)}, f32[784,384]{1,0:T(8,128)}, u32[]{:S(2)}, u32[]{:S(2)}) collective-permute-start(f32[784,384]{1,0:T(8,128)S(1)} %get-tuple-element.148), channel_id=1, source_target_pairs={{0,2},{1,3},{4,6},{5,7},{8,10},{9,11},{12,14},{13,15},{16,18},{17,... | collective-permute-start | bytes 3612680 | tf_op jit(solution)/shard_map/ppermute | solution.py:676
  266.2 32.0 %collective-permute-start.23 = (f32[192,384]{1,0:T(8,128)}, f32[192,384]{1,0:T(8,128)S(1)}, u32[]{:S(2)}, u32[]{:S(2)}) collective-permute-start(f32[192,384]{1,0:T(8,128)} %reduce-scatter.2.cloned.1.call-done), channel_id=1, source_target_pairs={{0,64},{1,65},{4,68},{5,69},{8,72},{9,73},{12,76},{13,77},{16,80},... | collective-permute-start | bytes 884744 | tf_op jit(solution)/shard_map/ppermute | solution.py:676
  266.9 31.2 %collective-permute-start.25 = (f32[96,384]{1,0:T(8,128)}, f32[96,384]{1,0:T(8,128)S(1)}, u32[]{:S(2)}, u32[]{:S(2)}) collective-permute-start(f32[96,384]{1,0:T(8,128)} %get-tuple-element.136), channel_id=1, source_target_pairs={{0,32},{1,33},{4,36},{5,37},{8,40},{9,41},{12,44},{13,45},{16,48},... | collective-permute-start | bytes 442376 | tf_op jit(solution)/shard_map/ppermute | solution.py:676
  269.5 28.7 %collective-permute-start.24 = (f32[96,384]{1,0:T(8,128)}, f32[96,384]{1,0:T(8,128)S(1)}, u32[]{:S(2)}, u32[]{:S(2)}) collective-permute-start(f32[96,384]{1,0:T(8,128)} %get-tuple-element.134), channel_id=1, source_target_pairs={{0,8},{1,9},{4,12},{5,13},{8,0},{9,1},{12,4},{13,5},{16,24},{17,25... | collective-permute-start | bytes 442376 | tf_op jit(solution)/shard_map/ppermute | solution.py:676
  271.1 27.7 %copy-start.15 = (f32[192,384]{1,0:T(8,128)S(1)}, f32[192,384]{1,0:T(8,128)}, u32[]{:S(2)}) copy-start(f32[192,384]{1,0:T(8,128)} %reduce-scatter.2.cloned.1.call-done) | copy-start | bytes 884740
  299.6 136.1 %all-gather.3.cloned.1.call-start = ((), (), s32[]{:S(2)}) async-start(), calls=%async_computation.2 | async-start | bytes 5013504 | tf_op jit(solution)/shard_map/all_gather | solution.py:849
  300.7 6.8 %collective-permute-start.49 = (f32[192,384]{1,0:T(8,128)S(1)}, f32[192,384]{1,0:T(8,128)S(1)}, u32[]{:S(2)}, u32[]{:S(2)}) collective-permute-start(f32[192,384]{1,0:T(8,128)S(1)} %pad_maximum_fusion.10), channel_id=1, source_target_pairs={{0,64},{1,65},{4,68},{5,69},{8,72},{9,73},{12,76},{13,77},{16,80},... | collective-permute-start | bytes 884744 | tf_op jit(solution)/shard_map/ppermute | solution.py:676
  314.5 3.8 collective-permute-start.27
  315.6 29.7 %collective-permute-start.34 = (f32[784,384]{1,0:T(8,128)S(1)}, f32[784,384]{1,0:T(8,128)S(1)}, u32[]{:S(2)}, u32[]{:S(2)}) collective-permute-start(f32[784,384]{1,0:T(8,128)S(1)} %copy-done.9), channel_id=1, source_target_pairs={{0,2},{1,3},{4,6},{5,7},{8,10},{9,11},{12,14},{13,15},{16,18},{17,... | collective-permute-start | bytes 3612680 | tf_op jit(solution)/shard_map/ppermute | solution.py:676
  318.5 26.8 %copy-start.8 = (f32[784,384]{1,0:T(8,128)S(1)}, f32[784,384]{1,0:T(8,128)}, u32[]{:S(2)}) copy-start(f32[784,384]{1,0:T(8,128)} %get-tuple-element.158) | copy-start | bytes 3612676
  318.5 8.4 %collective-permute-start.28 = (f32[128,384]{1,0:T(8,128)S(1)}, f32[128,384]{1,0:T(8,128)S(1)}, u32[]{:S(2)}, u32[]{:S(2)}) collective-permute-start(f32[128,384]{1,0:T(8,128)S(1)} %get-tuple-element.258), channel_id=1, source_target_pairs={{0,16},{1,17},{4,20},{5,21},{8,24},{9,25},{12,28},{13,29},{16,32},... | collective-permute-start | bytes 589832 | tf_op jit(solution)/shard_map/ppermute | solution.py:676
  318.8 9.3 %collective-permute-start.30 = (f32[128,384]{1,0:T(8,128)S(1)}, f32[128,384]{1,0:T(8,128)S(1)}, u32[]{:S(2)}, u32[]{:S(2)}) collective-permute-start(f32[128,384]{1,0:T(8,128)S(1)} %get-tuple-element.259), channel_id=1, source_target_pairs={{0,32},{1,33},{4,36},{5,37},{8,40},{9,41},{12,44},{13,45},{16,48},... | collective-permute-start | bytes 589832 | tf_op jit(solution)/shard_map/ppermute | solution.py:676
  321.8 9.4 %collective-permute-start.29 = (f32[128,384]{1,0:T(8,128)S(1)}, f32[128,384]{1,0:T(8,128)S(1)}, u32[]{:S(2)}, u32[]{:S(2)}) collective-permute-start(f32[128,384]{1,0:T(8,128)S(1)} %get-tuple-element.260), channel_id=1, source_target_pairs={{0,48},{1,49},{4,52},{5,53},{8,56},{9,57},{12,60},{13,61},{16,0},{... | collective-permute-start | bytes 589832 | tf_op jit(solution)/shard_map/ppermute | solution.py:676
  331.2 5.9 %collective-permute-start.31 = (f32[32,384]{1,0:T(8,128)S(1)}, f32[32,384]{1,0:T(8,128)S(1)}, u32[]{:S(2)}, u32[]{:S(2)}) collective-permute-start(f32[32,384]{1,0:T(8,128)S(1)} %get-tuple-element.271), channel_id=1, source_target_pairs={{0,4},{1,5},{4,8},{5,9},{8,12},{9,13},{12,0},{13,1},{16,20},{17,21... | collective-permute-start | bytes 147464 | tf_op jit(solution)/shard_map/ppermute | solution.py:676
  332.6 5.6 %collective-permute-start.33 = (f32[32,384]{1,0:T(8,128)S(1)}, f32[32,384]{1,0:T(8,128)S(1)}, u32[]{:S(2)}, u32[]{:S(2)}) collective-permute-start(f32[32,384]{1,0:T(8,128)S(1)} %get-tuple-element.272), channel_id=1, source_target_pairs={{0,8},{1,9},{4,12},{5,13},{8,0},{9,1},{12,4},{13,5},{16,24},{17,25... | collective-permute-start | bytes 147464 | tf_op jit(solution)/shard_map/ppermute | solution.py:676
  335.3 5.1 %collective-permute-start.32 = (f32[32,384]{1,0:T(8,128)S(1)}, f32[32,384]{1,0:T(8,128)S(1)}, u32[]{:S(2)}, u32[]{:S(2)}) collective-permute-start(f32[32,384]{1,0:T(8,128)S(1)} %get-tuple-element.273), channel_id=1, source_target_pairs={{0,12},{1,13},{4,0},{5,1},{8,4},{9,5},{12,8},{13,9},{16,28},{17,29... | collective-permute-start | bytes 147464 | tf_op jit(solution)/shard_map/ppermute | solution.py:676
  345.3 42.0 %collective-permute-start.35 = (f32[784,384]{1,0:T(8,128)S(1)}, f32[784,384]{1,0:T(8,128)}, u32[]{:S(2)}, u32[]{:S(2)}) collective-permute-start(f32[784,384]{1,0:T(8,128)S(1)} %copy-done.8), channel_id=1, source_target_pairs={{0,2},{1,3},{4,6},{5,7},{8,10},{9,11},{12,14},{13,15},{16,18},{17,... | collective-permute-start | bytes 3612680 | tf_op jit(solution)/shard_map/ppermute | solution.py:676
  347.9 44.4 %collective-permute-start.41 = (f32[784,384]{1,0:T(8,128)}, f32[784,384]{1,0:T(8,128)}, u32[]{:S(2)}, u32[]{:S(2)}) collective-permute-start(f32[784,384]{1,0:T(8,128)} %get-tuple-element.161.mine), channel_id=1, source_target_pairs={{0,1},{1,0},{4,5},{5,4},{8,9},{9,8},{12,13},{13,12},{16,17},{17,16... | collective-permute-start | bytes 3612680 | tf_op jit(solution)/shard_map/ppermute | solution.py:676
  347.9 28.5 %collective-permute-start.42 = (f32[32,384]{1,0:T(8,128)S(1)}, f32[32,384]{1,0:T(8,128)S(1)}, u32[]{:S(2)}, u32[]{:S(2)}) collective-permute-start(f32[32,384]{1,0:T(8,128)S(1)} %fusion.20), channel_id=1, source_target_pairs={{0,64},{1,65},{4,68},{5,69},{8,72},{9,73},{12,76},{13,77},{16,80},... | collective-permute-start | bytes 147464 | tf_op jit(solution)/shard_map/ppermute | solution.py:676
  350.0 37.3 %copy-start.11 = (f32[784,384]{1,0:T(8,128)S(1)}, f32[784,384]{1,0:T(8,128)}, u32[]{:S(2)}) copy-start(f32[784,384]{1,0:T(8,128)} %copy-done.10) | copy-start | bytes 3612676
  350.0 42.9 %collective-permute-start.40 = (f32[784,384]{1,0:T(8,128)}, f32[784,384]{1,0:T(8,128)}, u32[]{:S(2)}, u32[]{:S(2)}) collective-permute-start(f32[784,384]{1,0:T(8,128)} %get-tuple-element.160.mine), channel_id=1, source_target_pairs={{0,1},{1,0},{4,5},{5,4},{8,9},{9,8},{12,13},{13,12},{16,17},{17,16... | collective-permute-start | bytes 3612680 | tf_op jit(solution)/shard_map/ppermute | solution.py:676
  350.3 49.2 %collective-permute-start.39 = (f32[784,384]{1,0:T(8,128)}, f32[784,384]{1,0:T(8,128)}, u32[]{:S(2)}, u32[]{:S(2)}) collective-permute-start(f32[784,384]{1,0:T(8,128)} %get-tuple-element.159.mine), channel_id=1, source_target_pairs={{0,1},{1,0},{4,5},{5,4},{8,9},{9,8},{12,13},{13,12},{16,17},{17,16... | collective-permute-start | bytes 3612680 | tf_op jit(solution)/shard_map/ppermute | solution.py:676
  376.5 5.8 %collective-permute-start.43 = (f32[32,384]{1,0:T(8,128)S(1)}, f32[32,384]{1,0:T(8,128)S(1)}, u32[]{:S(2)}, u32[]{:S(2)}) collective-permute-start(f32[32,384]{1,0:T(8,128)S(1)} %get-tuple-element.228), channel_id=1, source_target_pairs={{0,4},{1,5},{4,8},{5,9},{8,12},{9,13},{12,0},{13,1},{16,20},{17,21... | collective-permute-start | bytes 147464 | tf_op jit(solution)/shard_map/ppermute | solution.py:676
  382.2 4.1 collective-permute-start.44
  386.3 6.5 %collective-permute-start.45 = (f32[32,384]{1,0:T(8,128)S(1)}, f32[32,384]{1,0:T(8,128)S(1)}, u32[]{:S(2)}, u32[]{:S(2)}) collective-permute-start(f32[32,384]{1,0:T(8,128)S(1)} %get-tuple-element.228), channel_id=1, source_target_pairs={{0,8},{1,9},{4,12},{5,13},{8,0},{9,1},{12,4},{13,5},{16,24},{17,25... | collective-permute-start | bytes 147464 | tf_op jit(solution)/shard_map/ppermute | solution.py:676
  392.2 37.9 %collective-permute-start.37 = (f32[784,384]{1,0:T(8,128)}, f32[784,384]{1,0:T(8,128)}, u32[]{:S(2)}, u32[]{:S(2)}) collective-permute-start(f32[784,384]{1,0:T(8,128)} %get-tuple-element.231.mine), channel_id=1, source_target_pairs={{0,1},{1,0},{4,5},{5,4},{8,9},{9,8},{12,13},{13,12},{16,17},{17,16... | collective-permute-start | bytes 3612680 | tf_op jit(solution)/shard_map/ppermute | solution.py:676
  392.3 40.6 %collective-permute-start.36 = (f32[784,384]{1,0:T(8,128)S(1)}, f32[784,384]{1,0:T(8,128)}, u32[]{:S(2)}, u32[]{:S(2)}) collective-permute-start(f32[784,384]{1,0:T(8,128)S(1)} %get-tuple-element.232.mine), channel_id=1, source_target_pairs={{0,1},{1,0},{4,5},{5,4},{8,9},{9,8},{12,13},{13,12},{16,17},{17,16... | collective-permute-start | bytes 3612680 | tf_op jit(solution)/shard_map/ppermute | solution.py:676
  392.8 34.6 %collective-permute-start.38 = (f32[784,384]{1,0:T(8,128)}, f32[784,384]{1,0:T(8,128)}, u32[]{:S(2)}, u32[]{:S(2)}) collective-permute-start(f32[784,384]{1,0:T(8,128)} %get-tuple-element.238.mine), channel_id=1, source_target_pairs={{0,1},{1,0},{4,5},{5,4},{8,9},{9,8},{12,13},{13,12},{16,17},{17,16... | collective-permute-start | bytes 3612680 | tf_op jit(solution)/shard_map/ppermute | solution.py:676
  392.9 11.9 %collective-permute-start.46 = (f32[128,384]{1,0:T(8,128)S(1)}, f32[128,384]{1,0:T(8,128)S(1)}, u32[]{:S(2)}, u32[]{:S(2)}) collective-permute-start(f32[128,384]{1,0:T(8,128)S(1)} %constant_dynamic-update-slice_fusion.4), channel_id=1, source_target_pairs={{0,16},{1,17},{4,20},{5,21},{8,24},{9,25},{12,28},{13,29},{16,32},... | collective-permute-start | bytes 589832 | tf_op jit(solution)/shard_map/ppermute | solution.py:676
  402.7 11.2 %collective-permute-start.47 = (f32[128,384]{1,0:T(8,128)S(1)}, f32[128,384]{1,0:T(8,128)S(1)}, u32[]{:S(2)}, u32[]{:S(2)}) collective-permute-start(f32[128,384]{1,0:T(8,128)S(1)} %constant_dynamic-update-slice_fusion.4), channel_id=1, source_target_pairs={{0,48},{1,49},{4,52},{5,53},{8,56},{9,57},{12,60},{13,61},{16,0},{... | collective-permute-start | bytes 589832 | tf_op jit(solution)/shard_map/ppermute | solution.py:676
  404.8 18.3 %collective-permute-start.48 = (f32[128,384]{1,0:T(8,128)S(1)}, f32[128,384]{1,0:T(8,128)S(1)}, u32[]{:S(2)}, u32[]{:S(2)}) collective-permute-start(f32[128,384]{1,0:T(8,128)S(1)} %constant_dynamic-update-slice_fusion.4), channel_id=1, source_target_pairs={{0,32},{1,33},{4,36},{5,37},{8,40},{9,41},{12,44},{13,45},{16,48},... | collective-permute-start | bytes 589832 | tf_op jit(solution)/shard_map/ppermute | solution.py:676
  (28 other events, 143.1 us)
Sparse Core Ops, SparseCore 0:
  135.9 94.2 reduce-scatter.1
  299.7 57.9 all-gather.4
  359.9 61.5 all-gather.2

commit v3 on v2

--- a/solution.py
+++ b/solution.py
@@ -34,6 +34,8 @@
 CHUNK = 240
 STORE = EXPERTS * SLOTS + 8
 CLEAR = 248
+CUTS = (0, 336, 1008, 1568, 2352)
+PIECES = (336, 336, 112, 784)
 MASK_FILL = -1e30
 SCALE = 32 ** (-0.5)
 VMEM = 60 * 1024 * 1024
@@ -509,18 +511,21 @@
 
 
 def backward_kernel(
-    first, core, gs_a, gs_b, hidden_ref, g_ref, x_ref, ids_ref, mixed_ref, qkv_ref, prob_ref, window_ref,
+    first, last, core, gs_a, gs_b, hidden_ref, g_ref, x_ref, ids_ref, mixed_ref, qkv_ref, prob_ref, window_ref,
     attn_gain, attn_shift, wqkv, place, place_t, heads, spread, wproj, moe_gain, moe_shift, router, out_bias_t,
     *refs,
 ):
     if first:
         input_grad, grad_wqkv, grad_wproj, small, table, raster_scr, mixed_scr = refs
+        turned = None
         grad_wqkv[...] = jnp.zeros_like(grad_wqkv)
         grad_wproj[...] = jnp.zeros_like(grad_wproj)
         small[...] = jnp.zeros_like(small)
         table[...] = jnp.zeros_like(table)
     else:
-        before, (input_grad, grad_wqkv, grad_wproj, small, table, raster_scr, mixed_scr) = refs[:4], refs[4:]
+        before, refs = refs[:4], refs[4:]
+        turned = refs[5] if last else None
+        input_grad, grad_wqkv, grad_wproj, small, table, raster_scr, mixed_scr = refs[:5] + refs[-2:]
         for was, now in zip(before, (grad_wqkv, grad_wproj, small, table)):
             now[...] = was[...]
 
@@ -587,6 +592,9 @@
         return carry
 
     lax.fori_loop(0, 4, image, 0)
+    if last:
+        for c in range(3):
+            turned[c * 256 : c * 256 + 256, :] = table[c * 64 : c * 64 + 64, :].T
     unit, inverse = norm_parts(x_ref[...].astype(F32))
     attn_low = (unit * attn_gain[...] + attn_shift[...]).astype(LOW)
     raster = raster_scr[...]
@@ -608,8 +616,10 @@
     fixed = fixed + [weights[n] for n in ("wproj", "moe_gain", "moe_shift", "router", "out_bias_t")]
     totals = [(3 * D, D), (D, D), (16, D), (192, 256)]
     before = [] if sums is None else list(sums)
+    last = block == BLOCKS - 1
+    extra = [(768, 64)] if last else []
     return pl.pallas_call(
-        functools.partial(backward_kernel, sums is None),
+        functools.partial(backward_kernel, sums is None, last),
         grid_spec=pltpu.PrefetchScalarGridSpec(
             num_scalar_prefetch=1,
             grid=(1,),
@@ -626,10 +636,10 @@
                 rows(4 * PADDED, D),
             ]
             + [whole(v.shape) for v in fixed + before],
-            out_specs=[whole((BLOCK, D))] + [whole(v) for v in totals],
+            out_specs=[whole((BLOCK, D))] + [whole(v) for v in totals + extra],
             scratch_shapes=[pltpu.VMEM((BLOCK, 3 * D), F32), pltpu.VMEM((BLOCK, D), LOW)],
         ),
-        out_shape=[jax.ShapeDtypeStruct(v, F32) for v in [(BLOCK, D)] + totals],
+        out_shape=[jax.ShapeDtypeStruct(v, F32) for v in [(BLOCK, D)] + totals + extra],
         compiler_params=pltpu.CompilerParams(vmem_limit_bytes=VMEM),
         cost_estimate=pl.CostEstimate(flops=1_000_000, bytes_accessed=100_000, transcendentals=0),
         name="attention_backward",
@@ -637,8 +647,8 @@
 
 
 def head_bias(table, lookup):
-    rows = lax.dot_general(table.astype(LOW), lookup.astype(LOW), (((0,), (1,)), ((), ())), preferred_element_type=F32)
-    return rows.reshape(96, 128)
+    rows = lax.dot_general(table.astype(LOW), jnp.asarray(lookup).astype(LOW), (((0,), (1,)), ((), ())), preferred_element_type=F32)
+    return rows.reshape(32, D)
 
 
 def position_bias(heads, fill):
@@ -647,8 +657,13 @@
 
 
 def table_gradient(sums, lookup):
-    rows = sums.reshape(3, 64, 4, 64).transpose(1, 3, 0, 2).reshape(4096, HEADS)
-    return lax.dot_general(lookup, rows, (((0,), (0,)), ((), ())), precision=lax.Precision.HIGHEST)
+    rows = sums.reshape(HEADS, 4096)
+    high = rows.astype(LOW)
+    rest = (rows - high.astype(F32)).astype(LOW)
+    turned = lookup.reshape(64, 64, 169).transpose(1, 0, 2).reshape(4096, 169)
+    turned = jnp.asarray(turned).astype(LOW)
+    found = nn(jnp.concatenate([high, rest]), turned)
+    return (found[:HEADS] + found[HEADS:]).T
 
 
 AXES = ("dp", "tensor")
@@ -672,6 +687,12 @@
 }
 
 
+PAIR = {
+    "y": pairs(lambda x, y, z, c: (x, y ^ 1, z, c)),
+    "z": pairs(lambda x, y, z, c: (x, y, z ^ 1, c)),
+}
+
+
 def send(values, table):
     return lax.ppermute(values, AXES, table)
 
@@ -680,8 +701,13 @@
     return lax.optimization_barrier((values,) + others)[0]
 
 
-def scatter_near(parts):
-    return [send(quarter(v, at + shift, dim), TURN[axis][shift]) for shift in (1, 3) for v, axis, at, dim in parts]
+def near_pieces(parts):
+    return [quarter(v, at + shift, dim) for shift in (1, 3) for v, axis, at, dim in parts]
+
+
+def near_sends(parts, pieces):
+    tables = [TURN[axis][shift] for shift in (1, 3) for v, axis, at, dim in parts]
+    return [send(piece, table) for piece, table in zip(pieces, tables)]
 
 
 def quarter(values, index, dim):
@@ -727,18 +753,19 @@
     refs[-1][...] = jnp.where(pl.program_id(0) == 0, mine[...], other[...]).astype(refs[-1].dtype)
 
 
-def assemble(core, b, mine, other, kind, before):
-    def spot(i, c):
-        return (jnp.where(i == 0, c[0], 1 - c[0]) * BLOCKS + b, 0)
+def assemble(core, size, first, mine, other, kind, before):
+    def spot(i, j, c):
+        return (jnp.where(i == 0, c[0], 1 - c[0]) * (HALF // size) + first // size + j, 0)
 
     kept = [] if before is None else [before]
+    rows = pl.BlockSpec((size, D), lambda i, j, c: (j, 0))
     return pl.pallas_call(
         assemble_kernel,
         grid_spec=pltpu.PrefetchScalarGridSpec(
             num_scalar_prefetch=1,
-            grid=(2,),
-            in_specs=[whole((BLOCK, D)), whole((BLOCK, D))] + [pl.BlockSpec(memory_space=pl.ANY)] * len(kept),
-            out_specs=pl.BlockSpec((BLOCK, D), spot),
+            grid=(2, mine.shape[0] // size),
+            in_specs=[rows, rows] + [pl.BlockSpec(memory_space=pl.ANY)] * len(kept),
+            out_specs=pl.BlockSpec((size, D), spot),
         ),
         out_shape=jax.ShapeDtypeStruct((2 * HALF, D), kind),
         input_output_aliases={3: 0} if kept else {},
@@ -748,8 +775,8 @@
 
 
 def gather_shards(far, core, own):
+    over = send(own, FAR_SWAP)
     near = send(own, CORE_SWAP)
-    over = send(own, FAR_SWAP)
     last = send(over, CORE_SWAP)
     pick = lambda flag, a, b: jnp.where(flag == 1, a, b)
     low = (pick(core, near, own), pick(core, own, near))
@@ -762,20 +789,20 @@
         [
             qkv_weight.astype(F32).transpose(0, 2, 1).reshape(3 * 96, D),
             proj_weight.astype(F32),
+            head_bias(rel_table, lookup),
+            jnp.pad(qv_bias.astype(F32), ((0, 6), (0, D - 96))),
         ]
     )
     shards = gather_shards(far, core, own)
     wqkv = jnp.stack([v[:288].reshape(3, 96, D) for v in shards], axis=1).reshape(3 * D, D)
     wproj = jnp.concatenate([v[288:384] for v in shards])
-    few = jnp.pad(qv_bias.astype(F32), ((0, 6), (0, 32)))
-    shards = gather_shards(far, core, jnp.concatenate([head_bias(after(rel_table, own), lookup), few]))
-    heads = jnp.stack([v[:96].reshape(3, 64, 64) for v in shards]).reshape(HEADS, 64, 64)
-    bias = jnp.concatenate([v[96:98, :96] for v in shards], axis=1)
+    heads = jnp.stack([v[384:416].reshape(3, 64, 64) for v in shards]).reshape(HEADS, 64, 64)
+    bias = jnp.concatenate([v[416:418, :96] for v in shards], axis=1)
     return wqkv, wproj, bias, heads
 
 
 def pack_rest(shard, sums, in_bias, out_bias, lookup):
-    grad_wqkv, grad_wproj, small, pair_sums = sums
+    grad_wqkv, grad_wproj, small, _, pair_sums = sums
     rows = jnp.pad(table_gradient(pair_sums, lookup).reshape(-1), (0, 8 * D - 169 * HEADS)).reshape(8, D)
     by_shard = jnp.concatenate([grad_wqkv.reshape(3, 4, 96, D), grad_wproj.reshape(1, 4, 96, D)])
 
@@ -797,7 +824,6 @@
     place, fill, lookup, heads, segment = layout_consts()
     consts = (place, place.transpose(0, 2, 1), heads, segment, heads.T)
     consts = tuple(jnp.asarray(v).astype(LOW) for v in consts)
-    lookup = jnp.asarray(lookup)
     wide = lambda v: v.astype(F32).reshape(1, -1)
 
     wqkv, wproj, bias_qv, table = gather_weights(
@@ -829,15 +855,27 @@
         router[:, :16].T, expert_in, expert_in_bias.astype(F32), expert_out,
     )
 
+    sixteen = [[i * 16 + j for j in range(16)] for i in range(2)]
+    gather = lambda v: lax.all_gather(v, "dp", axis=0, axis_index_groups=sixteen, tiled=True)
+    sum_out = lax.psum_scatter(grad_out, "dp", scatter_dimension=0, axis_index_groups=sixteen, tiled=True)
+    cells = grad_in.reshape(4, 4, 2, 96, D)
+    first = [(cells[:, :, 0], "y", at_y, 0), (cells[:, :, 1], "z", at_z, 1)]
+    pieces = near_pieces(first)
+
     gs_theirs = send(gs_theirs, CORE_SWAP).reshape(HALF, D)
-    gs_mine = gs_mine.reshape(HALF, D)
     gg = gg_mine.reshape(HALF) + send(gg_theirs.reshape(HALF), CORE_SWAP)
     gg = jnp.pad(gg.reshape(BLOCKS, BLOCK), ((0, 0), (0, 8 * D - BLOCK))).reshape(BLOCKS, 8, D)
-    gs = [
-        jnp.concatenate([gs_mine[b * BLOCK : (b + 1) * BLOCK] + gs_theirs[b * BLOCK : (b + 1) * BLOCK], gg[b]])
-        for b in range(BLOCKS)
-    ]
+    gs_mine = gs_mine.reshape(HALF, D)
+    pieces, gs_theirs, gs_mine = lax.optimization_barrier((pieces, gs_theirs, gs_mine))
+    near = near_sends(first, pieces)
+
+    def chip_block(b, mine, theirs):
+        return jnp.concatenate([mine[b * BLOCK : (b + 1) * BLOCK] + theirs[b * BLOCK : (b + 1) * BLOCK], gg[b]])
+
+    gs = [chip_block(0, gs_mine, gs_theirs)]
     gs_far = [send(gs[0], FAR_SWAP)]
+    later = lax.optimization_barrier((gs_mine, gs_theirs, gs[0]))
+    gs = gs + [chip_block(b, later[0], later[1]) for b in (1, 2)]
 
     def attend(b, sums):
         return attention_backward(
@@ -845,53 +883,57 @@
             consts, weights, sums,
         )
 
-    sixteen = [[i * 16 + j for j in range(16)] for i in range(2)]
-    gather = lambda v: lax.all_gather(v, "dp", axis=0, axis_index_groups=sixteen, tiled=True)
-    sum_out = lax.psum_scatter(grad_out, "dp", scatter_dimension=0, axis_index_groups=sixteen, tiled=True)
-    cells = grad_in.reshape(4, 4, 2, 96, D)
-    first = [(cells[:, :, 0], "y", at_y, 0), (cells[:, :, 1], "z", at_z, 1)]
-    near = scatter_near(first)
-    ep_theirs, ep_mine = experts_output(core, dest, chunks, after(act, gs[0]), meta, expert_out)
-    ep_mine, near = lax.optimization_barrier((ep_mine, near))
+    act, gs[1], gs[2] = lax.optimization_barrier((act, gs[1], gs[2]))
+    ep_theirs, ep_mine = experts_output(core, dest, chunks, act, meta, expert_out)
+    ep_mine, ep_theirs, near = lax.optimization_barrier((ep_mine, ep_theirs, near))
+    gs_far.append(send(after(gs[1], near[0]), FAR_SWAP))
     across = scatter_across(first, near)
-    gs_far.append(send(gs[1], FAR_SWAP))
-    ep_mine, ep_theirs, gs_far[0] = lax.optimization_barrier((ep_mine, ep_theirs, gs_far[0]))
+    gs_far.append(send(after(gs[2], near[0]), FAR_SWAP))
+    ep_theirs, gs_far[0] = lax.optimization_barrier((ep_theirs, gs_far[0]))
     ep_theirs = send(ep_theirs, CORE_SWAP)
-    gs_far.append(send(after(gs[2], gs_far[0]), FAR_SWAP))
     grad_0, *sums = attend(0, None)
     across, gs_far[1], grad_0, ep_theirs = lax.optimization_barrier((across, gs_far[1], grad_0, ep_theirs))
     halves = scatter_total(first, near, across)
-    second = [(halves[0], "z", at_z, 0), (halves[1], "y", at_y, 0)]
-    near = scatter_near(second)
+    second = [(halves[0], "z", at_z), (halves[1], "y", at_y)]
+    fold = [send(jnp.stack([quarter(v, at ^ 1, 0), quarter(v, at ^ 3, 0)]), PAIR[axis]) for v, axis, at in second]
+    ep = (ep_mine + ep_theirs).reshape(HALF, D)
+    ep = [ep[a:b] for a, b in zip(CUTS, CUTS[1:])]
+    gs_far[1], halves, ep = lax.optimization_barrier((gs_far[1], halves, ep))
+    ep_far = [send(ep[0], FAR_SWAP)]
     grad_1, *sums = attend(1, sums)
-    ep = (ep_mine + ep_theirs).reshape(HALF, D)
-    ep = [ep[b * BLOCK : (b + 1) * BLOCK] for b in range(BLOCKS)]
-    near, sum_out, gs_far[2], grad_1, ep[0] = lax.optimization_barrier((near, sum_out, gs_far[2], grad_1, ep[0]))
+    fold, sum_out, gs_far[2], grad_1, ep_far[0] = lax.optimization_barrier((fold, sum_out, gs_far[2], grad_1, ep_far[0]))
     near_out = send(sum_out, NEAR_SWAP)
-    across = scatter_across(second, near)
-    ep_far = [send(after(ep[0], gs_far[2]), FAR_SWAP)]
+    kept = [quarter(v, at, 0) + got[0] for (v, axis, at), got in zip(second, fold)]
+    over = [send(quarter(v, at ^ 2, 0) + got[1], TURN[axis][2]) for (v, axis, at), got in zip(second, fold)]
+    near_out, over, gs_far[2] = lax.optimization_barrier((near_out, over, gs_far[2]))
+    sum_out = gather(sum_out + near_out)
+    sum_in = jnp.concatenate([v + got for v, got in zip(kept, over)])
+    near_in = send(sum_in, NEAR_SWAP)
+    ep_far.append(send(after(ep[1], sum_in), FAR_SWAP))
+    gs_far[2], sum_in = lax.optimization_barrier((gs_far[2], sum_in))
     grad_2, *sums = attend(2, sums)
-    near_out, across, grad_2, sums, ep_far[0] = lax.optimization_barrier((near_out, across, grad_2, sums, ep_far[0]))
-    sum_out = gather(sum_out + near_out)
-    sum_in = jnp.concatenate(scatter_total(second, near, across))
-    sum_in = gather(sum_in + send(sum_in, NEAR_SWAP))
-    ep_far.append(send(after(ep[1], ep_far[0]), FAR_SWAP))
+    near_in, grad_2, sums, ep_far[1] = lax.optimization_barrier((near_in, grad_2, sums, ep_far[1]))
+    sum_in = gather(sum_in + near_in)
+    ep_far.append(send(after(ep[2], ep_far[1]), FAR_SWAP))
     packed = pack_rest(shard, sums, in_bias, out_bias, lookup)
     (packed,) = scatter_sums([(packed, "y", at_y, 0)])
     (packed,) = scatter_sums([(packed, "z", at_z, 0)])
-    packed, ep_far[1] = lax.optimization_barrier((packed.reshape(32, D), ep_far[1]))
-    packed = packed + send(packed, NEAR_SWAP)
-    ep_far.append(send(after(ep[2], ep_far[1]), FAR_SWAP))
-
-    block_out, input_grad = None, None
-    for b, grad in enumerate((grad_0, grad_1, grad_2)):
-        block = slice(b * BLOCK, (b + 1) * BLOCK)
-        block_half = base[block] + gate[block] * (ep[b] + ep_far[b])
-        block_out = assemble(core, b, block_half, send(block_half, CORE_SWAP), LOW, block_out)
-        input_grad = assemble(core, b, grad, send(grad, CORE_SWAP), F32, input_grad)
+    packed, ep_far[2] = lax.optimization_barrier((packed.reshape(32, D), ep_far[2]))
+    packed_near = send(packed, NEAR_SWAP)
+    ep_far.append(send(after(ep[3], packed_near), FAR_SWAP))
+    packed = packed + packed_near
 
     (packed,) = gather_rows([(packed, "z", at_z)])
     (packed,) = gather_rows([(packed, "y", at_y)])
+    ep_far[3], packed = lax.optimization_barrier((ep_far[3], packed))
+
+    block_out, input_grad = None, None
+    for n, block in enumerate(slice(a, b) for a, b in zip(CUTS, CUTS[1:])):
+        block_half = base[block] + gate[block] * (ep[n] + ep_far[n])
+        block_out = assemble(core, PIECES[n], block.start, block_half, send(block_half, CORE_SWAP), LOW, block_out)
+    for n, grad in enumerate((grad_0, grad_1, grad_2)):
+        input_grad = assemble(core, BLOCK, n * BLOCK, grad, send(grad, CORE_SWAP), F32, input_grad)
+
     few = packed[D : D + 24]
     grad_table = few[16:24].reshape(-1)[: 169 * HEADS].reshape(169, HEADS)
     return (

time: 458 us -> 430 us (0.939)
  the two profiles are of different devices: /device:TPU:10 before, /device:TPU:0 now
where the time goes in v3:
time: 430 us; the launch traced here: 422 us
  Pallas kernels  211 us (49%)
  starting transfers between devices  62.9 us (15%)
  waiting for transfers between devices  54.7 us (13%)
  local copies, waits for them, and re-layouts  41.6 us (10%)
  other arithmetic  32.8 us (8%)
  between operations  15.5 us (4%)
    pallas_call x3, Pallas kernels, attention_backward(): pl.pallas_call(functools.partial(backward_kernel, sums is None, last), gr...  80.8 us
    ppermute x47, starting transfers between devices, send(): return lax.ppermute(values, AXES, table)  62.8 us
    pallas_call x1, Pallas kernels, experts(): pl.pallas_call(experts_kernel, grid_spec=pltpu.PrefetchScalarGridSpec(num...  56.3 us
    ppermute x47, waiting for transfers between devices, send(): return lax.ppermute(values, AXES, table)  54.6 us
    pallas_call x1, Pallas kernels, attention_forward(): pl.pallas_call(attention_kernel, grid_spec=pltpu.PrefetchScalarGridSpec(n...  32.5 us
    pallas_call x7, Pallas kernels, assemble(): pl.pallas_call(assemble_kernel, grid_spec=pltpu.PrefetchScalarGridSpec(nu...  25.3 us
    pallas_call x1, Pallas kernels, experts_output(): pl.pallas_call(output_kernel, grid_spec=pltpu.PrefetchScalarGridSpec(num_...  16.1 us
    unnamed x111, local copies, waits for them, and re-layouts  14.3 us
  transfers between devices with their start and end apart: 50, of which 15 were waited for; matrix products, arithmetic and copies ran while one was open for 12% of the time, Pallas kernels for 29%

profile of v3, /device:TPU:0, one launch (start us, length us, event | category | flops | bytes accessed | tf_op | source)
XLA Modules:
  0.0 421.6 jit_solution(693283369953121004)
XLA Ops:
  8.1 2.3 convolution_bitcast_fusion
  10.5 3.2 collective-permute-start
  13.7 14.6 %collective-permute-done = f32[424,384]{1,0:T(8,128)S(1)} collective-permute-done((f32[424,384]{1,0:T(8,128)S(1)}, f32[424,384]{1,0:T(8,128)S(1)}, u32[]{:S(2)}, u32[]{:S(2)}) %collective-permute-start) | collective-permute-done | bytes 651296 | tf_op jit(solution)/shard_map/ppermute | solution.py:697
  32.9 2.1 copy.101.ids_ref
  39.7 1.4 copy.97
  43.5 32.5 %attention_forward.1 = (f32[2352,384]{1,0:T(8,128)}, f32[2352,384]{1,0:T(8,128)}, f32[2352,384]{1,0:T(8,128)}, f32[2352,1]{1,0:T(8,128)}, bf16[2352,384]{1,0:T(8...) custom-call(s32[1]{0:T(128)} %bitcast.core, ...), custom_call_target="tpu_custom_call" | custom-call | flops 1000000 | bytes 100000 | tf_op jit(solution)/shard_map/attention_forward/pallas_call | solution.py:214
  83.1 56.3 %experts.1 = (f32[3072,384]{1,0:T(8,128)}, f32[3072,384]{1,0:T(8,128)}, f32[8,384]{1,0:T(8,128)}, f32[8,384]{1,0:T(8,128)}, bf16[7680,384]{1,0:T(8,128)(2,1)}, /...) custom-call(s32[1]{0:T(128)} %bitcast.core, ...), custom_call_target="tpu_custom_call" | custom-call | flops 1000000 | bytes 100000 | tf_op jit(solution)/shard_map/experts/pallas_call | solution.py:386
  141.0 2.7 fusion.27
  143.7 1.3 dynamic-slice_bitcast_fusion
  145.5 1.2 dynamic-slice_bitcast_fusion.2
  147.1 1.8 slice_add_fusion.2
  150.0 3.3 collective-permute-start.13
  153.2 1.7 collective-permute-start.6
  154.9 1.9 collective-permute-start.7
  156.8 1.5 collective-permute-start.8
  158.3 2.6 collective-permute-start.9
  160.9 2.6 slice_add_fusion
  163.6 1.2 pad_maximum_fusion.3.gs_a
  165.9 16.1 %experts_output.1 = (f32[14,168,384]{2,1,0:T(8,128)}, f32[14,168,384]{2,1,0:T(8,128)}) custom-call(s32[1]{0:T(128)} %bitcast.core, s32[784]{0:T(1024)} %select_n.305.dest, s32[8]{0:T(128)} %and_select_fusion.chunks, bf16[7680,384]{1,0:T(8,128)(2,1)} %get-tuple-element.122.act_ref, s32[28,2,168]{2,1,0:T(2,128)} %pad_add_fusion.meta_ref, ...), custom_call_target="tpu_custom_call" | custom-call | flops 1000000 | bytes 100000 | tf_op jit(solution)/shard_map/experts_output/pallas_call | solution.py:467
  182.2 1.9 collective-permute-start.12
  184.1 3.2 collective-permute-start.10
  187.3 3.9 collective-permute-start.11
  192.3 26.4 %attention_backward.3 = (f32[784,384]{1,0:T(8,128)}, f32[1152,384]{1,0:T(8,128)}, f32[384,384]{1,0:T(8,128)}, f32[16,384]{1,0:T(8,128)}, f32[192,256]{1,0:T(8,128)}) custom-call(s32[1]{0:T(128)} %bitcast.core, f32[792,384]{1,0:T(8,128)} %pad_maximum_fusion.1.gs_a, f32[792,384]{1,0:T(8,128)} %collective-permute-done.13.gs_b, ...), custom_call_target="tpu_custom_call" | custom-call | flops 1000000 | bytes 100000 | tf_op jit(solution)/shard_map/attention_backward/pallas_call | solution.py:621
  218.7 3.7 add.484
  225.4 2.2 fusion.7
  229.7 3.0 collective-permute-start.18
  233.7 27.1 %attention_backward.4 = (f32[784,384]{1,0:T(8,128)}, f32[1152,384]{1,0:T(8,128)}, f32[384,384]{1,0:T(8,128)}, f32[16,384]{1,0:T(8,128)}, f32[192,256]{1,0:T(8,128)}) custom-call(s32[1]{0:T(128)} %bitcast.core, f32[792,384]{1,0:T(8,128)} %pad_maximum_fusion.2.gs_a, f32[792,384]{1,0:T(8,128)} %collective-permute-done.12.gs_b, ...), custom_call_target="tpu_custom_call" | custom-call | flops 1000000 | bytes 100000 | tf_op jit(solution)/shard_map/attention_backward/pallas_call | solution.py:621
  262.0 1.2 collective-permute-start.21
  263.2 1.4 collective-permute-start.19
  266.7 2.1 collective-permute-done.21
  268.7 3.5 collective-permute-done.20
  272.3 1.7 add.543
  276.0 2.1 collective-permute-start.23
  278.3 27.3 %attention_backward.5 = (f32[784,384]{1,0:T(8,128)}, f32[1152,384]{1,0:T(8,128)}, f32[384,384]{1,0:T(8,128)}, f32[16,384]{1,0:T(8,128)}, f32[192,256]{1,0:T(8,128)}, /*index=5*/f32[768,64]{1,0:T(8,128)}) custom-call(s32[1]{0:T(128)} %bitcast.core, f32[792,384]{1,0:T(8,128)} %pad_maximum_fusion.3.gs_a, f32[792,384]{1,0:T(8,128)} %collective-permute-done.17.gs_b, ...), custom_call_target="tpu_custom_call" | custom-call | flops 1000000 | bytes 100000 | tf_op jit(solution)/shard_map/attention_backward/pallas_call | solution.py:621
  308.3 1.3 fusion.5
  310.6 1.2 slice_reduce_fusion.1
  311.8 2.8 collective-permute-start.31
  315.1 4.2 collective-permute-start.27
  320.4 7.5 %collective-permute-done.25 = f32[128,384]{1,0:T(8,128)S(1)} collective-permute-done((f32[128,384]{1,0:T(8,128)S(1)}, f32[128,384]{1,0:T(8,128)S(1)}, u32[]{:S(2)}, u32[]{:S(2)}) %collective-permute-start.25) | collective-permute-done | bytes 196640 | tf_op jit(solution)/shard_map/ppermute | solution.py:697
  327.8 6.2 %collective-permute-done.27 = f32[128,384]{1,0:T(8,128)S(1)} collective-permute-done((f32[128,384]{1,0:T(8,128)S(1)}, f32[128,384]{1,0:T(8,128)S(1)}, u32[]{:S(2)}, u32[]{:S(2)}) %collective-permute-start.27) | collective-permute-done | bytes 196640 | tf_op jit(solution)/shard_map/ppermute | solution.py:697
  334.1 1.6 collective-permute-start.28
  335.7 3.2 collective-permute-start.30
  338.8 1.3 collective-permute-start.29
  341.5 1.4 collective-permute-done.29
  343.2 1.2 multiply_add_fusion.3.mine
  344.4 2.7 collective-permute-done.32
  347.5 2.4 collective-permute-start.33
  349.9 1.5 multiply_add_fusion.1.mine
  351.4 2.3 collective-permute-start.35
  353.7 1.2 collective-permute-start.36
  355.8 3.9 collective-permute-done.36
  360.0 1.8 collective-permute-start.39
  361.8 2.6 collective-permute-start.38
  364.5 4.2 collective-permute-done.37
  369.9 4.6 %collective-permute-done.33 = f32[784,384]{1,0:T(8,128)S(1)} collective-permute-done((f32[784,384]{1,0:T(8,128)S(1)}, f32[784,384]{1,0:T(8,128)S(1)}, u32[]{:S(2)}, u32[]{:S(2)}) %collective-permute-start.33) | collective-permute-done | bytes 1204256 | tf_op jit(solution)/shard_map/ppermute | solution.py:697
  377.8 3.3 assemble.11.refs_0_
  381.1 2.1 assemble.7.refs_0_
  383.1 3.2 assemble.12.refs_0_
  386.4 4.0 assemble.8.refs_0_
  390.4 3.2 assemble.13
  393.6 6.8 %assemble.9.refs_0_ = bf16[4704,384]{1,0:T(8,128)(2,1)} custom-call(s32[1]{0:T(128)} %bitcast.core, f32[560,384]{1,0:T(8,128)} %copy-done.9, f32[560,384]{1,0:T(8,128)} %collective-permute-done.41.other, bf16[4704,384]{1,0:T(8,128)(2,1)} %assemble.8.refs_0_), custom_call_target="tpu_custom_call", output_to_operand_aliasing={{}: (3, {})} | custom-call | flops 1000000 | bytes 100000 | tf_op jit(solution)/shard_map/assemble/pallas_call | solution.py:762
  404.7 2.8 assemble.10
  407.4 5.0 %copy.130 = f32[8,384,384]{2,1,0:T(8,128)} copy(f32[8,384,384]{2,1,0:T(8,128)} %bitcast.120) | data formatting | bytes 9437184
  412.4 2.2 copy.131
  (319 shorter events, 53.6 us)
Async XLA Ops:
  7.2 253.7 %reduce-scatter.2.cloned.1.call-start = ((), (), s32[]{:S(2)}) async-start(), calls=%async_computation.1 | async-start | bytes 5013504 | tf_op jit(solution)/shard_map/reduce_scatter | solution.py:860
  8.1 23.1 %copy-start.42 = (bf16[384,8]{0,1:T(8,128)(2,1)S(1)}, bf16[384,8]{0,1:T(8,128)(2,1)}, u32[]{:S(2)}) copy-start(bf16[384,8]{0,1:T(8,128)(2,1)} %param.38) | copy-start | bytes 18436
  10.3 22.6 %copy-start.34 = (s32[4704,1]{0,1:T(1,128)S(1)}, s32[4704,1]{0,1:T(1,128)}, u32[]{:S(2)}) copy-start(s32[4704,1]{0,1:T(1,128)} %param.43) | copy-start | bytes 56452
  10.5 17.8 %collective-permute-start = (f32[424,384]{1,0:T(8,128)S(1)}, f32[424,384]{1,0:T(8,128)S(1)}, u32[]{:S(2)}, u32[]{:S(2)}) collective-permute-start(f32[424,384]{1,0:T(8,128)S(1)} %pad_maximum_fusion.8), channel_id=1, source_target_pairs={{0,2},{1,3},{4,6},{5,7},{8,10},{9,11},{12,14},{13,15},{16,18},{17,... | collective-permute-start | bytes 1953800 | tf_op jit(solution)/shard_map/ppermute | solution.py:697
  13.7 21.4 %collective-permute-start.2 = (f32[424,384]{1,0:T(8,128)S(1)}, f32[424,384]{1,0:T(8,128)S(1)}, u32[]{:S(2)}, u32[]{:S(2)}) collective-permute-start(f32[424,384]{1,0:T(8,128)S(1)} %pad_maximum_fusion.8), channel_id=1, source_target_pairs={{0,1},{1,0},{4,5},{5,4},{8,9},{9,8},{12,13},{13,12},{16,17},{17,16... | collective-permute-start | bytes 1953800 | tf_op jit(solution)/shard_map/ppermute | solution.py:697
  28.4 6.7 %collective-permute-start.1 = (f32[424,384]{1,0:T(8,128)S(1)}, f32[424,384]{1,0:T(8,128)S(1)}, u32[]{:S(2)}, u32[]{:S(2)}) collective-permute-start(f32[424,384]{1,0:T(8,128)S(1)} %collective-permute-done), channel_id=1, source_target_pairs={{0,1},{1,0},{4,5},{5,4},{8,9},{9,8},{12,13},{13,12},{16,17},{17,16... | collective-permute-start | bytes 1953800 | tf_op jit(solution)/shard_map/ppermute | solution.py:697
  43.5 33.4 %copy-start.35 = (s32[4704,1]{0,1:T(1,128)S(1)}, s32[4704,1]{0,1:T(1,128)}, u32[]{:S(2)}) copy-start(s32[4704,1]{0,1:T(1,128)} %param.43) | copy-start | bytes 56452
  43.5 33.6 %copy-start.44 = (bf16[8,384]{1,0:T(8,128)(2,1)S(1)}, bf16[8,384]{1,0:T(8,128)(2,1)}, u32[]{:S(2)}) copy-start(bf16[8,384]{1,0:T(8,128)(2,1)} %param.40) | copy-start | bytes 18436
  43.5 34.5 %copy-start.45 = (s32[8,8]{1,0:T(8,128)S(1)}, s32[8,8]{1,0:T(8,128)}, u32[]{:S(2)}) copy-start(s32[8,8]{1,0:T(8,128)} %constant.329.clone) | copy-start | bytes 772
  43.5 34.8 %copy-start.51 = (bf16[168,168,1]{1,0,2:T(8,128)(2,1)S(1)}, bf16[168,168,1]{1,0,2:T(8,128)(2,1)}, u32[]{:S(2)}) copy-start(bf16[168,168,1]{1,0,2:T(8,128)(2,1)} %constant.479) | copy-start | bytes 169348
  43.5 35.1 %copy-start.37 = (s32[28,28]{1,0:T(8,128)S(1)}, s32[28,28]{1,0:T(8,128)}, u32[]{:S(2)}) copy-start(s32[28,28]{1,0:T(8,128)} %constant.330.clone) | copy-start | bytes 9412
  76.0 7.1 %collective-permute-start.3 = (f32[14,168,384]{2,1,0:T(8,128)}, f32[14,168,384]{2,1,0:T(8,128)}, u32[]{:S(2)}, u32[]{:S(2)}) collective-permute-start(f32[14,168,384]{2,1,0:T(8,128)} %bitcast.126), channel_id=1, source_target_pairs={{0,1},{1,0},{4,5},{5,4},{8,9},{9,8},{12,13},{13,12},{16,17},{17,16... | collective-permute-start | bytes 10838024 | tf_op jit(solution)/shard_map/ppermute | solution.py:697
  139.5 7.6 %collective-permute-start.4 = (f32[14,168,384]{2,1,0:T(8,128)}, f32[14,168,384]{2,1,0:T(8,128)}, u32[]{:S(2)}, u32[]{:S(2)}) collective-permute-start(f32[14,168,384]{2,1,0:T(8,128)} %get-tuple-element.114), channel_id=1, source_target_pairs={{0,1},{1,0},{4,5},{5,4},{8,9},{9,8},{12,13},{13,12},{16,17},{17,16... | collective-permute-start | bytes 10838024 | tf_op jit(solution)/shard_map/ppermute | solution.py:697
  139.9 267.5 %all-gather.5.cloned.1.call-start = ((), (), s32[]{:S(2)}) async-start(), calls=%async_computation.3 | async-start | bytes 5013504 | tf_op jit(solution)/shard_map/all_gather | solution.py:859
  140.8 6.1 %collective-permute-start.5 = (f32[2352]{0:T(1024)S(1)}, f32[2352]{0:T(1024)S(1)}, u32[]{:S(2)}, u32[]{:S(2)}) collective-permute-start(f32[2352]{0:T(1024)S(1)} %reshape.286), channel_id=1, source_target_pairs={{0,1},{1,0},{4,5},{5,4},{8,9},{9,8},{12,13},{13,12},{16,17},{17,16... | collective-permute-start | bytes 28232 | tf_op jit(solution)/shard_map/ppermute | solution.py:697
  150.0 32.2 %collective-permute-start.13 = (f32[792,384]{1,0:T(8,128)}, f32[792,384]{1,0:T(8,128)}, u32[]{:S(2)}, u32[]{:S(2)}) collective-permute-start(f32[792,384]{1,0:T(8,128)} %pad_maximum_fusion.1.gs_a), channel_id=1, source_target_pairs={{0,2},{1,3},{4,6},{5,7},{8,10},{9,11},{12,14},{13,15},{16,18},{17,... | collective-permute-start | bytes 3649544 | tf_op jit(solution)/shard_map/ppermute | solution.py:697
  153.2 28.7 %collective-permute-start.6 = (f32[4,96,384]{2,1,0:T(8,128)}, f32[4,96,384]{2,1,0:T(8,128)}, u32[]{:S(2)}, u32[]{:S(2)}) collective-permute-start(f32[4,96,384]{2,1,0:T(8,128)} %get-tuple-element.125), channel_id=1, source_target_pairs={{0,16},{1,17},{4,20},{5,21},{8,24},{9,25},{12,28},{13,29},{16,32},... | collective-permute-start | bytes 1769480 | tf_op jit(solution)/shard_map/ppermute | solution.py:697
  154.9 27.1 %collective-permute-start.7 = (f32[4,96,384]{2,1,0:T(8,128)}, f32[4,96,384]{2,1,0:T(8,128)}, u32[]{:S(2)}, u32[]{:S(2)}) collective-permute-start(f32[4,96,384]{2,1,0:T(8,128)} %get-tuple-element.126), channel_id=1, source_target_pairs={{0,4},{1,5},{4,8},{5,9},{8,12},{9,13},{12,0},{13,1},{16,20},{17,21... | collective-permute-start | bytes 1769480 | tf_op jit(solution)/shard_map/ppermute | solution.py:697
  156.8 25.2 %collective-permute-start.8 = (f32[4,96,384]{2,1,0:T(8,128)}, f32[4,96,384]{2,1,0:T(8,128)}, u32[]{:S(2)}, u32[]{:S(2)}) collective-permute-start(f32[4,96,384]{2,1,0:T(8,128)} %get-tuple-element.127), channel_id=1, source_target_pairs={{0,48},{1,49},{4,52},{5,53},{8,56},{9,57},{12,60},{13,61},{16,0},{... | collective-permute-start | bytes 1769480 | tf_op jit(solution)/shard_map/ppermute | solution.py:697
  158.3 23.9 %collective-permute-start.9 = (f32[4,96,384]{2,1,0:T(8,128)S(1)}, f32[4,96,384]{2,1,0:T(8,128)}, u32[]{:S(2)}, u32[]{:S(2)}) collective-permute-start(f32[4,96,384]{2,1,0:T(8,128)S(1)} %get-tuple-element.128), channel_id=1, source_target_pairs={{0,12},{1,13},{4,0},{5,1},{8,4},{9,5},{12,8},{13,9},{16,28},{17,29... | collective-permute-start | bytes 1769480 | tf_op jit(solution)/shard_map/ppermute | solution.py:697
  182.2 36.5 %collective-permute-start.14 = (f32[14,168,384]{2,1,0:T(8,128)}, f32[14,168,384]{2,1,0:T(8,128)}, u32[]{:S(2)}, u32[]{:S(2)}) collective-permute-start(f32[14,168,384]{2,1,0:T(8,128)} %get-tuple-element.143), channel_id=1, source_target_pairs={{0,1},{1,0},{4,5},{5,4},{8,9},{9,8},{12,13},{13,12},{16,17},{17,16... | collective-permute-start | bytes 10838024 | tf_op jit(solution)/shard_map/ppermute | solution.py:697
  182.2 36.5 %collective-permute-start.12 = (f32[792,384]{1,0:T(8,128)}, f32[792,384]{1,0:T(8,128)}, u32[]{:S(2)}, u32[]{:S(2)}) collective-permute-start(f32[792,384]{1,0:T(8,128)} %pad_maximum_fusion.2.gs_a), channel_id=1, source_target_pairs={{0,2},{1,3},{4,6},{5,7},{8,10},{9,11},{12,14},{13,15},{16,18},{17,... | collective-permute-start | bytes 3649544 | tf_op jit(solution)/shard_map/ppermute | solution.py:697
  184.1 34.6 %collective-permute-start.10 = (f32[4,96,384]{2,1,0:T(8,128)}, f32[4,96,384]{2,1,0:T(8,128)S(1)}, u32[]{:S(2)}, u32[]{:S(2)}) collective-permute-start(f32[4,96,384]{2,1,0:T(8,128)} %get-tuple-element.130), channel_id=1, source_target_pairs={{0,32},{1,33},{4,36},{5,37},{8,40},{9,41},{12,44},{13,45},{16,48},... | collective-permute-start | bytes 1769480 | tf_op jit(solution)/shard_map/ppermute | solution.py:697
  187.3 31.4 %collective-permute-start.11 = (f32[4,96,384]{2,1,0:T(8,128)}, f32[4,96,384]{2,1,0:T(8,128)}, u32[]{:S(2)}, u32[]{:S(2)}) collective-permute-start(f32[4,96,384]{2,1,0:T(8,128)} %get-tuple-element.132), channel_id=1, source_target_pairs={{0,8},{1,9},{4,12},{5,13},{8,0},{9,1},{12,4},{13,5},{16,24},{17,25... | collective-permute-start | bytes 1769480 | tf_op jit(solution)/shard_map/ppermute | solution.py:697
  191.1 69.7 %collective-permute-start.17 = (f32[792,384]{1,0:T(8,128)}, f32[792,384]{1,0:T(8,128)}, u32[]{:S(2)}, u32[]{:S(2)}) collective-permute-start(f32[792,384]{1,0:T(8,128)} %pad_maximum_fusion.3.gs_a), channel_id=1, source_target_pairs={{0,2},{1,3},{4,6},{5,7},{8,10},{9,11},{12,14},{13,15},{16,18},{17,... | collective-permute-start | bytes 3649544 | tf_op jit(solution)/shard_map/ppermute | solution.py:697
  228.5 32.3 %collective-permute-start.15 = (f32[2,96,384]{2,1,0:T(8,128)S(1)}, f32[2,96,384]{2,1,0:T(8,128)}, u32[]{:S(2)}, u32[]{:S(2)}) collective-permute-start(f32[2,96,384]{2,1,0:T(8,128)S(1)} %pad_maximum_fusion.11), channel_id=1, source_target_pairs={{0,4},{1,5},{4,0},{5,1},{8,12},{9,13},{12,8},{13,9},{16,20},{17,21... | collective-permute-start | bytes 884744 | tf_op jit(solution)/shard_map/ppermute | solution.py:697
  229.7 31.2 %collective-permute-start.18 = (f32[336,384]{1,0:T(8,128)}, f32[336,384]{1,0:T(8,128)S(1)}, u32[]{:S(2)}, u32[]{:S(2)}) collective-permute-start(f32[336,384]{1,0:T(8,128)} %bitcast.29), channel_id=1, source_target_pairs={{0,2},{1,3},{4,6},{5,7},{8,10},{9,11},{12,14},{13,15},{16,18},{17,... | collective-permute-start | bytes 1548296 | tf_op jit(solution)/shard_map/ppermute | solution.py:697
  232.7 28.2 %collective-permute-start.16 = (f32[2,96,384]{2,1,0:T(8,128)S(1)}, f32[2,96,384]{2,1,0:T(8,128)}, u32[]{:S(2)}, u32[]{:S(2)}) collective-permute-start(f32[2,96,384]{2,1,0:T(8,128)S(1)} %pad_maximum_fusion.12), channel_id=1, source_target_pairs={{0,16},{1,17},{4,20},{5,21},{8,24},{9,25},{12,28},{13,29},{16,0},{... | collective-permute-start | bytes 884744 | tf_op jit(solution)/shard_map/ppermute | solution.py:697
  233.7 27.2 %copy-start.16 = (f32[4,96,384]{2,1,0:T(8,128)S(1)}, f32[4,96,384]{2,1,0:T(8,128)}, u32[]{:S(2)}) copy-start(f32[4,96,384]{2,1,0:T(8,128)} %copy-done.15) | copy-start | bytes 1769476
  233.7 30.9 %copy-start.14 = (f32[4,96,384]{2,1,0:T(8,128)S(1)}, f32[4,96,384]{2,1,0:T(8,128)}, u32[]{:S(2)}) copy-start(f32[4,96,384]{2,1,0:T(8,128)} %copy-done.13) | copy-start | bytes 1769476
  262.0 6.7 %collective-permute-start.21 = (f32[96,384]{1,0:T(8,128)S(1)}, f32[96,384]{1,0:T(8,128)S(1)}, u32[]{:S(2)}, u32[]{:S(2)}) collective-permute-start(f32[96,384]{1,0:T(8,128)S(1)} %add_bitcast_fusion), channel_id=1, source_target_pairs={{0,32},{1,33},{4,36},{5,37},{8,40},{9,41},{12,44},{13,45},{16,48},... | collective-permute-start | bytes 442376 | tf_op jit(solution)/shard_map/ppermute | solution.py:697
  263.2 9.1 %collective-permute-start.19 = (f32[192,384]{1,0:T(8,128)}, f32[192,384]{1,0:T(8,128)S(1)}, u32[]{:S(2)}, u32[]{:S(2)}) collective-permute-start(f32[192,384]{1,0:T(8,128)} %reduce-scatter.2.cloned.1.call-done), channel_id=1, source_target_pairs={{0,64},{1,65},{4,68},{5,69},{8,72},{9,73},{12,76},{13,77},{16,80},... | collective-permute-start | bytes 884744 | tf_op jit(solution)/shard_map/ppermute | solution.py:697
  265.5 6.7 %collective-permute-start.20 = (f32[96,384]{1,0:T(8,128)S(1)}, f32[96,384]{1,0:T(8,128)S(1)}, u32[]{:S(2)}, u32[]{:S(2)}) collective-permute-start(f32[96,384]{1,0:T(8,128)S(1)} %add_bitcast_fusion.1), channel_id=1, source_target_pairs={{0,8},{1,9},{4,12},{5,13},{8,0},{9,1},{12,4},{13,5},{16,24},{17,25... | collective-permute-start | bytes 442376 | tf_op jit(solution)/shard_map/ppermute | solution.py:697
  274.0 133.4 %all-gather.3.cloned.1.call-start = ((), (), s32[]{:S(2)}) async-start(), calls=%async_computation.2 | async-start | bytes 5013504 | tf_op jit(solution)/shard_map/all_gather | solution.py:859
  276.0 29.6 %collective-permute-start.23 = (f32[672,384]{1,0:T(8,128)S(1)}, f32[672,384]{1,0:T(8,128)}, u32[]{:S(2)}, u32[]{:S(2)}) collective-permute-start(f32[672,384]{1,0:T(8,128)S(1)} %bitcast.122), channel_id=1, source_target_pairs={{0,2},{1,3},{4,6},{5,7},{8,10},{9,11},{12,14},{13,15},{16,18},{17,... | collective-permute-start | bytes 3096584 | tf_op jit(solution)/shard_map/ppermute | solution.py:697
  278.1 27.6 %collective-permute-start.22 = (f32[192,384]{1,0:T(8,128)S(1)}, f32[192,384]{1,0:T(8,128)S(1)}, u32[]{:S(2)}, u32[]{:S(2)}) collective-permute-start(f32[192,384]{1,0:T(8,128)S(1)} %pad_maximum_fusion.13), channel_id=1, source_target_pairs={{0,64},{1,65},{4,68},{5,69},{8,72},{9,73},{12,76},{13,77},{16,80},... | collective-permute-start | bytes 884744 | tf_op jit(solution)/shard_map/ppermute | solution.py:697
  310.5 4.0 collective-permute-start.24
  311.8 31.2 %collective-permute-start.31 = (f32[560,384]{1,0:T(8,128)S(1)}, f32[560,384]{1,0:T(8,128)S(1)}, u32[]{:S(2)}, u32[]{:S(2)}) collective-permute-start(f32[560,384]{1,0:T(8,128)S(1)} %copy-done.8), channel_id=1, source_target_pairs={{0,2},{1,3},{4,6},{5,7},{8,10},{9,11},{12,14},{13,15},{16,18},{17,... | collective-permute-start | bytes 2580488 | tf_op jit(solution)/shard_map/ppermute | solution.py:697
  314.5 25.7 %copy-start.20 = (f32[784,384]{1,0:T(8,128)S(1)}, f32[784,384]{1,0:T(8,128)}, u32[]{:S(2)}) copy-start(f32[784,384]{1,0:T(8,128)} %get-tuple-element.197.mine) | copy-start | bytes 3612676
  314.5 28.6 %copy-start.27 = (f32[336,384]{1,0:T(8,128)S(1)}, f32[336,384]{1,0:T(8,128)}, u32[]{:S(2)}) copy-start(f32[336,384]{1,0:T(8,128)} %copy-done.26) | copy-start | bytes 1548292
  314.7 28.5 %copy-start.7 = (f32[2352,384]{1,0:T(8,128)S(1)}, f32[2352,384]{1,0:T(8,128)}, u32[]{:S(2)}) copy-start(f32[2352,384]{1,0:T(8,128)} %get-tuple-element.109) | copy-start | bytes 10838020
  314.9 12.9 %collective-permute-start.25 = (f32[128,384]{1,0:T(8,128)S(1)}, f32[128,384]{1,0:T(8,128)S(1)}, u32[]{:S(2)}, u32[]{:S(2)}) collective-permute-start(f32[128,384]{1,0:T(8,128)S(1)} %get-tuple-element.299), channel_id=1, source_target_pairs={{0,16},{1,17},{4,20},{5,21},{8,24},{9,25},{12,28},{13,29},{16,32},... | collective-permute-start | bytes 589832 | tf_op jit(solution)/shard_map/ppermute | solution.py:697
  315.1 18.9 %collective-permute-start.27 = (f32[128,384]{1,0:T(8,128)S(1)}, f32[128,384]{1,0:T(8,128)S(1)}, u32[]{:S(2)}, u32[]{:S(2)}) collective-permute-start(f32[128,384]{1,0:T(8,128)S(1)} %get-tuple-element.300), channel_id=1, source_target_pairs={{0,32},{1,33},{4,36},{5,37},{8,40},{9,41},{12,44},{13,45},{16,48},... | collective-permute-start | bytes 589832 | tf_op jit(solution)/shard_map/ppermute | solution.py:697
  319.2 14.8 %collective-permute-start.26 = (f32[128,384]{1,0:T(8,128)S(1)}, f32[128,384]{1,0:T(8,128)S(1)}, u32[]{:S(2)}, u32[]{:S(2)}) collective-permute-start(f32[128,384]{1,0:T(8,128)S(1)} %get-tuple-element.301), channel_id=1, source_target_pairs={{0,48},{1,49},{4,52},{5,53},{8,56},{9,57},{12,60},{13,61},{16,0},{... | collective-permute-start | bytes 589832 | tf_op jit(solution)/shard_map/ppermute | solution.py:697
  334.1 6.3 %collective-permute-start.28 = (f32[32,384]{1,0:T(8,128)S(1)}, f32[32,384]{1,0:T(8,128)S(1)}, u32[]{:S(2)}, u32[]{:S(2)}) collective-permute-start(f32[32,384]{1,0:T(8,128)S(1)} %get-tuple-element.306), channel_id=1, source_target_pairs={{0,4},{1,5},{4,8},{5,9},{8,12},{9,13},{12,0},{13,1},{16,20},{17,21... | collective-permute-start | bytes 147464 | tf_op jit(solution)/shard_map/ppermute | solution.py:697
  335.7 5.8 %collective-permute-start.30 = (f32[32,384]{1,0:T(8,128)S(1)}, f32[32,384]{1,0:T(8,128)S(1)}, u32[]{:S(2)}, u32[]{:S(2)}) collective-permute-start(f32[32,384]{1,0:T(8,128)S(1)} %get-tuple-element.307), channel_id=1, source_target_pairs={{0,8},{1,9},{4,12},{5,13},{8,0},{9,1},{12,4},{13,5},{16,24},{17,25... | collective-permute-start | bytes 147464 | tf_op jit(solution)/shard_map/ppermute | solution.py:697
  338.8 4.1 collective-permute-start.29
  340.3 34.3 %collective-permute-start.46 = (f32[784,384]{1,0:T(8,128)S(1)}, f32[784,384]{1,0:T(8,128)S(1)}, u32[]{:S(2)}, u32[]{:S(2)}) collective-permute-start(f32[784,384]{1,0:T(8,128)S(1)} %copy-done.20), channel_id=1, source_target_pairs={{0,1},{1,0},{4,5},{5,4},{8,9},{9,8},{12,13},{13,12},{16,17},{17,16... | collective-permute-start | bytes 3612680 | tf_op jit(solution)/shard_map/ppermute | solution.py:697
  342.9 4.2 collective-permute-start.32
  344.4 24.3 %copy-start.18 = (f32[336,384]{1,0:T(8,128)}, f32[336,384]{1,0:T(8,128)S(1)}, u32[]{:S(2)}) copy-start(f32[336,384]{1,0:T(8,128)S(1)} %multiply_add_fusion.3.mine) | copy-start | bytes 1548292
  347.1 7.8 %collective-permute-start.34 = (f32[32,384]{1,0:T(8,128)S(1)}, f32[32,384]{1,0:T(8,128)S(1)}, u32[]{:S(2)}, u32[]{:S(2)}) collective-permute-start(f32[32,384]{1,0:T(8,128)S(1)} %get-tuple-element.275), channel_id=1, source_target_pairs={{0,4},{1,5},{4,8},{5,9},{8,12},{9,13},{12,0},{13,1},{16,20},{17,21... | collective-permute-start | bytes 147464 | tf_op jit(solution)/shard_map/ppermute | solution.py:697
  347.5 27.0 %collective-permute-start.33 = (f32[784,384]{1,0:T(8,128)S(1)}, f32[784,384]{1,0:T(8,128)S(1)}, u32[]{:S(2)}, u32[]{:S(2)}) collective-permute-start(f32[784,384]{1,0:T(8,128)S(1)} %copy-done.3), channel_id=1, source_target_pairs={{0,2},{1,3},{4,6},{5,7},{8,10},{9,11},{12,14},{13,15},{16,18},{17,... | collective-permute-start | bytes 3612680 | tf_op jit(solution)/shard_map/ppermute | solution.py:697
  351.4 23.1 %copy-start.6 = (f32[672,384]{1,0:T(8,128)}, f32[672,384]{1,0:T(8,128)S(1)}, u32[]{:S(2)}) copy-start(f32[672,384]{1,0:T(8,128)S(1)} %multiply_add_fusion.1.mine) | copy-start | bytes 3096580
  351.4 4.4 %collective-permute-start.35 = (f32[32,384]{1,0:T(8,128)S(1)}, f32[32,384]{1,0:T(8,128)S(1)}, u32[]{:S(2)}, u32[]{:S(2)}) collective-permute-start(f32[32,384]{1,0:T(8,128)S(1)} %get-tuple-element.275), channel_id=1, source_target_pairs={{0,12},{1,13},{4,0},{5,1},{8,4},{9,5},{12,8},{13,9},{16,28},{17,29... | collective-permute-start | bytes 147464 | tf_op jit(solution)/shard_map/ppermute | solution.py:697
  353.7 6.0 %collective-permute-start.36 = (f32[32,384]{1,0:T(8,128)S(1)}, f32[32,384]{1,0:T(8,128)S(1)}, u32[]{:S(2)}, u32[]{:S(2)}) collective-permute-start(f32[32,384]{1,0:T(8,128)S(1)} %get-tuple-element.275), channel_id=1, source_target_pairs={{0,8},{1,9},{4,12},{5,13},{8,0},{9,1},{12,4},{13,5},{16,24},{17,25... | collective-permute-start | bytes 147464 | tf_op jit(solution)/shard_map/ppermute | solution.py:697
  359.7 9.0 %collective-permute-start.37 = (f32[128,384]{1,0:T(8,128)S(1)}, f32[128,384]{1,0:T(8,128)S(1)}, u32[]{:S(2)}, u32[]{:S(2)}) collective-permute-start(f32[128,384]{1,0:T(8,128)S(1)} %constant_dynamic-update-slice_fusion.4), channel_id=1, source_target_pairs={{0,16},{1,17},{4,20},{5,21},{8,24},{9,25},{12,28},{13,29},{16,32},... | collective-permute-start | bytes 589832 | tf_op jit(solution)/shard_map/ppermute | solution.py:697
  360.0 8.7 %collective-permute-start.39 = (f32[128,384]{1,0:T(8,128)S(1)}, f32[128,384]{1,0:T(8,128)S(1)}, u32[]{:S(2)}, u32[]{:S(2)}) collective-permute-start(f32[128,384]{1,0:T(8,128)S(1)} %constant_dynamic-update-slice_fusion.4), channel_id=1, source_target_pairs={{0,32},{1,33},{4,36},{5,37},{8,40},{9,41},{12,44},{13,45},{16,48},... | collective-permute-start | bytes 589832 | tf_op jit(solution)/shard_map/ppermute | solution.py:697
  361.8 8.1 %collective-permute-start.38 = (f32[128,384]{1,0:T(8,128)S(1)}, f32[128,384]{1,0:T(8,128)S(1)}, u32[]{:S(2)}, u32[]{:S(2)}) collective-permute-start(f32[128,384]{1,0:T(8,128)S(1)} %constant_dynamic-update-slice_fusion.4), channel_id=1, source_target_pairs={{0,48},{1,49},{4,52},{5,53},{8,56},{9,57},{12,60},{13,61},{16,0},{... | collective-permute-start | bytes 589832 | tf_op jit(solution)/shard_map/ppermute | solution.py:697
  368.7 7.8 %collective-permute-start.43 = (f32[336,384]{1,0:T(8,128)S(1)}, f32[336,384]{1,0:T(8,128)S(1)}, u32[]{:S(2)}, u32[]{:S(2)}) collective-permute-start(f32[336,384]{1,0:T(8,128)S(1)} %multiply_add_fusion.3.mine), channel_id=1, source_target_pairs={{0,1},{1,0},{4,5},{5,4},{8,9},{9,8},{12,13},{13,12},{16,17},{17,16... | collective-permute-start | bytes 1548296 | tf_op jit(solution)/shard_map/ppermute | solution.py:697
  368.7 14.4 %collective-permute-start.45 = (f32[784,384]{1,0:T(8,128)}, f32[784,384]{1,0:T(8,128)}, u32[]{:S(2)}, u32[]{:S(2)}) collective-permute-start(f32[784,384]{1,0:T(8,128)} %get-tuple-element.196.mine), channel_id=1, source_target_pairs={{0,1},{1,0},{4,5},{5,4},{8,9},{9,8},{12,13},{13,12},{16,17},{17,16... | collective-permute-start | bytes 3612680 | tf_op jit(solution)/shard_map/ppermute | solution.py:697
  369.9 20.5 %collective-permute-start.44 = (f32[784,384]{1,0:T(8,128)}, f32[784,384]{1,0:T(8,128)}, u32[]{:S(2)}, u32[]{:S(2)}) collective-permute-start(f32[784,384]{1,0:T(8,128)} %get-tuple-element.195.mine), channel_id=1, source_target_pairs={{0,1},{1,0},{4,5},{5,4},{8,9},{9,8},{12,13},{13,12},{16,17},{17,16... | collective-permute-start | bytes 3612680 | tf_op jit(solution)/shard_map/ppermute | solution.py:697
  374.5 11.8 %collective-permute-start.42 = (f32[672,384]{1,0:T(8,128)S(1)}, f32[672,384]{1,0:T(8,128)}, u32[]{:S(2)}, u32[]{:S(2)}) collective-permute-start(f32[672,384]{1,0:T(8,128)S(1)} %multiply_add_fusion.1.mine), channel_id=1, source_target_pairs={{0,1},{1,0},{4,5},{5,4},{8,9},{9,8},{12,13},{13,12},{16,17},{17,16... | collective-permute-start | bytes 3096584 | tf_op jit(solution)/shard_map/ppermute | solution.py:697
  375.4 18.1 %collective-permute-start.41 = (f32[560,384]{1,0:T(8,128)S(1)}, f32[560,384]{1,0:T(8,128)}, u32[]{:S(2)}, u32[]{:S(2)}) collective-permute-start(f32[560,384]{1,0:T(8,128)S(1)} %multiply_add_fusion.2.mine), channel_id=1, source_target_pairs={{0,1},{1,0},{4,5},{5,4},{8,9},{9,8},{12,13},{13,12},{16,17},{17,16... | collective-permute-start | bytes 2580488 | tf_op jit(solution)/shard_map/ppermute | solution.py:697
  377.3 27.4 %collective-permute-start.40 = (f32[784,384]{1,0:T(8,128)S(1)}, f32[784,384]{1,0:T(8,128)}, u32[]{:S(2)}, u32[]{:S(2)}) collective-permute-start(f32[784,384]{1,0:T(8,128)S(1)} %multiply_add_fusion.mine), channel_id=1, source_target_pairs={{0,1},{1,0},{4,5},{5,4},{8,9},{9,8},{12,13},{13,12},{16,17},{17,16... | collective-permute-start | bytes 3612680 | tf_op jit(solution)/shard_map/ppermute | solution.py:697
  (40 other events, 253.2 us)
Sparse Core Ops, SparseCore 0:
  140.1 91.7 reduce-scatter.1
  274.1 56.5 all-gather.4
  333.0 59.0 all-gather.2

commit v4 on v3

--- a/solution.py
+++ b/solution.py
@@ -34,8 +34,8 @@
 CHUNK = 240
 STORE = EXPERTS * SLOTS + 8
 CLEAR = 248
-CUTS = (0, 336, 1008, 1568, 2352)
-PIECES = (336, 336, 112, 784)
+PIECE = 336
+CUTS = (0, 336, 1008, 1680, 2352)
 MASK_FILL = -1e30
 SCALE = 32 ** (-0.5)
 VMEM = 60 * 1024 * 1024
@@ -110,15 +110,22 @@
 
 
 def attention_kernel(
-    core, x_ref, ids_ref, attn_gain, attn_shift, wqkv_wide, bqkv, bias, place, place_t, heads, segment,
-    wproj_wide, bproj, moe_gain, moe_shift, router, out_bias,
-    hidden_ref, base_ref, second_ref, gate_ref, mixed_ref, qkv_ref, prob_ref, window_ref,
-    low_scr, raster_scr, wqkv, wproj, power_scr,
+    core, x_ref, ids_ref, attn_gain, attn_shift, own, near, over, last, bqkv, bias, place, place_t, heads, segment,
+    bproj, moe_gain, moe_shift, router, out_bias,
+    hidden_ref, base_ref, second_ref, gate_ref, mixed_ref, qkv_ref, prob_ref, window_ref, wqkv_rows, wproj,
+    low_scr, raster_scr, wqkv, power_scr,
 ):
     @pl.when(pl.program_id(0) == 0)
     def _():
-        wqkv[...] = wqkv_wide[...].T.astype(LOW)
-        wproj[...] = wproj_wide[...].astype(LOW)
+        for j in range(4):
+            found = last[:D, :]
+            for step, shard in ((2, over), (1, near), (0, own)):
+                found = jnp.where(core[1] == j ^ step, shard[:D, :], found)
+            found = found.astype(LOW)
+            for k in range(3):
+                wqkv_rows[k * D + j * 96 : k * D + j * 96 + 96, :] = found[k * 96 : k * 96 + 96, :]
+            wproj[j * 96 : j * 96 + 96, :] = found[288:, :]
+        wqkv[...] = wqkv_rows[...].astype(F32).T.astype(LOW)
 
     x = x_ref[...].astype(F32)
     unit, _ = norm_parts(x)
@@ -204,12 +211,12 @@
     return pl.BlockSpec(shape, lambda *_: (0,) * len(shape))
 
 
-def attention_forward(core, x, ids, consts, weights, bias):
+def attention_forward(core, x, ids, shards, consts, weights, bias):
     place, place_t, heads, segment, _ = consts
     at_block = lambda width: pl.BlockSpec((BLOCK, width), lambda i, s: (s[0] * BLOCKS + i, 0))
     rows = lambda height, width: pl.BlockSpec((height, width), lambda i, s: (i, 0))
-    fixed = [weights[n] for n in ("attn_gain", "attn_shift", "wqkv", "bqkv")]
-    tail = [weights[n] for n in ("wproj", "bproj", "moe_gain", "moe_shift", "router", "out_bias_pad")]
+    fixed = [weights[n] for n in ("attn_gain", "attn_shift")] + list(shards) + [weights["bqkv"]]
+    tail = [weights[n] for n in ("bproj", "moe_gain", "moe_shift", "router", "out_bias_pad")]
     operands = fixed + [bias, place, place_t, heads, segment] + tail
     return pl.pallas_call(
         attention_kernel,
@@ -226,12 +233,13 @@
                 rows(4 * PADDED, 3 * D),
                 rows(48 * 64, 256),
                 rows(4 * PADDED, D),
+                whole((3 * D, D)),
+                whole((D, D)),
             ],
             scratch_shapes=[
                 pltpu.VMEM((BLOCK, D), LOW),
                 pltpu.VMEM((BLOCK, D), F32),
                 pltpu.VMEM((D, 3 * D), LOW),
-                pltpu.VMEM((D, D), LOW),
                 pltpu.VMEM((768, 256), LOW),
             ],
         ),
@@ -244,6 +252,8 @@
             jax.ShapeDtypeStruct((BLOCKS * 4 * PADDED, 3 * D), LOW),
             jax.ShapeDtypeStruct((BLOCKS * 48 * 64, 256), LOW),
             jax.ShapeDtypeStruct((BLOCKS * 4 * PADDED, D), LOW),
+            jax.ShapeDtypeStruct((3 * D, D), LOW),
+            jax.ShapeDtypeStruct((D, D), LOW),
         ],
         compiler_params=pltpu.CompilerParams(vmem_limit_bytes=VMEM),
         cost_estimate=pl.CostEstimate(flops=1_000_000, bytes_accessed=100_000, transcendentals=0),
@@ -511,24 +521,40 @@
 
 
 def backward_kernel(
-    first, last, core, gs_a, gs_b, hidden_ref, g_ref, x_ref, ids_ref, mixed_ref, qkv_ref, prob_ref, window_ref,
-    attn_gain, attn_shift, wqkv, place, place_t, heads, spread, wproj, moe_gain, moe_shift, router, out_bias_t,
+    block, core, gs_a, gs_b, hidden_ref, g_ref, ids_ref,
+    attn_gain, attn_shift, place, place_t, heads, spread, moe_gain, moe_shift, router, out_bias_t,
+    x_hbm, mixed_hbm, qkv_hbm, prob_hbm, window_hbm, wqkv_hbm, wproj_hbm,
     *refs,
 ):
+    first, last = block == 0, block == BLOCKS - 1
     if first:
-        input_grad, grad_wqkv, grad_wproj, small, table, raster_scr, mixed_scr = refs
-        turned = None
-        grad_wqkv[...] = jnp.zeros_like(grad_wqkv)
-        grad_wproj[...] = jnp.zeros_like(grad_wproj)
-        small[...] = jnp.zeros_like(small)
-        table[...] = jnp.zeros_like(table)
+        before = ()
     else:
         before, refs = refs[:4], refs[4:]
-        turned = refs[5] if last else None
-        input_grad, grad_wqkv, grad_wproj, small, table, raster_scr, mixed_scr = refs[:5] + refs[-2:]
-        for was, now in zip(before, (grad_wqkv, grad_wproj, small, table)):
-            now[...] = was[...]
-
+    input_grad, totals, refs = refs[0], refs[1:5], refs[5:]
+    turned = refs[0] if last else None
+    raster_scr, mixed_scr, x_ref, mixed_ref, qkv_ref, prob_ref, window_ref, wqkv, wproj, sems = refs[-10:]
+    grad_wqkv, grad_wproj, small, table = totals
+
+    def part(ref, rows):
+        return ref.at[pl.ds(block * rows, rows), :]
+
+    here = pl.multiple_of((core[0] * BLOCKS + block) * BLOCK, 16)
+    moves = [
+        (wproj_hbm, wproj),
+        (part(mixed_hbm, BLOCK), mixed_ref),
+        (part(window_hbm, 4 * PADDED), window_ref),
+        (part(qkv_hbm, 4 * PADDED), qkv_ref),
+        (part(prob_hbm, 48 * 64), prob_ref),
+        (x_hbm.at[pl.ds(here, BLOCK), :], x_ref),
+        (wqkv_hbm, wqkv),
+    ] + list(zip(before, totals))
+    moves = [pltpu.make_async_copy(source, target, sems.at[n]) for n, (source, target) in enumerate(moves)]
+    for move in moves[7:] + moves[:7]:
+        move.start()
+    if first:
+        for total in totals:
+            total[...] = jnp.zeros_like(total)
     g_low = g_ref[...]
     g = g_low.astype(F32)
     unit, inverse = norm_parts(hidden_ref[...])
@@ -549,15 +575,21 @@
     logit_rest = (grad_logit - logit_high.astype(F32)).astype(LOW)
     grad_router = tn(logit_high, second) + tn(logit_rest, second)
     grad_second = gs_a[:BLOCK, :] + gs_b[:BLOCK, :] + nt(logit_high, router[...]) + nt(logit_rest, router[...])
+    for move in moves[7:]:
+        move.wait()
     small[3:4, :] += column_sum(grad_second * unit)
     small[4:5, :] += column_sum(grad_second)
     small[8:16, :] += grad_router[:EXPERTS, :]
     grad_hidden = g + norm_back(grad_second, unit, inverse, moe_gain[...])
     grad_low = grad_hidden.astype(LOW)
     small[2:3, :] += column_sum(grad_low.astype(F32))
+    for move in moves[:2]:
+        move.wait()
     grad_wproj[...] += tn(mixed_ref[...], grad_low)
-    mixed_scr[...] = nt(grad_low, wproj[...].astype(LOW)).astype(LOW)
+    mixed_scr[...] = nt(grad_low, wproj[...]).astype(LOW)
     raster_scr[...] = jnp.zeros_like(raster_scr)
+    for move in moves[2:5]:
+        move.wait()
 
     def image(k, carry):
         start = pl.multiple_of(k * 192, 64)
@@ -595,6 +627,8 @@
     if last:
         for c in range(3):
             turned[c * 256 : c * 256 + 256, :] = table[c * 64 : c * 64 + 64, :].T
+    for move in moves[5:7]:
+        move.wait()
     unit, inverse = norm_parts(x_ref[...].astype(F32))
     attn_low = (unit * attn_gain[...] + attn_shift[...]).astype(LOW)
     raster = raster_scr[...]
@@ -602,7 +636,7 @@
     small[6:7, :] += column_sum(raster[:, 2 * D :])
     grads = raster.astype(LOW)
     grad_wqkv[...] += tn(grads, attn_low)
-    grad_in = nn(grads, wqkv[...].astype(LOW))
+    grad_in = nn(grads, wqkv[...])
     small[0:1, :] += column_sum(grad_in * unit)
     small[1:2, :] += column_sum(grad_in)
     input_grad[...] = grad_hidden + norm_back(grad_in, unit, inverse, attn_gain[...])
@@ -612,14 +646,14 @@
     place, place_t, heads, _, spread = consts
     at_block = lambda width: pl.BlockSpec((BLOCK, width), lambda i, s: (s[0] * BLOCKS + block, 0))
     rows = lambda height, width: pl.BlockSpec((height, width), lambda i, s: (block, 0))
-    fixed = [weights[n] for n in ("attn_gain", "attn_shift", "wqkv")] + [place, place_t, heads, spread]
-    fixed = fixed + [weights[n] for n in ("wproj", "moe_gain", "moe_shift", "router", "out_bias_t")]
+    fixed = [weights[n] for n in ("attn_gain", "attn_shift")] + [place, place_t, heads, spread]
+    fixed = fixed + [weights[n] for n in ("moe_gain", "moe_shift", "router", "out_bias_t")]
     totals = [(3 * D, D), (D, D), (16, D), (192, 256)]
     before = [] if sums is None else list(sums)
-    last = block == BLOCKS - 1
-    extra = [(768, 64)] if last else []
+    late = [x, mixed, qkv, prob, window, weights["wqkv"], weights["wproj"]] + before
+    extra = [(768, 64)] if block == BLOCKS - 1 else []
     return pl.pallas_call(
-        functools.partial(backward_kernel, sums is None, last),
+        functools.partial(backward_kernel, block),
         grid_spec=pltpu.PrefetchScalarGridSpec(
             num_scalar_prefetch=1,
             grid=(1,),
@@ -628,22 +662,29 @@
                 whole((BLOCK + 8, D)),
                 rows(BLOCK, D),
                 at_block(D),
-                at_block(D),
                 at_block(1),
-                rows(BLOCK, D),
-                rows(4 * PADDED, 3 * D),
-                rows(48 * 64, 256),
-                rows(4 * PADDED, D),
             ]
-            + [whole(v.shape) for v in fixed + before],
+            + [whole(v.shape) for v in fixed]
+            + [pl.BlockSpec(memory_space=pl.ANY) for v in late],
             out_specs=[whole((BLOCK, D))] + [whole(v) for v in totals + extra],
-            scratch_shapes=[pltpu.VMEM((BLOCK, 3 * D), F32), pltpu.VMEM((BLOCK, D), LOW)],
+            scratch_shapes=[
+                pltpu.VMEM((BLOCK, 3 * D), F32),
+                pltpu.VMEM((BLOCK, D), LOW),
+                pltpu.VMEM((BLOCK, D), LOW),
+                pltpu.VMEM((BLOCK, D), LOW),
+                pltpu.VMEM((4 * PADDED, 3 * D), LOW),
+                pltpu.VMEM((48 * 64, 256), LOW),
+                pltpu.VMEM((4 * PADDED, D), LOW),
+                pltpu.VMEM((3 * D, D), LOW),
+                pltpu.VMEM((D, D), LOW),
+                pltpu.SemaphoreType.DMA((len(late),)),
+            ],
         ),
         out_shape=[jax.ShapeDtypeStruct(v, F32) for v in [(BLOCK, D)] + totals + extra],
         compiler_params=pltpu.CompilerParams(vmem_limit_bytes=VMEM),
         cost_estimate=pl.CostEstimate(flops=1_000_000, bytes_accessed=100_000, transcendentals=0),
         name="attention_backward",
-    )(core, gs_a, gs_b, hidden, g, x, ids, mixed, qkv, prob, window, *fixed, *before)
+    )(core, gs_a, gs_b, hidden, g, ids, *fixed, *late)
 
 
 def head_bias(table, lookup):
@@ -779,9 +820,11 @@
     near = send(own, CORE_SWAP)
     last = send(over, CORE_SWAP)
     pick = lambda flag, a, b: jnp.where(flag == 1, a, b)
-    low = (pick(core, near, own), pick(core, own, near))
-    high = (pick(core, last, over), pick(core, over, last))
-    return [pick(far, high[i], low[i]) for i in (0, 1)] + [pick(far, low[i], high[i]) for i in (0, 1)]
+    few = [v[D:] for v in (own, near, over, last)]
+    low = (pick(core, few[1], few[0]), pick(core, few[0], few[1]))
+    high = (pick(core, few[3], few[2]), pick(core, few[2], few[3]))
+    few = [pick(far, high[i], low[i]) for i in (0, 1)] + [pick(far, low[i], high[i]) for i in (0, 1)]
+    return (own, near, over, last), few
 
 
 def gather_weights(far, core, qkv_weight, qv_bias, rel_table, proj_weight, lookup):
@@ -793,12 +836,10 @@
             jnp.pad(qv_bias.astype(F32), ((0, 6), (0, D - 96))),
         ]
     )
-    shards = gather_shards(far, core, own)
-    wqkv = jnp.stack([v[:288].reshape(3, 96, D) for v in shards], axis=1).reshape(3 * D, D)
-    wproj = jnp.concatenate([v[288:384] for v in shards])
-    heads = jnp.stack([v[384:416].reshape(3, 64, 64) for v in shards]).reshape(HEADS, 64, 64)
-    bias = jnp.concatenate([v[416:418, :96] for v in shards], axis=1)
-    return wqkv, wproj, bias, heads
+    whole_shards, shards = gather_shards(far, core, own)
+    heads = jnp.stack([v[:32].reshape(3, 64, 64) for v in shards]).reshape(HEADS, 64, 64)
+    bias = jnp.concatenate([v[32:34, :96] for v in shards], axis=1)
+    return whole_shards, bias, heads
 
 
 def pack_rest(shard, sums, in_bias, out_bias, lookup):
@@ -826,16 +867,14 @@
     consts = tuple(jnp.asarray(v).astype(LOW) for v in consts)
     wide = lambda v: v.astype(F32).reshape(1, -1)
 
-    wqkv, wproj, bias_qv, table = gather_weights(
+    weight_shards, bias_qv, table = gather_weights(
         far, side, qkv_weight, qv_bias, rel_table, proj_weight, lookup
     )
     router = jnp.pad(router_weight, ((0, 0), (0, 128 - EXPERTS)))
     weights = dict(
         attn_gain=wide(attn_gain),
         attn_shift=wide(attn_shift),
-        wqkv=wqkv,
         bqkv=jnp.concatenate([bias_qv[0:1], jnp.zeros((1, D), F32), bias_qv[1:2]], axis=1),
-        wproj=wproj,
         bproj=wide(proj_bias),
         moe_gain=wide(moe_gain),
         moe_shift=wide(moe_shift),
@@ -846,12 +885,15 @@
     bias = position_bias(table, jnp.asarray(fill))
     spot, dest, chunks = sort_plan(expert_ids)
     meta = jnp.stack([spot, expert_ids.reshape(TILES, TILE)], axis=1)
-    hidden, base, second, gate, mixed, qkv, prob, window = attention_forward(
-        core, tokens_in, expert_ids, consts, weights, bias
+    place_here = jnp.stack([side, shard]).astype(jnp.int32)
+    hidden, base, second, gate, mixed, qkv, prob, window, weights["wqkv"], weights["wproj"] = attention_forward(
+        place_here, tokens_in, expert_ids, weight_shards, consts, weights, bias
     )
     second = second.reshape(HALF_TILES, TILE, D)
+    second_other = send(second, CORE_SWAP)
+    gate, second_other = lax.optimization_barrier((gate.reshape(HALF), second_other))
     grad_in, grad_out, in_bias, out_bias, act, gs_theirs, gg_theirs, gs_mine, gg_mine = experts(
-        core, dest, chunks, second, send(second, CORE_SWAP), cotangent.reshape(TILES, TILE, D), meta,
+        core, dest, chunks, second, second_other, cotangent.reshape(TILES, TILE, D), meta,
         router[:, :16].T, expert_in, expert_in_bias.astype(F32), expert_out,
     )
 
@@ -899,14 +941,18 @@
     ep = (ep_mine + ep_theirs).reshape(HALF, D)
     ep = [ep[a:b] for a, b in zip(CUTS, CUTS[1:])]
     gs_far[1], halves, ep = lax.optimization_barrier((gs_far[1], halves, ep))
+    sum_out, halves = lax.optimization_barrier((sum_out, halves))
+    near_out = send(sum_out, NEAR_SWAP)
     ep_far = [send(ep[0], FAR_SWAP)]
+    gs_far[1], sum_out = lax.optimization_barrier((gs_far[1], sum_out))
     grad_1, *sums = attend(1, sums)
-    fold, sum_out, gs_far[2], grad_1, ep_far[0] = lax.optimization_barrier((fold, sum_out, gs_far[2], grad_1, ep_far[0]))
-    near_out = send(sum_out, NEAR_SWAP)
+    fold, near_out, gs_far[2], grad_1, ep_far[0] = lax.optimization_barrier(
+        (fold, near_out, gs_far[2], grad_1, ep_far[0])
+    )
+    sum_out = gather(sum_out + near_out)
     kept = [quarter(v, at, 0) + got[0] for (v, axis, at), got in zip(second, fold)]
     over = [send(quarter(v, at ^ 2, 0) + got[1], TURN[axis][2]) for (v, axis, at), got in zip(second, fold)]
-    near_out, over, gs_far[2] = lax.optimization_barrier((near_out, over, gs_far[2]))
-    sum_out = gather(sum_out + near_out)
+    over, gs_far[2] = lax.optimization_barrier((over, gs_far[2]))
     sum_in = jnp.concatenate([v + got for v, got in zip(kept, over)])
     near_in = send(sum_in, NEAR_SWAP)
     ep_far.append(send(after(ep[1], sum_in), FAR_SWAP))
@@ -915,24 +961,45 @@
     near_in, grad_2, sums, ep_far[1] = lax.optimization_barrier((near_in, grad_2, sums, ep_far[1]))
     sum_in = gather(sum_in + near_in)
     ep_far.append(send(after(ep[2], ep_far[1]), FAR_SWAP))
+    hold = lax.optimization_barrier
+
+    def half_of(n):
+        block = slice(CUTS[n], CUTS[n + 1])
+        return base[block] + gate[block][:, None] * (ep[n] + ep_far[n])
+
+    def put_grad(n, grad, other, whole_grad):
+        return assemble(core, BLOCK, n * BLOCK, grad, other, F32, whole_grad)
+
+    def put_out(n, half, other, whole_out):
+        return assemble(core, PIECE, CUTS[n], half, other, LOW, whole_out)
+
+    halves_out = [half_of(0), half_of(1)]
     packed = pack_rest(shard, sums, in_bias, out_bias, lookup)
+    others = [send(v, CORE_SWAP) for v in (grad_0, grad_1, halves_out[0])]
+    packed, others, halves_out = hold((packed, others, halves_out))
     (packed,) = scatter_sums([(packed, "y", at_y, 0)])
+    input_grad = put_grad(1, grad_1, others[1], put_grad(0, grad_0, others[0], None))
+    block_out = put_out(0, halves_out[0], others[2], None)
+    packed, input_grad, block_out, half_1, grad_2 = hold((packed, input_grad, block_out, halves_out[1], grad_2))
     (packed,) = scatter_sums([(packed, "z", at_z, 0)])
-    packed, ep_far[2] = lax.optimization_barrier((packed.reshape(32, D), ep_far[2]))
+    other_out = send(half_1, CORE_SWAP)
+    packed, other_out, ep_far[2], grad_2 = hold((packed.reshape(32, D), other_out, ep_far[2], grad_2))
     packed_near = send(packed, NEAR_SWAP)
+    other_grad = send(grad_2, CORE_SWAP)
     ep_far.append(send(after(ep[3], packed_near), FAR_SWAP))
-    packed = packed + packed_near
-
+    half_2 = half_of(2)
+    packed, other_grad, half_2 = hold((packed + packed_near, other_grad, half_2))
     (packed,) = gather_rows([(packed, "z", at_z)])
+    other_half = send(half_2, CORE_SWAP)
+    packed, other_half = hold((packed, other_half))
     (packed,) = gather_rows([(packed, "y", at_y)])
-    ep_far[3], packed = lax.optimization_barrier((ep_far[3], packed))
-
-    block_out, input_grad = None, None
-    for n, block in enumerate(slice(a, b) for a, b in zip(CUTS, CUTS[1:])):
-        block_half = base[block] + gate[block] * (ep[n] + ep_far[n])
-        block_out = assemble(core, PIECES[n], block.start, block_half, send(block_half, CORE_SWAP), LOW, block_out)
-    for n, grad in enumerate((grad_0, grad_1, grad_2)):
-        input_grad = assemble(core, BLOCK, n * BLOCK, grad, send(grad, CORE_SWAP), F32, input_grad)
+    block_out = put_out(1, half_1, other_out, block_out)
+    ep_far[3], packed, block_out, other_half, other_grad = hold((ep_far[3], packed, block_out, other_half, other_grad))
+    half_3 = half_of(3)
+    other_last = send(half_3, CORE_SWAP)
+    input_grad = put_grad(2, grad_2, other_grad, input_grad)
+    block_out = put_out(2, half_2, other_half, block_out)
+    block_out = put_out(3, half_3, other_last, block_out)
 
     few = packed[D : D + 24]
     grad_table = few[16:24].reshape(-1)[: 169 * HEADS].reshape(169, HEADS)

time: 430 us -> 418 us (0.972)
  the two profiles are of different devices: /device:TPU:0 before, /device:TPU:1 now
where the time goes in v4:
time: 418 us; the launch traced here: 410 us
  Pallas kernels  203 us (49%)
  starting transfers between devices  74.7 us (18%)
  waiting for transfers between devices  40.7 us (10%)
  other arithmetic  37.4 us (9%)
  local copies, waits for them, and re-layouts  34 us (8%)
  between operations  15.5 us (4%)
  matrix products  4.49 us (1%)
    ppermute x47, starting transfers between devices, send(): return lax.ppermute(values, AXES, table)  74.6 us
    pallas_call x3, Pallas kernels, attention_backward(): pl.pallas_call(functools.partial(backward_kernel, block), grid_spec=pltpu...  72.5 us
    pallas_call x1, Pallas kernels, experts(): pl.pallas_call(experts_kernel, grid_spec=pltpu.PrefetchScalarGridSpec(num...  56.4 us
    ppermute x47, waiting for transfers between devices, send(): return lax.ppermute(values, AXES, table)  37.7 us
    pallas_call x1, Pallas kernels, attention_forward(): pl.pallas_call(attention_kernel, grid_spec=pltpu.PrefetchScalarGridSpec(n...  34.1 us
    pallas_call x7, Pallas kernels, assemble(): pl.pallas_call(assemble_kernel, grid_spec=pltpu.PrefetchScalarGridSpec(nu...  23.6 us
    pallas_call x1, Pallas kernels, experts_output(): pl.pallas_call(output_kernel, grid_spec=pltpu.PrefetchScalarGridSpec(num_...  16.1 us
    unnamed x97, local copies, waits for them, and re-layouts  13.2 us
  transfers between devices with their start and end apart: 50, of which 12 were waited for; matrix products, arithmetic and copies ran while one was open for 14% of the time, Pallas kernels for 27%

profile of v4, /device:TPU:1, one launch (start us, length us, event | category | flops | bytes accessed | tf_op | source)
XLA Modules:
  0.0 409.5 jit_solution(8492188533878628170)
XLA Ops:
  8.1 2.2 convolution_bitcast_fusion
  11.4 3.7 collective-permute-start.1
  16.0 12.9 %collective-permute-done.1.over = f32[424,384]{1,0:T(8,128)S(1)} collective-permute-done((f32[424,384]{1,0:T(8,128)S(1)}, f32[424,384]{1,0:T(8,128)S(1)}, u32[]{:S(2)}, u32[]{:S(2)}) %collective-permute-start.1) | collective-permute-done | bytes 651296 | tf_op jit(solution)/shard_map/ppermute | solution.py:738
  28.9 1.7 collective-permute-start.2
  35.2 2.1 copy.87.ids_ref
  40.8 34.1 %attention_forward.1 = (f32[2352,384]{1,0:T(8,128)}, f32[2352,384]{1,0:T(8,128)}, f32[2352,384]{1,0:T(8,128)}, f32[2352,1]{1,0:T(8,128)}, bf16[2352,384]{1,0:T(8...) custom-call(s32[2]{0:T(128)} %pad_add_fusion.1.core, ...), custom_call_target="tpu_custom_call" | custom-call | flops 1000000 | bytes 100000 | tf_op jit(solution)/shard_map/attention_forward/pallas_call | solution.py:221
  81.9 56.4 %experts.1 = (f32[3072,384]{1,0:T(8,128)}, f32[3072,384]{1,0:T(8,128)}, f32[8,384]{1,0:T(8,128)}, f32[8,384]{1,0:T(8,128)}, bf16[7680,384]{1,0:T(8,128)(2,1)}, /...) custom-call(s32[1]{0:T(128)} %bitcast.core, ...), custom_call_target="tpu_custom_call" | custom-call | flops 1000000 | bytes 100000 | tf_op jit(solution)/shard_map/experts/pallas_call | solution.py:396
  139.8 2.8 fusion.27
  142.6 1.3 dynamic-slice_bitcast_fusion
  143.9 1.3 dynamic-slice_bitcast_fusion.2
  145.5 1.8 slice_add_fusion.2
  148.4 3.0 collective-permute-start.13
  151.4 1.4 collective-permute-start.6
  152.8 1.6 collective-permute-start.7
  154.4 1.5 collective-permute-start.8
  155.9 2.6 collective-permute-start.9
  158.5 2.6 slice_add_fusion
  163.5 16.1 %experts_output.1 = (f32[14,168,384]{2,1,0:T(8,128)}, f32[14,168,384]{2,1,0:T(8,128)}) custom-call(s32[1]{0:T(128)} %bitcast.core, s32[784]{0:T(1024)} %select_n.305.dest, s32[8]{0:T(128)} %and_select_fusion.chunks, bf16[7680,384]{1,0:T(8,128)(2,1)} %get-tuple-element.150.act_ref, s32[28,2,168]{2,1,0:T(2,128)} %pad_add_fusion.meta_ref, ...), custom_call_target="tpu_custom_call" | custom-call | flops 1000000 | bytes 100000 | tf_op jit(solution)/shard_map/experts_output/pallas_call | solution.py:477
  179.6 1.3 collective-permute-start.14
  180.9 1.5 collective-permute-start.12
  182.4 2.9 collective-permute-start.10
  185.3 3.5 collective-permute-start.11
  189.7 24.0 %attention_backward.3 = (f32[784,384]{1,0:T(8,128)}, f32[1152,384]{1,0:T(8,128)}, f32[384,384]{1,0:T(8,128)}, f32[16,384]{1,0:T(8,128)}, f32[192,256]{1,0:T(8,128)}) custom-call(s32[1]{0:T(128)} %bitcast.core, f32[792,384]{1,0:T(8,128)} %pad_maximum_fusion.gs_a, f32[792,384]{1,0:T(8,128)} %collective-permute-done.13.gs_b, ...), custom_call_target="tpu_custom_call" | custom-call | flops 1000000 | bytes 100000 | tf_op jit(solution)/shard_map/attention_backward/pallas_call | solution.py:655
  213.8 2.6 fusion.7
  218.1 2.6 add.484
  221.9 2.9 collective-permute-start.19
  225.9 3.0 reduce-scatter.2.cloned.1.call-done
  230.0 24.2 %attention_backward.4 = (f32[784,384]{1,0:T(8,128)}, f32[1152,384]{1,0:T(8,128)}, f32[384,384]{1,0:T(8,128)}, f32[16,384]{1,0:T(8,128)}, f32[192,256]{1,0:T(8,128)}) custom-call(s32[1]{0:T(128)} %bitcast.core, f32[792,384]{1,0:T(8,128)} %pad_maximum_fusion.1.gs_a, f32[792,384]{1,0:T(8,128)} %collective-permute-done.12.gs_b, ...), custom_call_target="tpu_custom_call" | custom-call | flops 1000000 | bytes 100000 | tf_op jit(solution)/shard_map/attention_backward/pallas_call | solution.py:655
  256.1 2.1 collective-permute-start.21
  259.2 3.6 collective-permute-start.20
  262.8 2.5 collective-permute-done.20
  267.5 2.2 collective-permute-start.23
  269.9 24.4 %attention_backward.5 = (f32[784,384]{1,0:T(8,128)}, f32[1152,384]{1,0:T(8,128)}, f32[384,384]{1,0:T(8,128)}, f32[16,384]{1,0:T(8,128)}, f32[192,256]{1,0:T(8,128)}, /*index=5*/f32[768,64]{1,0:T(8,128)}) custom-call(s32[1]{0:T(128)} %bitcast.core, f32[792,384]{1,0:T(8,128)} %pad_maximum_fusion.2.gs_a, f32[792,384]{1,0:T(8,128)} %collective-permute-done.18.gs_b, ...), custom_call_target="tpu_custom_call" | custom-call | flops 1000000 | bytes 100000 | tf_op jit(solution)/shard_map/attention_backward/pallas_call | solution.py:655
  296.1 4.3 %collective-permute-start.25 = (f32[784,384]{1,0:T(8,128)}, f32[784,384]{1,0:T(8,128)}, u32[]{:S(2)}, u32[]{:S(2)}) collective-permute-start(f32[784,384]{1,0:T(8,128)} %get-tuple-element.217.mine), channel_id=1, source_target_pairs={{0,1},{1,0},{4,5},{5,4},{8,9},{9,8},{12,13},{13,12},{16,17},{17,16... | collective-permute-start | bytes 3612680 | tf_op jit(solution)/shard_map/ppermute | solution.py:738
  301.6 2.0 fusion.12
  303.9 1.3 fusion.5
  305.8 1.5 multiply_add_fusion.3.mine
  307.5 1.7 multiply_add_fusion.2.mine
  311.0 1.9 collective-permute-start.30
  313.9 3.2 collective-permute-start.35
  317.1 3.2 assemble.7.refs_0_
  320.2 2.0 assemble.9.refs_0_
  322.3 3.3 assemble.8.refs_0_
  328.7 3.3 collective-permute-start.33
  333.9 2.4 collective-permute-done.33
  336.3 2.6 collective-permute-done.35
  339.0 2.0 collective-permute-start.38
  340.9 1.4 collective-permute-start.36
  342.3 1.8 multiply_add_fusion.1.mine
  346.1 3.0 collective-permute-start.37
  349.1 2.5 collective-permute-start.41
  353.1 4.6 %collective-permute-done.39 = f32[32,384]{1,0:T(8,128)S(1)} collective-permute-done((f32[32,384]{1,0:T(8,128)S(1)}, f32[32,384]{1,0:T(8,128)S(1)}, u32[]{:S(2)}, u32[]{:S(2)}) %collective-permute-start.39) | collective-permute-done | bytes 49184 | tf_op jit(solution)/shard_map/ppermute | solution.py:738
  358.6 4.0 assemble.10.refs_0_
  362.6 1.9 collective-permute-start.45
  364.5 1.9 collective-permute-start.44
  366.5 3.1 collective-permute-done.43
  369.6 5.2 %collective-permute-done.44 = f32[128,384]{1,0:T(8,128)S(1)} collective-permute-done((f32[128,384]{1,0:T(8,128)S(1)}, f32[128,384]{1,0:T(8,128)S(1)}, u32[]{:S(2)}, u32[]{:S(2)}) %collective-permute-start.44) | collective-permute-done | bytes 196640 | tf_op jit(solution)/shard_map/ppermute | solution.py:738
  375.9 1.8 multiply_add_fusion.mine
  377.7 1.3 collective-permute-start.46
  382.0 3.2 assemble.13
  385.2 4.0 assemble.11.refs_0_
  391.4 4.0 assemble.12
  395.3 5.0 %copy.116 = f32[8,384,384]{2,1,0:T(8,128)} copy(f32[8,384,384]{2,1,0:T(8,128)} %bitcast.108) | data formatting | bytes 9437184
  400.4 2.2 copy.117
  (291 shorter events, 56.0 us)
Async XLA Ops:
  7.2 24.0 %copy-start.40 = (bf16[384]{0:T(512)(128)(2,1)S(1)}, bf16[384]{0:T(512)(128)(2,1)}, u32[]{:S(2)}) copy-start(bf16[384]{0:T(512)(128)(2,1)} %param.30) | copy-start | bytes 2308
  7.2 24.6 %copy-start.41 = (bf16[384]{0:T(512)(128)(2,1)S(1)}, bf16[384]{0:T(512)(128)(2,1)}, u32[]{:S(2)}) copy-start(bf16[384]{0:T(512)(128)(2,1)} %param.36) | copy-start | bytes 2308
  7.2 25.1 %copy-start.42 = (bf16[384]{0:T(512)(128)(2,1)S(1)}, bf16[384]{0:T(512)(128)(2,1)}, u32[]{:S(2)}) copy-start(bf16[384]{0:T(512)(128)(2,1)} %param.37) | copy-start | bytes 2308
  7.3 25.7 %copy-start.43 = (bf16[384]{0:T(512)(128)(2,1)S(1)}, bf16[384]{0:T(512)(128)(2,1)}, u32[]{:S(2)}) copy-start(bf16[384]{0:T(512)(128)(2,1)} %param.35) | copy-start | bytes 2308
  7.3 26.2 %copy-start.35 = (bf16[384,8]{0,1:T(8,128)(2,1)S(1)}, bf16[384,8]{0,1:T(8,128)(2,1)}, u32[]{:S(2)}) copy-start(bf16[384,8]{0,1:T(8,128)(2,1)} %param.38) | copy-start | bytes 18436
  7.3 26.4 %copy-start.36 = (bf16[8,384]{1,0:T(8,128)(2,1)S(1)}, bf16[8,384]{1,0:T(8,128)(2,1)}, u32[]{:S(2)}) copy-start(bf16[8,384]{1,0:T(8,128)(2,1)} %param.42) | copy-start | bytes 18436
  7.3 221.5 %reduce-scatter.2.cloned.1.call-start = ((), (), s32[]{:S(2)}) async-start(), calls=%async_computation.1 | async-start | bytes 5013504 | tf_op jit(solution)/shard_map/reduce_scatter | solution.py:902
  8.1 27.1 %copy-start.29 = (s32[4704,1]{0,1:T(1,128)S(1)}, s32[4704,1]{0,1:T(1,128)}, u32[]{:S(2)}) copy-start(s32[4704,1]{0,1:T(1,128)} %param.43) | copy-start | bytes 56452
  11.4 27.1 %copy-start.11 = (f32[424,384]{1,0:T(8,128)}, f32[424,384]{1,0:T(8,128)S(1)}, u32[]{:S(2)}) copy-start(f32[424,384]{1,0:T(8,128)S(1)} %pad_maximum_fusion.7.own) | copy-start | bytes 1953796
  11.4 17.5 %collective-permute-start.1 = (f32[424,384]{1,0:T(8,128)S(1)}, f32[424,384]{1,0:T(8,128)S(1)}, u32[]{:S(2)}, u32[]{:S(2)}) collective-permute-start(f32[424,384]{1,0:T(8,128)S(1)} %pad_maximum_fusion.7.own), channel_id=1, source_target_pairs={{0,2},{1,3},{4,6},{5,7},{8,10},{9,11},{12,14},{13,15},{16,18},{17,... | collective-permute-start | bytes 1953800 | tf_op jit(solution)/shard_map/ppermute | solution.py:738
  15.0 22.9 %collective-permute-start = (f32[424,384]{1,0:T(8,128)S(1)}, f32[424,384]{1,0:T(8,128)S(1)}, u32[]{:S(2)}, u32[]{:S(2)}) collective-permute-start(f32[424,384]{1,0:T(8,128)S(1)} %pad_maximum_fusion.7.own), channel_id=1, source_target_pairs={{0,1},{1,0},{4,5},{5,4},{8,9},{9,8},{12,13},{13,12},{16,17},{17,16... | collective-permute-start | bytes 1953800 | tf_op jit(solution)/shard_map/ppermute | solution.py:738
  28.9 9.0 %collective-permute-start.2 = (f32[424,384]{1,0:T(8,128)S(1)}, f32[424,384]{1,0:T(8,128)S(1)}, u32[]{:S(2)}, u32[]{:S(2)}) collective-permute-start(f32[424,384]{1,0:T(8,128)S(1)} %collective-permute-done.1.over), channel_id=1, source_target_pairs={{0,1},{1,0},{4,5},{5,4},{8,9},{9,8},{12,13},{13,12},{16,17},{17,16... | collective-permute-start | bytes 1953800 | tf_op jit(solution)/shard_map/ppermute | solution.py:738
  40.7 34.8 %copy-start.37 = (bf16[8,384]{1,0:T(8,128)(2,1)S(1)}, bf16[8,384]{1,0:T(8,128)(2,1)}, u32[]{:S(2)}) copy-start(bf16[8,384]{1,0:T(8,128)(2,1)} %param.40) | copy-start | bytes 18436
  40.7 35.6 %copy-start.38 = (s32[8,8]{1,0:T(8,128)S(1)}, s32[8,8]{1,0:T(8,128)}, u32[]{:S(2)}) copy-start(s32[8,8]{1,0:T(8,128)} %constant.329.clone) | copy-start | bytes 772
  40.7 35.9 %copy-start.44 = (bf16[168,168,1]{1,0,2:T(8,128)(2,1)S(1)}, bf16[168,168,1]{1,0,2:T(8,128)(2,1)}, u32[]{:S(2)}) copy-start(bf16[168,168,1]{1,0,2:T(8,128)(2,1)} %constant.464) | copy-start | bytes 169348
  40.8 36.2 %copy-start.30 = (s32[28,28]{1,0:T(8,128)S(1)}, s32[28,28]{1,0:T(8,128)}, u32[]{:S(2)}) copy-start(s32[28,28]{1,0:T(8,128)} %constant.330.clone) | copy-start | bytes 9412
  74.9 7.0 %collective-permute-start.3 = (f32[14,168,384]{2,1,0:T(8,128)}, f32[14,168,384]{2,1,0:T(8,128)}, u32[]{:S(2)}, u32[]{:S(2)}) collective-permute-start(f32[14,168,384]{2,1,0:T(8,128)} %bitcast.118), channel_id=1, source_target_pairs={{0,1},{1,0},{4,5},{5,4},{8,9},{9,8},{12,13},{13,12},{16,17},{17,16... | collective-permute-start | bytes 10838024 | tf_op jit(solution)/shard_map/ppermute | solution.py:738
  138.2 7.3 %collective-permute-start.4 = (f32[14,168,384]{2,1,0:T(8,128)}, f32[14,168,384]{2,1,0:T(8,128)}, u32[]{:S(2)}, u32[]{:S(2)}) collective-permute-start(f32[14,168,384]{2,1,0:T(8,128)} %get-tuple-element.142), channel_id=1, source_target_pairs={{0,1},{1,0},{4,5},{5,4},{8,9},{9,8},{12,13},{13,12},{16,17},{17,16... | collective-permute-start | bytes 10838024 | tf_op jit(solution)/shard_map/ppermute | solution.py:738
  138.4 256.9 %all-gather.5.cloned.1.call-start = ((), (), s32[]{:S(2)}) async-start(), calls=%async_computation.3 | async-start | bytes 5013504 | tf_op jit(solution)/shard_map/all_gather | solution.py:901
  139.3 6.1 %collective-permute-start.5 = (f32[2352]{0:T(1024)S(1)}, f32[2352]{0:T(1024)S(1)}, u32[]{:S(2)}, u32[]{:S(2)}) collective-permute-start(f32[2352]{0:T(1024)S(1)} %reshape.290), channel_id=1, source_target_pairs={{0,1},{1,0},{4,5},{5,4},{8,9},{9,8},{12,13},{13,12},{16,17},{17,16... | collective-permute-start | bytes 28232 | tf_op jit(solution)/shard_map/ppermute | solution.py:738
  148.4 31.2 %collective-permute-start.13 = (f32[792,384]{1,0:T(8,128)}, f32[792,384]{1,0:T(8,128)}, u32[]{:S(2)}, u32[]{:S(2)}) collective-permute-start(f32[792,384]{1,0:T(8,128)} %pad_maximum_fusion.gs_a), channel_id=1, source_target_pairs={{0,2},{1,3},{4,6},{5,7},{8,10},{9,11},{12,14},{13,15},{16,18},{17,... | collective-permute-start | bytes 3649544 | tf_op jit(solution)/shard_map/ppermute | solution.py:738
  151.4 28.1 %collective-permute-start.6 = (f32[4,96,384]{2,1,0:T(8,128)}, f32[4,96,384]{2,1,0:T(8,128)S(1)}, u32[]{:S(2)}, u32[]{:S(2)}) collective-permute-start(f32[4,96,384]{2,1,0:T(8,128)} %get-tuple-element.153), channel_id=1, source_target_pairs={{0,16},{1,17},{4,20},{5,21},{8,24},{9,25},{12,28},{13,29},{16,32},... | collective-permute-start | bytes 1769480 | tf_op jit(solution)/shard_map/ppermute | solution.py:738
  152.8 26.8 %collective-permute-start.7 = (f32[4,96,384]{2,1,0:T(8,128)}, f32[4,96,384]{2,1,0:T(8,128)}, u32[]{:S(2)}, u32[]{:S(2)}) collective-permute-start(f32[4,96,384]{2,1,0:T(8,128)} %get-tuple-element.154), channel_id=1, source_target_pairs={{0,4},{1,5},{4,8},{5,9},{8,12},{9,13},{12,0},{13,1},{16,20},{17,21... | collective-permute-start | bytes 1769480 | tf_op jit(solution)/shard_map/ppermute | solution.py:738
  154.4 25.1 %collective-permute-start.8 = (f32[4,96,384]{2,1,0:T(8,128)}, f32[4,96,384]{2,1,0:T(8,128)}, u32[]{:S(2)}, u32[]{:S(2)}) collective-permute-start(f32[4,96,384]{2,1,0:T(8,128)} %get-tuple-element.155), channel_id=1, source_target_pairs={{0,48},{1,49},{4,52},{5,53},{8,56},{9,57},{12,60},{13,61},{16,0},{... | collective-permute-start | bytes 1769480 | tf_op jit(solution)/shard_map/ppermute | solution.py:738
  155.9 23.6 %collective-permute-start.9 = (f32[4,96,384]{2,1,0:T(8,128)}, f32[4,96,384]{2,1,0:T(8,128)}, u32[]{:S(2)}, u32[]{:S(2)}) collective-permute-start(f32[4,96,384]{2,1,0:T(8,128)} %get-tuple-element.156), channel_id=1, source_target_pairs={{0,12},{1,13},{4,0},{5,1},{8,4},{9,5},{12,8},{13,9},{16,28},{17,29... | collective-permute-start | bytes 1769480 | tf_op jit(solution)/shard_map/ppermute | solution.py:738
  179.6 34.2 %collective-permute-start.14 = (f32[14,168,384]{2,1,0:T(8,128)}, f32[14,168,384]{2,1,0:T(8,128)}, u32[]{:S(2)}, u32[]{:S(2)}) collective-permute-start(f32[14,168,384]{2,1,0:T(8,128)} %get-tuple-element.173), channel_id=1, source_target_pairs={{0,1},{1,0},{4,5},{5,4},{8,9},{9,8},{12,13},{13,12},{16,17},{17,16... | collective-permute-start | bytes 10838024 | tf_op jit(solution)/shard_map/ppermute | solution.py:738
  180.9 32.9 %collective-permute-start.12 = (f32[792,384]{1,0:T(8,128)}, f32[792,384]{1,0:T(8,128)}, u32[]{:S(2)}, u32[]{:S(2)}) collective-permute-start(f32[792,384]{1,0:T(8,128)} %pad_maximum_fusion.1.gs_a), channel_id=1, source_target_pairs={{0,2},{1,3},{4,6},{5,7},{8,10},{9,11},{12,14},{13,15},{16,18},{17,... | collective-permute-start | bytes 3649544 | tf_op jit(solution)/shard_map/ppermute | solution.py:738
  182.4 31.3 %collective-permute-start.10 = (f32[4,96,384]{2,1,0:T(8,128)}, f32[4,96,384]{2,1,0:T(8,128)}, u32[]{:S(2)}, u32[]{:S(2)}) collective-permute-start(f32[4,96,384]{2,1,0:T(8,128)} %get-tuple-element.158), channel_id=1, source_target_pairs={{0,32},{1,33},{4,36},{5,37},{8,40},{9,41},{12,44},{13,45},{16,48},... | collective-permute-start | bytes 1769480 | tf_op jit(solution)/shard_map/ppermute | solution.py:738
  185.3 28.4 %collective-permute-start.11 = (f32[4,96,384]{2,1,0:T(8,128)}, f32[4,96,384]{2,1,0:T(8,128)}, u32[]{:S(2)}, u32[]{:S(2)}) collective-permute-start(f32[4,96,384]{2,1,0:T(8,128)} %get-tuple-element.160), channel_id=1, source_target_pairs={{0,8},{1,9},{4,12},{5,13},{8,0},{9,1},{12,4},{13,5},{16,24},{17,25... | collective-permute-start | bytes 1769480 | tf_op jit(solution)/shard_map/ppermute | solution.py:738
  189.5 64.6 %collective-permute-start.18 = (f32[792,384]{1,0:T(8,128)}, f32[792,384]{1,0:T(8,128)}, u32[]{:S(2)}, u32[]{:S(2)}) collective-permute-start(f32[792,384]{1,0:T(8,128)} %pad_maximum_fusion.2.gs_a), channel_id=1, source_target_pairs={{0,2},{1,3},{4,6},{5,7},{8,10},{9,11},{12,14},{13,15},{16,18},{17,... | collective-permute-start | bytes 3649544 | tf_op jit(solution)/shard_map/ppermute | solution.py:738
  217.4 36.8 %collective-permute-start.15 = (f32[2,96,384]{2,1,0:T(8,128)}, f32[2,96,384]{2,1,0:T(8,128)}, u32[]{:S(2)}, u32[]{:S(2)}) collective-permute-start(f32[2,96,384]{2,1,0:T(8,128)} %pad_maximum_fusion.9), channel_id=1, source_target_pairs={{0,4},{1,5},{4,0},{5,1},{8,12},{9,13},{12,8},{13,9},{16,20},{17,21... | collective-permute-start | bytes 884744 | tf_op jit(solution)/shard_map/ppermute | solution.py:738
  221.9 45.6 %copy-start.7 = (f32[4,168,384]{2,1,0:T(8,128)}, f32[4,168,384]{2,1,0:T(8,128)S(1)}, u32[]{:S(2)}) copy-start(f32[4,168,384]{2,1,0:T(8,128)S(1)} %get-tuple-element.320) | copy-start | bytes 3096580
  221.9 32.3 %collective-permute-start.19 = (f32[336,384]{1,0:T(8,128)}, f32[336,384]{1,0:T(8,128)}, u32[]{:S(2)}, u32[]{:S(2)}) collective-permute-start(f32[336,384]{1,0:T(8,128)} %bitcast.25), channel_id=1, source_target_pairs={{0,2},{1,3},{4,6},{5,7},{8,10},{9,11},{12,14},{13,15},{16,18},{17,... | collective-permute-start | bytes 1548296 | tf_op jit(solution)/shard_map/ppermute | solution.py:738
  225.5 28.7 %collective-permute-start.16 = (f32[2,96,384]{2,1,0:T(8,128)}, f32[2,96,384]{2,1,0:T(8,128)}, u32[]{:S(2)}, u32[]{:S(2)}) collective-permute-start(f32[2,96,384]{2,1,0:T(8,128)} %pad_maximum_fusion.10), channel_id=1, source_target_pairs={{0,16},{1,17},{4,20},{5,21},{8,24},{9,25},{12,28},{13,29},{16,0},{... | collective-permute-start | bytes 884744 | tf_op jit(solution)/shard_map/ppermute | solution.py:738
  228.8 25.4 %collective-permute-start.17 = (f32[192,384]{1,0:T(8,128)}, f32[192,384]{1,0:T(8,128)S(1)}, u32[]{:S(2)}, u32[]{:S(2)}) collective-permute-start(f32[192,384]{1,0:T(8,128)} %reduce-scatter.2.cloned.1.call-done), channel_id=1, source_target_pairs={{0,64},{1,65},{4,68},{5,69},{8,72},{9,73},{12,76},{13,77},{16,80},... | collective-permute-start | bytes 884744 | tf_op jit(solution)/shard_map/ppermute | solution.py:738
  230.0 24.2 %copy-start.25 = (f32[192,384]{1,0:T(8,128)S(1)}, f32[192,384]{1,0:T(8,128)}, u32[]{:S(2)}) copy-start(f32[192,384]{1,0:T(8,128)} %reduce-scatter.2.cloned.1.call-done) | copy-start | bytes 884740
  255.0 140.3 %all-gather.3.cloned.1.call-start = ((), (), s32[]{:S(2)}) async-start(), calls=%async_computation.2 | async-start | bytes 5013504 | tf_op jit(solution)/shard_map/all_gather | solution.py:901
  256.1 6.7 %collective-permute-start.21 = (f32[96,384]{1,0:T(8,128)S(1)}, f32[96,384]{1,0:T(8,128)S(1)}, u32[]{:S(2)}, u32[]{:S(2)}) collective-permute-start(f32[96,384]{1,0:T(8,128)S(1)} %add_bitcast_fusion), channel_id=1, source_target_pairs={{0,32},{1,33},{4,36},{5,37},{8,40},{9,41},{12,44},{13,45},{16,48},... | collective-permute-start | bytes 442376 | tf_op jit(solution)/shard_map/ppermute | solution.py:738
  259.2 6.1 %collective-permute-start.20 = (f32[96,384]{1,0:T(8,128)S(1)}, f32[96,384]{1,0:T(8,128)S(1)}, u32[]{:S(2)}, u32[]{:S(2)}) collective-permute-start(f32[96,384]{1,0:T(8,128)S(1)} %add_bitcast_fusion.1), channel_id=1, source_target_pairs={{0,8},{1,9},{4,12},{5,13},{8,0},{9,1},{12,4},{13,5},{16,24},{17,25... | collective-permute-start | bytes 442376 | tf_op jit(solution)/shard_map/ppermute | solution.py:738
  267.5 27.7 %collective-permute-start.23 = (f32[672,384]{1,0:T(8,128)S(1)}, f32[672,384]{1,0:T(8,128)}, u32[]{:S(2)}, u32[]{:S(2)}) collective-permute-start(f32[672,384]{1,0:T(8,128)S(1)} %bitcast.114), channel_id=1, source_target_pairs={{0,2},{1,3},{4,6},{5,7},{8,10},{9,11},{12,14},{13,15},{16,18},{17,... | collective-permute-start | bytes 3096584 | tf_op jit(solution)/shard_map/ppermute | solution.py:738
  269.7 25.5 %collective-permute-start.22 = (f32[192,384]{1,0:T(8,128)S(1)}, f32[192,384]{1,0:T(8,128)S(1)}, u32[]{:S(2)}, u32[]{:S(2)}) collective-permute-start(f32[192,384]{1,0:T(8,128)S(1)} %pad_maximum_fusion.11), channel_id=1, source_target_pairs={{0,64},{1,65},{4,68},{5,69},{8,72},{9,73},{12,76},{13,77},{16,80},... | collective-permute-start | bytes 884744 | tf_op jit(solution)/shard_map/ppermute | solution.py:738
  296.1 13.5 %collective-permute-start.25 = (f32[784,384]{1,0:T(8,128)}, f32[784,384]{1,0:T(8,128)}, u32[]{:S(2)}, u32[]{:S(2)}) collective-permute-start(f32[784,384]{1,0:T(8,128)} %get-tuple-element.217.mine), channel_id=1, source_target_pairs={{0,1},{1,0},{4,5},{5,4},{8,9},{9,8},{12,13},{13,12},{16,17},{17,16... | collective-permute-start | bytes 3612680 | tf_op jit(solution)/shard_map/ppermute | solution.py:738
  300.4 9.2 %collective-permute-start.26 = (f32[784,384]{1,0:T(8,128)}, f32[784,384]{1,0:T(8,128)}, u32[]{:S(2)}, u32[]{:S(2)}) collective-permute-start(f32[784,384]{1,0:T(8,128)} %get-tuple-element.218.mine), channel_id=1, source_target_pairs={{0,1},{1,0},{4,5},{5,4},{8,9},{9,8},{12,13},{13,12},{16,17},{17,16... | collective-permute-start | bytes 3612680 | tf_op jit(solution)/shard_map/ppermute | solution.py:738
  305.3 4.0 collective-permute-start.24
  307.3 2.3 collective-permute-start.27
  310.6 14.9 %collective-permute-start.28 = (f32[128,384]{1,0:T(8,128)}, f32[128,384]{1,0:T(8,128)S(1)}, u32[]{:S(2)}, u32[]{:S(2)}) collective-permute-start(f32[128,384]{1,0:T(8,128)} %get-tuple-element.336), channel_id=1, source_target_pairs={{0,16},{1,17},{4,20},{5,21},{8,24},{9,25},{12,28},{13,29},{16,32},... | collective-permute-start | bytes 589832 | tf_op jit(solution)/shard_map/ppermute | solution.py:738
  311.0 14.6 %collective-permute-start.30 = (f32[128,384]{1,0:T(8,128)}, f32[128,384]{1,0:T(8,128)}, u32[]{:S(2)}, u32[]{:S(2)}) collective-permute-start(f32[128,384]{1,0:T(8,128)} %get-tuple-element.337), channel_id=1, source_target_pairs={{0,32},{1,33},{4,36},{5,37},{8,40},{9,41},{12,44},{13,45},{16,48},... | collective-permute-start | bytes 589832 | tf_op jit(solution)/shard_map/ppermute | solution.py:738
  312.9 12.7 %collective-permute-start.29 = (f32[128,384]{1,0:T(8,128)S(1)}, f32[128,384]{1,0:T(8,128)}, u32[]{:S(2)}, u32[]{:S(2)}) collective-permute-start(f32[128,384]{1,0:T(8,128)S(1)} %get-tuple-element.338), channel_id=1, source_target_pairs={{0,48},{1,49},{4,52},{5,53},{8,56},{9,57},{12,60},{13,61},{16,0},{... | collective-permute-start | bytes 589832 | tf_op jit(solution)/shard_map/ppermute | solution.py:738
  313.9 25.1 %collective-permute-start.35 = (f32[672,384]{1,0:T(8,128)S(1)}, f32[672,384]{1,0:T(8,128)}, u32[]{:S(2)}, u32[]{:S(2)}) collective-permute-start(f32[672,384]{1,0:T(8,128)S(1)} %bitcast.112), channel_id=1, source_target_pairs={{0,2},{1,3},{4,6},{5,7},{8,10},{9,11},{12,14},{13,15},{16,18},{17,... | collective-permute-start | bytes 3096584 | tf_op jit(solution)/shard_map/ppermute | solution.py:738
  326.8 12.2 %collective-permute-start.34 = (f32[672,384]{1,0:T(8,128)S(1)}, f32[672,384]{1,0:T(8,128)S(1)}, u32[]{:S(2)}, u32[]{:S(2)}) collective-permute-start(f32[672,384]{1,0:T(8,128)S(1)} %multiply_add_fusion.2.mine), channel_id=1, source_target_pairs={{0,1},{1,0},{4,5},{5,4},{8,9},{9,8},{12,13},{13,12},{16,17},{17,16... | collective-permute-start | bytes 3096584 | tf_op jit(solution)/shard_map/ppermute | solution.py:738
  328.0 5.8 %collective-permute-start.31 = (f32[32,384]{1,0:T(8,128)S(1)}, f32[32,384]{1,0:T(8,128)S(1)}, u32[]{:S(2)}, u32[]{:S(2)}) collective-permute-start(f32[32,384]{1,0:T(8,128)S(1)} %get-tuple-element.343), channel_id=1, source_target_pairs={{0,4},{1,5},{4,8},{5,9},{8,12},{9,13},{12,0},{13,1},{16,20},{17,21... | collective-permute-start | bytes 147464 | tf_op jit(solution)/shard_map/ppermute | solution.py:738
  328.7 7.6 %collective-permute-start.33 = (f32[32,384]{1,0:T(8,128)S(1)}, f32[32,384]{1,0:T(8,128)S(1)}, u32[]{:S(2)}, u32[]{:S(2)}) collective-permute-start(f32[32,384]{1,0:T(8,128)S(1)} %get-tuple-element.344), channel_id=1, source_target_pairs={{0,8},{1,9},{4,12},{5,13},{8,0},{9,1},{12,4},{13,5},{16,24},{17,25... | collective-permute-start | bytes 147464 | tf_op jit(solution)/shard_map/ppermute | solution.py:738
  332.0 4.3 %collective-permute-start.32 = (f32[32,384]{1,0:T(8,128)S(1)}, f32[32,384]{1,0:T(8,128)S(1)}, u32[]{:S(2)}, u32[]{:S(2)}) collective-permute-start(f32[32,384]{1,0:T(8,128)S(1)} %get-tuple-element.345), channel_id=1, source_target_pairs={{0,12},{1,13},{4,0},{5,1},{8,4},{9,5},{12,8},{13,9},{16,28},{17,29... | collective-permute-start | bytes 147464 | tf_op jit(solution)/shard_map/ppermute | solution.py:738
  339.0 5.2 %collective-permute-start.38 = (f32[784,384]{1,0:T(8,128)}, f32[784,384]{1,0:T(8,128)S(1)}, u32[]{:S(2)}, u32[]{:S(2)}) collective-permute-start(f32[784,384]{1,0:T(8,128)} %get-tuple-element.235.mine), channel_id=1, source_target_pairs={{0,1},{1,0},{4,5},{5,4},{8,9},{9,8},{12,13},{13,12},{16,17},{17,16... | collective-permute-start | bytes 3612680 | tf_op jit(solution)/shard_map/ppermute | solution.py:738
  340.9 3.2 collective-permute-start.36
  345.2 12.6 %collective-permute-start.42 = (f32[672,384]{1,0:T(8,128)S(1)}, f32[672,384]{1,0:T(8,128)S(1)}, u32[]{:S(2)}, u32[]{:S(2)}) collective-permute-start(f32[672,384]{1,0:T(8,128)S(1)} %multiply_add_fusion.1.mine), channel_id=1, source_target_pairs={{0,1},{1,0},{4,5},{5,4},{8,9},{9,8},{12,13},{13,12},{16,17},{17,16... | collective-permute-start | bytes 3096584 | tf_op jit(solution)/shard_map/ppermute | solution.py:738
  346.1 29.7 %collective-permute-start.37 = (f32[672,384]{1,0:T(8,128)S(1)}, f32[672,384]{1,0:T(8,128)}, u32[]{:S(2)}, u32[]{:S(2)}) collective-permute-start(f32[672,384]{1,0:T(8,128)S(1)} %bitcast.110), channel_id=1, source_target_pairs={{0,2},{1,3},{4,6},{5,7},{8,10},{9,11},{12,14},{13,15},{16,18},{17,... | collective-permute-start | bytes 3096584 | tf_op jit(solution)/shard_map/ppermute | solution.py:738
  349.1 8.7 %collective-permute-start.41 = (f32[32,384]{1,0:T(8,128)S(1)}, f32[32,384]{1,0:T(8,128)S(1)}, u32[]{:S(2)}, u32[]{:S(2)}) collective-permute-start(f32[32,384]{1,0:T(8,128)S(1)} %add.521), channel_id=1, source_target_pairs={{0,8},{1,9},{4,12},{5,13},{8,0},{9,1},{12,4},{13,5},{16,24},{17,25... | collective-permute-start | bytes 147464 | tf_op jit(solution)/shard_map/ppermute | solution.py:738
  351.6 6.1 %collective-permute-start.40 = (f32[32,384]{1,0:T(8,128)S(1)}, f32[32,384]{1,0:T(8,128)S(1)}, u32[]{:S(2)}, u32[]{:S(2)}) collective-permute-start(f32[32,384]{1,0:T(8,128)S(1)} %add.521), channel_id=1, source_target_pairs={{0,12},{1,13},{4,0},{5,1},{8,4},{9,5},{12,8},{13,9},{16,28},{17,29... | collective-permute-start | bytes 147464 | tf_op jit(solution)/shard_map/ppermute | solution.py:738
  352.1 5.7 %collective-permute-start.39 = (f32[32,384]{1,0:T(8,128)S(1)}, f32[32,384]{1,0:T(8,128)S(1)}, u32[]{:S(2)}, u32[]{:S(2)}) collective-permute-start(f32[32,384]{1,0:T(8,128)S(1)} %add.521), channel_id=1, source_target_pairs={{0,4},{1,5},{4,8},{5,9},{8,12},{9,13},{12,0},{13,1},{16,20},{17,21... | collective-permute-start | bytes 147464 | tf_op jit(solution)/shard_map/ppermute | solution.py:738
  357.8 11.7 %collective-permute-start.43 = (f32[128,384]{1,0:T(8,128)S(1)}, f32[128,384]{1,0:T(8,128)S(1)}, u32[]{:S(2)}, u32[]{:S(2)}) collective-permute-start(f32[128,384]{1,0:T(8,128)S(1)} %constant_dynamic-update-slice_fusion.4), channel_id=1, source_target_pairs={{0,16},{1,17},{4,20},{5,21},{8,24},{9,25},{12,28},{13,29},{16,32},... | collective-permute-start | bytes 589832 | tf_op jit(solution)/shard_map/ppermute | solution.py:738
  362.6 13.3 %collective-permute-start.45 = (f32[128,384]{1,0:T(8,128)S(1)}, f32[128,384]{1,0:T(8,128)S(1)}, u32[]{:S(2)}, u32[]{:S(2)}) collective-permute-start(f32[128,384]{1,0:T(8,128)S(1)} %constant_dynamic-update-slice_fusion.4), channel_id=1, source_target_pairs={{0,32},{1,33},{4,36},{5,37},{8,40},{9,41},{12,44},{13,45},{16,48},... | collective-permute-start | bytes 589832 | tf_op jit(solution)/shard_map/ppermute | solution.py:738
  364.5 10.2 %collective-permute-start.44 = (f32[128,384]{1,0:T(8,128)S(1)}, f32[128,384]{1,0:T(8,128)S(1)}, u32[]{:S(2)}, u32[]{:S(2)}) collective-permute-start(f32[128,384]{1,0:T(8,128)S(1)} %constant_dynamic-update-slice_fusion.4), channel_id=1, source_target_pairs={{0,48},{1,49},{4,52},{5,53},{8,56},{9,57},{12,60},{13,61},{16,0},{... | collective-permute-start | bytes 589832 | tf_op jit(solution)/shard_map/ppermute | solution.py:738
  377.7 12.7 %collective-permute-start.46 = (f32[672,384]{1,0:T(8,128)S(1)}, f32[672,384]{1,0:T(8,128)S(1)}, u32[]{:S(2)}, u32[]{:S(2)}) collective-permute-start(f32[672,384]{1,0:T(8,128)S(1)} %multiply_add_fusion.mine), channel_id=1, source_target_pairs={{0,1},{1,0},{4,5},{5,4},{8,9},{9,8},{12,13},{13,12},{16,17},{17,16... | collective-permute-start | bytes 3096584 | tf_op jit(solution)/shard_map/ppermute | solution.py:738
  (31 other events, 154.9 us)
Sparse Core Ops, SparseCore 0:
  138.6 90.2 reduce-scatter.1
  255.1 54.9 all-gather.4
  312.3 63.2 all-gather.2

commit v5 on v4

--- a/solution.py
+++ b/solution.py
@@ -34,8 +34,7 @@
 CHUNK = 240
 STORE = EXPERTS * SLOTS + 8
 CLEAR = 248
-PIECE = 336
-CUTS = (0, 336, 1008, 1680, 2352)
+CUTS = (0, 336, 1008, 1568, 2352)
 MASK_FILL = -1e30
 SCALE = 32 ** (-0.5)
 VMEM = 60 * 1024 * 1024
@@ -790,26 +789,33 @@
     return fulls
 
 
-def assemble_kernel(core, mine, other, *refs):
-    refs[-1][...] = jnp.where(pl.program_id(0) == 0, mine[...], other[...]).astype(refs[-1].dtype)
-
-
-def assemble(core, size, first, mine, other, kind, before):
-    def spot(i, j, c):
-        return (jnp.where(i == 0, c[0], 1 - c[0]) * (HALF // size) + first // size + j, 0)
-
+def assemble_kernel(first, core, mine, other, *refs):
+    out, ready, sems = refs[-3:]
+    rows = mine.shape[0]
+    moves = []
+    for n, (source, half) in enumerate(((mine, core[0]), (other, 1 - core[0]))):
+        ready[n] = source[...].astype(out.dtype)
+        target = out.at[pl.ds(pl.multiple_of(half * HALF + first, 16), rows), :]
+        moves.append(pltpu.make_async_copy(ready.at[n], target, sems.at[n]))
+        moves[n].start()
+    for move in moves:
+        move.wait()
+
+
+def assemble(core, first, mine, other, kind, before):
     kept = [] if before is None else [before]
-    rows = pl.BlockSpec((size, D), lambda i, j, c: (j, 0))
     return pl.pallas_call(
-        assemble_kernel,
+        functools.partial(assemble_kernel, first),
         grid_spec=pltpu.PrefetchScalarGridSpec(
             num_scalar_prefetch=1,
-            grid=(2, mine.shape[0] // size),
-            in_specs=[rows, rows] + [pl.BlockSpec(memory_space=pl.ANY)] * len(kept),
-            out_specs=pl.BlockSpec((size, D), spot),
+            grid=(1,),
+            in_specs=[whole(mine.shape), whole(other.shape)] + [pl.BlockSpec(memory_space=pl.ANY)] * len(kept),
+            out_specs=pl.BlockSpec(memory_space=pl.ANY),
+            scratch_shapes=[pltpu.VMEM((2,) + mine.shape, kind), pltpu.SemaphoreType.DMA((2,))],
         ),
         out_shape=jax.ShapeDtypeStruct((2 * HALF, D), kind),
         input_output_aliases={3: 0} if kept else {},
+        compiler_params=pltpu.CompilerParams(vmem_limit_bytes=VMEM),
         cost_estimate=pl.CostEstimate(flops=1_000_000, bytes_accessed=100_000, transcendentals=0),
         name="assemble",
     )(core, mine, other, *kept)
@@ -929,38 +935,30 @@
     ep_theirs, ep_mine = experts_output(core, dest, chunks, act, meta, expert_out)
     ep_mine, ep_theirs, near = lax.optimization_barrier((ep_mine, ep_theirs, near))
     gs_far.append(send(after(gs[1], near[0]), FAR_SWAP))
-    across = scatter_across(first, near)
     gs_far.append(send(after(gs[2], near[0]), FAR_SWAP))
     ep_theirs, gs_far[0] = lax.optimization_barrier((ep_theirs, gs_far[0]))
     ep_theirs = send(ep_theirs, CORE_SWAP)
     grad_0, *sums = attend(0, None)
-    across, gs_far[1], grad_0, ep_theirs = lax.optimization_barrier((across, gs_far[1], grad_0, ep_theirs))
+    near, gs_far[1], grad_0, ep_theirs = lax.optimization_barrier((near, gs_far[1], grad_0, ep_theirs))
+    across = scatter_across(first, near)
+    ep = (ep_mine + ep_theirs).reshape(HALF, D)
+    ep = [ep[a:b] for a, b in zip(CUTS, CUTS[1:])]
+    gs_far[1], ep = lax.optimization_barrier((gs_far[1], ep))
+    ep_far = [send(ep[0], FAR_SWAP)]
+    grad_1, *sums = attend(1, sums)
+    across, sum_out, gs_far[2], grad_1 = lax.optimization_barrier((across, sum_out, gs_far[2], grad_1))
+    near_out = send(sum_out, NEAR_SWAP)
     halves = scatter_total(first, near, across)
     second = [(halves[0], "z", at_z), (halves[1], "y", at_y)]
     fold = [send(jnp.stack([quarter(v, at ^ 1, 0), quarter(v, at ^ 3, 0)]), PAIR[axis]) for v, axis, at in second]
-    ep = (ep_mine + ep_theirs).reshape(HALF, D)
-    ep = [ep[a:b] for a, b in zip(CUTS, CUTS[1:])]
-    gs_far[1], halves, ep = lax.optimization_barrier((gs_far[1], halves, ep))
-    sum_out, halves = lax.optimization_barrier((sum_out, halves))
-    near_out = send(sum_out, NEAR_SWAP)
-    ep_far = [send(ep[0], FAR_SWAP)]
-    gs_far[1], sum_out = lax.optimization_barrier((gs_far[1], sum_out))
-    grad_1, *sums = attend(1, sums)
-    fold, near_out, gs_far[2], grad_1, ep_far[0] = lax.optimization_barrier(
-        (fold, near_out, gs_far[2], grad_1, ep_far[0])
-    )
+    ep_far.append(send(ep[1], FAR_SWAP))
+    gs_far[2], halves = lax.optimization_barrier((gs_far[2], halves))
+    grad_2, *sums = attend(2, sums)
+    fold, near_out, grad_2, sums, ep_far[0] = lax.optimization_barrier((fold, near_out, grad_2, sums, ep_far[0]))
     sum_out = gather(sum_out + near_out)
     kept = [quarter(v, at, 0) + got[0] for (v, axis, at), got in zip(second, fold)]
     over = [send(quarter(v, at ^ 2, 0) + got[1], TURN[axis][2]) for (v, axis, at), got in zip(second, fold)]
-    over, gs_far[2] = lax.optimization_barrier((over, gs_far[2]))
-    sum_in = jnp.concatenate([v + got for v, got in zip(kept, over)])
-    near_in = send(sum_in, NEAR_SWAP)
-    ep_far.append(send(after(ep[1], sum_in), FAR_SWAP))
-    gs_far[2], sum_in = lax.optimization_barrier((gs_far[2], sum_in))
-    grad_2, *sums = attend(2, sums)
-    near_in, grad_2, sums, ep_far[1] = lax.optimization_barrier((near_in, grad_2, sums, ep_far[1]))
-    sum_in = gather(sum_in + near_in)
-    ep_far.append(send(after(ep[2], ep_far[1]), FAR_SWAP))
+
     hold = lax.optimization_barrier
 
     def half_of(n):
@@ -968,15 +966,21 @@
         return base[block] + gate[block][:, None] * (ep[n] + ep_far[n])
 
     def put_grad(n, grad, other, whole_grad):
-        return assemble(core, BLOCK, n * BLOCK, grad, other, F32, whole_grad)
+        return assemble(core, n * BLOCK, grad, other, F32, whole_grad)
 
     def put_out(n, half, other, whole_out):
-        return assemble(core, PIECE, CUTS[n], half, other, LOW, whole_out)
-
-    halves_out = [half_of(0), half_of(1)]
+        return assemble(core, CUTS[n], half, other, LOW, whole_out)
+
+    halves_out = [half_of(0)]
     packed = pack_rest(shard, sums, in_bias, out_bias, lookup)
+    packed, over, ep_far[1] = hold((packed, over, ep_far[1]))
+    sum_in = jnp.concatenate([v + got for v, got in zip(kept, over)])
+    near_in = send(sum_in, NEAR_SWAP)
+    ep_far.append(send(after(ep[2], sum_in), FAR_SWAP))
+    halves_out.append(half_of(1))
     others = [send(v, CORE_SWAP) for v in (grad_0, grad_1, halves_out[0])]
-    packed, others, halves_out = hold((packed, others, halves_out))
+    others, near_in = hold((others, near_in))
+    sum_in = gather(sum_in + near_in)
     (packed,) = scatter_sums([(packed, "y", at_y, 0)])
     input_grad = put_grad(1, grad_1, others[1], put_grad(0, grad_0, others[0], None))
     block_out = put_out(0, halves_out[0], others[2], None)

time: 418 us -> 448 us (1.072)
  the two profiles are of different devices: /device:TPU:1 before, /device:TPU:0 now
where the time goes in v5:
time: 448 us; the launch traced here: 440 us
  Pallas kernels  198 us (44%)
  waiting for transfers between devices  87.9 us (20%)
  starting transfers between devices  60.5 us (14%)
  local copies, waits for them, and re-layouts  37.9 us (8%)
  other arithmetic  36.5 us (8%)
  between operations  15.8 us (4%)
    ppermute x47, waiting for transfers between devices, send(): return lax.ppermute(values, AXES, table)  87.8 us
    pallas_call x3, Pallas kernels, attention_backward(): pl.pallas_call(functools.partial(backward_kernel, block), grid_spec=pltpu...  72.3 us
    ppermute x47, starting transfers between devices, send(): return lax.ppermute(values, AXES, table)  60.4 us
    pallas_call x1, Pallas kernels, experts(): pl.pallas_call(experts_kernel, grid_spec=pltpu.PrefetchScalarGridSpec(num...  56.3 us
    pallas_call x1, Pallas kernels, attention_forward(): pl.pallas_call(attention_kernel, grid_spec=pltpu.PrefetchScalarGridSpec(n...  34.1 us
    pallas_call x7, Pallas kernels, assemble(): pl.pallas_call(functools.partial(assemble_kernel, first), grid_spec=pltpu...  19.4 us
    pallas_call x1, Pallas kernels, experts_output(): pl.pallas_call(output_kernel, grid_spec=pltpu.PrefetchScalarGridSpec(num_...  15.9 us
    unnamed x105, local copies, waits for them, and re-layouts  14.8 us
  transfers between devices with their start and end apart: 50, of which 19 were waited for; matrix products, arithmetic and copies ran while one was open for 13% of the time, Pallas kernels for 24%

profile of v5, /device:TPU:0, one launch (start us, length us, event | category | flops | bytes accessed | tf_op | source)
XLA Modules:
  0.0 439.5 jit_solution(8448701986887122152)
XLA Ops:
  8.1 2.3 convolution_bitcast_fusion
  10.6 3.2 collective-permute-start.1
  13.8 14.6 %collective-permute-done.1.over = f32[424,384]{1,0:T(8,128)S(1)} collective-permute-done((f32[424,384]{1,0:T(8,128)S(1)}, f32[424,384]{1,0:T(8,128)S(1)}, u32[]{:S(2)}, u32[]{:S(2)}) %collective-permute-start.1) | collective-permute-done | bytes 651296 | tf_op jit(solution)/shard_map/ppermute | solution.py:737
  33.0 2.1 copy.87.ids_ref
  38.5 34.1 %attention_forward.1 = (f32[2352,384]{1,0:T(8,128)}, f32[2352,384]{1,0:T(8,128)}, f32[2352,384]{1,0:T(8,128)}, f32[2352,1]{1,0:T(8,128)}, bf16[2352,384]{1,0:T(8...) custom-call(s32[2]{0:T(128)} %pad_add_fusion.1.core, ...), custom_call_target="tpu_custom_call" | custom-call | flops 1000000 | bytes 100000 | tf_op jit(solution)/shard_map/attention_forward/pallas_call | solution.py:220
  79.7 56.3 %experts.1 = (f32[3072,384]{1,0:T(8,128)}, f32[3072,384]{1,0:T(8,128)}, f32[8,384]{1,0:T(8,128)}, f32[8,384]{1,0:T(8,128)}, bf16[7680,384]{1,0:T(8,128)(2,1)}, /...) custom-call(s32[1]{0:T(128)} %bitcast.core, ...), custom_call_target="tpu_custom_call" | custom-call | flops 1000000 | bytes 100000 | tf_op jit(solution)/shard_map/experts/pallas_call | solution.py:395
  137.6 2.8 fusion.28
  143.3 1.8 slice_add_fusion.2
  146.2 3.3 collective-permute-start.11
  149.5 1.6 collective-permute-start.6
  151.1 1.9 collective-permute-start.7
  153.1 1.7 collective-permute-start.8
  154.7 2.5 collective-permute-start.9
  157.2 2.6 slice_add_fusion
  162.1 15.9 %experts_output.1 = (f32[14,168,384]{2,1,0:T(8,128)}, f32[14,168,384]{2,1,0:T(8,128)}) custom-call(s32[1]{0:T(128)} %bitcast.core, s32[784]{0:T(1024)} %select_n.305.dest, s32[8]{0:T(128)} %and_select_fusion.chunks, bf16[7680,384]{1,0:T(8,128)(2,1)} %get-tuple-element.148.act_ref, s32[28,2,168]{2,1,0:T(2,128)} %pad_add_fusion.meta_ref, ...), custom_call_target="tpu_custom_call" | custom-call | flops 1000000 | bytes 100000 | tf_op jit(solution)/shard_map/experts_output/pallas_call | solution.py:476
  178.5 1.8 collective-permute-start.10
  180.3 1.7 collective-permute-start.15
  182.7 23.9 %attention_backward.3 = (f32[784,384]{1,0:T(8,128)}, f32[1152,384]{1,0:T(8,128)}, f32[384,384]{1,0:T(8,128)}, f32[16,384]{1,0:T(8,128)}, f32[192,256]{1,0:T(8,128)}) custom-call(s32[1]{0:T(128)} %bitcast.core, f32[792,384]{1,0:T(8,128)} %pad_maximum_fusion.gs_a, f32[792,384]{1,0:T(8,128)} %collective-permute-done.11.gs_b, ...), custom_call_target="tpu_custom_call" | custom-call | flops 1000000 | bytes 100000 | tf_op jit(solution)/shard_map/attention_backward/pallas_call | solution.py:654
  206.6 3.2 collective-permute-done.10.gs_b
  209.9 2.8 collective-permute-start.14
  212.6 2.2 collective-permute-start.13
  214.8 3.5 add.468
  221.4 3.0 collective-permute-start.19
  224.4 24.1 %attention_backward.4 = (f32[784,384]{1,0:T(8,128)}, f32[1152,384]{1,0:T(8,128)}, f32[384,384]{1,0:T(8,128)}, f32[16,384]{1,0:T(8,128)}, f32[192,256]{1,0:T(8,128)}) custom-call(s32[1]{0:T(128)} %bitcast.core, f32[792,384]{1,0:T(8,128)} %pad_maximum_fusion.1.gs_a, f32[792,384]{1,0:T(8,128)} %collective-permute-done.10.gs_b, ...), custom_call_target="tpu_custom_call" | custom-call | flops 1000000 | bytes 100000 | tf_op jit(solution)/shard_map/attention_backward/pallas_call | solution.py:654
  248.6 2.4 fusion.7
  253.6 1.8 collective-permute-start.17
  256.2 24.2 %attention_backward.5 = (f32[784,384]{1,0:T(8,128)}, f32[1152,384]{1,0:T(8,128)}, f32[384,384]{1,0:T(8,128)}, f32[16,384]{1,0:T(8,128)}, f32[192,256]{1,0:T(8,128)}, /*index=5*/f32[768,64]{1,0:T(8,128)}) custom-call(s32[1]{0:T(128)} %bitcast.core, f32[792,384]{1,0:T(8,128)} %pad_maximum_fusion.2.gs_a, f32[792,384]{1,0:T(8,128)} %collective-permute-done.15.gs_b, ...), custom_call_target="tpu_custom_call" | custom-call | flops 1000000 | bytes 100000 | tf_op jit(solution)/shard_map/attention_backward/pallas_call | solution.py:654
  280.5 1.9 add.543
  282.6 2.1 collective-permute-start.23
  287.0 1.4 fusion.5
  289.5 1.9 collective-permute-start.22
  292.4 1.5 multiply_add_fusion.3.mine
  295.4 11.2 %collective-permute-done.23 = f32[672,384]{1,0:T(8,128)} collective-permute-done((f32[672,384]{1,0:T(8,128)S(1)}, f32[672,384]{1,0:T(8,128)}, u32[]{:S(2)}, u32[]{:S(2)}) %collective-permute-start.23) | collective-permute-done | bytes 1032224 | tf_op jit(solution)/shard_map/ppermute | solution.py:737
  308.5 1.8 collective-permute-start.30
  311.1 7.2 %collective-permute-done.30 = f32[192,384]{1,0:T(8,128)S(1)} collective-permute-done((f32[192,384]{1,0:T(8,128)S(1)}, f32[192,384]{1,0:T(8,128)S(1)}, u32[]{:S(2)}, u32[]{:S(2)}) %collective-permute-start.30) | collective-permute-done | bytes 294944 | tf_op jit(solution)/shard_map/ppermute | solution.py:737
  319.2 1.4 collective-permute-start.24
  321.4 2.3 collective-permute-start.25
  323.7 1.8 multiply_add_fusion.1.mine
  325.6 7.6 %collective-permute-done.24 = f32[128,384]{1,0:T(8,128)S(1)} collective-permute-done((f32[128,384]{1,0:T(8,128)S(1)}, f32[128,384]{1,0:T(8,128)S(1)}, u32[]{:S(2)}, u32[]{:S(2)}) %collective-permute-start.24) | collective-permute-done | bytes 196640 | tf_op jit(solution)/shard_map/ppermute | solution.py:737
  333.2 6.2 %collective-permute-done.26 = f32[128,384]{1,0:T(8,128)S(1)} collective-permute-done((f32[128,384]{1,0:T(8,128)S(1)}, f32[128,384]{1,0:T(8,128)S(1)}, u32[]{:S(2)}, u32[]{:S(2)}) %collective-permute-start.26) | collective-permute-done | bytes 196640 | tf_op jit(solution)/shard_map/ppermute | solution.py:737
  339.4 1.8 collective-permute-done.25
  341.2 2.0 assemble.9.refs_0_
  343.2 3.2 assemble.7.refs_0_
  346.4 3.2 assemble.8.refs_0_
  349.8 2.1 collective-permute-start.35
  353.4 2.1 collective-permute-start.32
  355.6 2.1 collective-permute-done.31
  358.7 14.1 %collective-permute-done.35 = f32[560,384]{1,0:T(8,128)S(1)} collective-permute-done((f32[560,384]{1,0:T(8,128)S(1)}, f32[560,384]{1,0:T(8,128)S(1)}, u32[]{:S(2)}, u32[]{:S(2)}) %collective-permute-start.35) | collective-permute-done | bytes 860192 | tf_op jit(solution)/shard_map/ppermute | solution.py:737
  373.8 1.4 collective-permute-start.36
  375.2 1.4 multiply_add_fusion.2.mine
  378.9 2.1 collective-permute-start.37
  381.9 2.4 collective-permute-start.40
  384.3 6.4 %collective-permute-done.39 = f32[32,384]{1,0:T(8,128)S(1)} collective-permute-done((f32[32,384]{1,0:T(8,128)S(1)}, f32[32,384]{1,0:T(8,128)S(1)}, u32[]{:S(2)}, u32[]{:S(2)}) %collective-permute-start.39) | collective-permute-done | bytes 49184 | tf_op jit(solution)/shard_map/ppermute | solution.py:737
  391.1 2.7 assemble.10.refs_0_
  393.8 2.2 collective-permute-start.45
  396.0 2.5 collective-permute-start.44
  398.6 7.1 %collective-permute-done.43 = f32[128,384]{1,0:T(8,128)} collective-permute-done((f32[128,384]{1,0:T(8,128)S(1)}, f32[128,384]{1,0:T(8,128)}, u32[]{:S(2)}, u32[]{:S(2)}) %collective-permute-start.43) | collective-permute-done | bytes 196640 | tf_op jit(solution)/shard_map/ppermute | solution.py:737
  406.6 1.3 collective-permute-done.44
  409.4 1.9 multiply_add_fusion.mine
  414.7 3.2 assemble.13
  417.8 2.4 assemble.11.refs_0_
  422.5 2.7 assemble.12
  425.3 5.0 %copy.116 = f32[8,384,384]{2,1,0:T(8,128)} copy(f32[8,384,384]{2,1,0:T(8,128)} %bitcast.109) | data formatting | bytes 9437184
  430.4 2.2 copy.117
  (304 shorter events, 56.6 us)
Async XLA Ops:
  7.2 241.4 %reduce-scatter.2.cloned.1.call-start = ((), (), s32[]{:S(2)}) async-start(), calls=%async_computation.1 | async-start | bytes 5013504 | tf_op jit(solution)/shard_map/reduce_scatter | solution.py:908
  8.0 22.7 %copy-start.47 = (bf16[384]{0:T(512)(128)(2,1)S(1)}, bf16[384]{0:T(512)(128)(2,1)}, u32[]{:S(2)}) copy-start(bf16[384]{0:T(512)(128)(2,1)} %param.35) | copy-start | bytes 2308
  8.1 23.2 %copy-start.39 = (bf16[384,8]{0,1:T(8,128)(2,1)S(1)}, bf16[384,8]{0,1:T(8,128)(2,1)}, u32[]{:S(2)}) copy-start(bf16[384,8]{0,1:T(8,128)(2,1)} %param.38) | copy-start | bytes 18436
  8.1 23.4 %copy-start.40 = (bf16[8,384]{1,0:T(8,128)(2,1)S(1)}, bf16[8,384]{1,0:T(8,128)(2,1)}, u32[]{:S(2)}) copy-start(bf16[8,384]{1,0:T(8,128)(2,1)} %param.42) | copy-start | bytes 18436
  8.1 24.9 %copy-start.30 = (s32[4704,1]{0,1:T(1,128)S(1)}, s32[4704,1]{0,1:T(1,128)}, u32[]{:S(2)}) copy-start(s32[4704,1]{0,1:T(1,128)} %param.43) | copy-start | bytes 56452
  10.6 25.4 %copy-start.9 = (f32[424,384]{1,0:T(8,128)}, f32[424,384]{1,0:T(8,128)S(1)}, u32[]{:S(2)}) copy-start(f32[424,384]{1,0:T(8,128)S(1)} %pad_maximum_fusion.7.own) | copy-start | bytes 1953796
  10.6 17.8 %collective-permute-start.1 = (f32[424,384]{1,0:T(8,128)S(1)}, f32[424,384]{1,0:T(8,128)S(1)}, u32[]{:S(2)}, u32[]{:S(2)}) collective-permute-start(f32[424,384]{1,0:T(8,128)S(1)} %pad_maximum_fusion.7.own), channel_id=1, source_target_pairs={{0,2},{1,3},{4,6},{5,7},{8,10},{9,11},{12,14},{13,15},{16,18},{17,... | collective-permute-start | bytes 1953800 | tf_op jit(solution)/shard_map/ppermute | solution.py:737
  13.8 22.0 %collective-permute-start = (f32[424,384]{1,0:T(8,128)S(1)}, f32[424,384]{1,0:T(8,128)S(1)}, u32[]{:S(2)}, u32[]{:S(2)}) collective-permute-start(f32[424,384]{1,0:T(8,128)S(1)} %pad_maximum_fusion.7.own), channel_id=1, source_target_pairs={{0,1},{1,0},{4,5},{5,4},{8,9},{9,8},{12,13},{13,12},{16,17},{17,16... | collective-permute-start | bytes 1953800 | tf_op jit(solution)/shard_map/ppermute | solution.py:737
  28.4 7.4 %collective-permute-start.2 = (f32[424,384]{1,0:T(8,128)S(1)}, f32[424,384]{1,0:T(8,128)S(1)}, u32[]{:S(2)}, u32[]{:S(2)}) collective-permute-start(f32[424,384]{1,0:T(8,128)S(1)} %collective-permute-done.1.over), channel_id=1, source_target_pairs={{0,1},{1,0},{4,5},{5,4},{8,9},{9,8},{12,13},{13,12},{16,17},{17,16... | collective-permute-start | bytes 1953800 | tf_op jit(solution)/shard_map/ppermute | solution.py:737
  38.5 35.2 %copy-start.41 = (bf16[8,384]{1,0:T(8,128)(2,1)S(1)}, bf16[8,384]{1,0:T(8,128)(2,1)}, u32[]{:S(2)}) copy-start(bf16[8,384]{1,0:T(8,128)(2,1)} %param.40) | copy-start | bytes 18436
  38.5 36.0 %copy-start.42 = (s32[8,8]{1,0:T(8,128)S(1)}, s32[8,8]{1,0:T(8,128)}, u32[]{:S(2)}) copy-start(s32[8,8]{1,0:T(8,128)} %constant.329.clone) | copy-start | bytes 772
  38.5 36.3 %copy-start.48 = (bf16[168,168,1]{1,0,2:T(8,128)(2,1)S(1)}, bf16[168,168,1]{1,0,2:T(8,128)(2,1)}, u32[]{:S(2)}) copy-start(bf16[168,168,1]{1,0,2:T(8,128)(2,1)} %constant.467) | copy-start | bytes 169348
  38.5 36.6 %copy-start.34 = (s32[28,28]{1,0:T(8,128)S(1)}, s32[28,28]{1,0:T(8,128)}, u32[]{:S(2)}) copy-start(s32[28,28]{1,0:T(8,128)} %constant.330.clone) | copy-start | bytes 9412
  72.7 7.1 %collective-permute-start.3 = (f32[14,168,384]{2,1,0:T(8,128)}, f32[14,168,384]{2,1,0:T(8,128)}, u32[]{:S(2)}, u32[]{:S(2)}) collective-permute-start(f32[14,168,384]{2,1,0:T(8,128)} %bitcast.115), channel_id=1, source_target_pairs={{0,1},{1,0},{4,5},{5,4},{8,9},{9,8},{12,13},{13,12},{16,17},{17,16... | collective-permute-start | bytes 10838024 | tf_op jit(solution)/shard_map/ppermute | solution.py:737
  79.1 203.5 %copy-start.32 = (f32[2352]{0:T(1024)}, f32[2352]{0:T(1024)S(1)}, u32[]{:S(2)}) copy-start(f32[2352]{0:T(1024)S(1)} %reduce) | copy-start | bytes 28228
  136.1 7.3 %collective-permute-start.4 = (f32[14,168,384]{2,1,0:T(8,128)}, f32[14,168,384]{2,1,0:T(8,128)}, u32[]{:S(2)}, u32[]{:S(2)}) collective-permute-start(f32[14,168,384]{2,1,0:T(8,128)} %get-tuple-element.140), channel_id=1, source_target_pairs={{0,1},{1,0},{4,5},{5,4},{8,9},{9,8},{12,13},{13,12},{16,17},{17,16... | collective-permute-start | bytes 10838024 | tf_op jit(solution)/shard_map/ppermute | solution.py:737
  136.6 288.7 %all-gather.5.cloned.1.call-start = ((), (), s32[]{:S(2)}) async-start(), calls=%async_computation.3 | async-start | bytes 5013504 | tf_op jit(solution)/shard_map/all_gather | solution.py:907
  137.4 5.8 %collective-permute-start.5 = (f32[2352]{0:T(1024)S(1)}, f32[2352]{0:T(1024)S(1)}, u32[]{:S(2)}, u32[]{:S(2)}) collective-permute-start(f32[2352]{0:T(1024)S(1)} %reshape.290), channel_id=1, source_target_pairs={{0,1},{1,0},{4,5},{5,4},{8,9},{9,8},{12,13},{13,12},{16,17},{17,16... | collective-permute-start | bytes 28232 | tf_op jit(solution)/shard_map/ppermute | solution.py:737
  146.2 32.3 %collective-permute-start.11 = (f32[792,384]{1,0:T(8,128)}, f32[792,384]{1,0:T(8,128)}, u32[]{:S(2)}, u32[]{:S(2)}) collective-permute-start(f32[792,384]{1,0:T(8,128)} %pad_maximum_fusion.gs_a), channel_id=1, source_target_pairs={{0,2},{1,3},{4,6},{5,7},{8,10},{9,11},{12,14},{13,15},{16,18},{17,... | collective-permute-start | bytes 3649544 | tf_op jit(solution)/shard_map/ppermute | solution.py:737
  149.5 28.4 %collective-permute-start.6 = (f32[4,96,384]{2,1,0:T(8,128)}, f32[4,96,384]{2,1,0:T(8,128)S(1)}, u32[]{:S(2)}, u32[]{:S(2)}) collective-permute-start(f32[4,96,384]{2,1,0:T(8,128)} %get-tuple-element.151), channel_id=1, source_target_pairs={{0,16},{1,17},{4,20},{5,21},{8,24},{9,25},{12,28},{13,29},{16,32},... | collective-permute-start | bytes 1769480 | tf_op jit(solution)/shard_map/ppermute | solution.py:737
  151.1 26.8 %collective-permute-start.7 = (f32[4,96,384]{2,1,0:T(8,128)}, f32[4,96,384]{2,1,0:T(8,128)}, u32[]{:S(2)}, u32[]{:S(2)}) collective-permute-start(f32[4,96,384]{2,1,0:T(8,128)} %get-tuple-element.152), channel_id=1, source_target_pairs={{0,4},{1,5},{4,8},{5,9},{8,12},{9,13},{12,0},{13,1},{16,20},{17,21... | collective-permute-start | bytes 1769480 | tf_op jit(solution)/shard_map/ppermute | solution.py:737
  153.1 24.9 %collective-permute-start.8 = (f32[4,96,384]{2,1,0:T(8,128)}, f32[4,96,384]{2,1,0:T(8,128)}, u32[]{:S(2)}, u32[]{:S(2)}) collective-permute-start(f32[4,96,384]{2,1,0:T(8,128)} %get-tuple-element.153), channel_id=1, source_target_pairs={{0,48},{1,49},{4,52},{5,53},{8,56},{9,57},{12,60},{13,61},{16,0},{... | collective-permute-start | bytes 1769480 | tf_op jit(solution)/shard_map/ppermute | solution.py:737
  154.7 23.8 %collective-permute-start.9 = (f32[4,96,384]{2,1,0:T(8,128)}, f32[4,96,384]{2,1,0:T(8,128)}, u32[]{:S(2)}, u32[]{:S(2)}) collective-permute-start(f32[4,96,384]{2,1,0:T(8,128)} %get-tuple-element.154), channel_id=1, source_target_pairs={{0,12},{1,13},{4,0},{5,1},{8,4},{9,5},{12,8},{13,9},{16,28},{17,29... | collective-permute-start | bytes 1769480 | tf_op jit(solution)/shard_map/ppermute | solution.py:737
  177.9 28.7 %copy-start.24 = (f32[4,96,384]{2,1,0:T(8,128)}, f32[4,96,384]{2,1,0:T(8,128)S(1)}, u32[]{:S(2)}) copy-start(f32[4,96,384]{2,1,0:T(8,128)S(1)} %collective-permute-done.6) | copy-start | bytes 1769476
  178.5 31.4 %collective-permute-start.12 = (f32[14,168,384]{2,1,0:T(8,128)}, f32[14,168,384]{2,1,0:T(8,128)}, u32[]{:S(2)}, u32[]{:S(2)}) collective-permute-start(f32[14,168,384]{2,1,0:T(8,128)} %get-tuple-element.171), channel_id=1, source_target_pairs={{0,1},{1,0},{4,5},{5,4},{8,9},{9,8},{12,13},{13,12},{16,17},{17,16... | collective-permute-start | bytes 10838024 | tf_op jit(solution)/shard_map/ppermute | solution.py:737
  178.5 31.4 %collective-permute-start.10 = (f32[792,384]{1,0:T(8,128)}, f32[792,384]{1,0:T(8,128)}, u32[]{:S(2)}, u32[]{:S(2)}) collective-permute-start(f32[792,384]{1,0:T(8,128)} %pad_maximum_fusion.1.gs_a), channel_id=1, source_target_pairs={{0,2},{1,3},{4,6},{5,7},{8,10},{9,11},{12,14},{13,15},{16,18},{17,... | collective-permute-start | bytes 3649544 | tf_op jit(solution)/shard_map/ppermute | solution.py:737
  180.3 68.2 %collective-permute-start.15 = (f32[792,384]{1,0:T(8,128)}, f32[792,384]{1,0:T(8,128)}, u32[]{:S(2)}, u32[]{:S(2)}) collective-permute-start(f32[792,384]{1,0:T(8,128)} %pad_maximum_fusion.2.gs_a), channel_id=1, source_target_pairs={{0,2},{1,3},{4,6},{5,7},{8,10},{9,11},{12,14},{13,15},{16,18},{17,... | collective-permute-start | bytes 3649544 | tf_op jit(solution)/shard_map/ppermute | solution.py:737
  209.9 38.7 %collective-permute-start.14 = (f32[4,96,384]{2,1,0:T(8,128)}, f32[4,96,384]{2,1,0:T(8,128)}, u32[]{:S(2)}, u32[]{:S(2)}) collective-permute-start(f32[4,96,384]{2,1,0:T(8,128)} %get-tuple-element.180), channel_id=1, source_target_pairs={{0,8},{1,9},{4,12},{5,13},{8,0},{9,1},{12,4},{13,5},{16,24},{17,25... | collective-permute-start | bytes 1769480 | tf_op jit(solution)/shard_map/ppermute | solution.py:737
  212.6 35.9 %collective-permute-start.13 = (f32[4,96,384]{2,1,0:T(8,128)}, f32[4,96,384]{2,1,0:T(8,128)}, u32[]{:S(2)}, u32[]{:S(2)}) collective-permute-start(f32[4,96,384]{2,1,0:T(8,128)} %get-tuple-element.178), channel_id=1, source_target_pairs={{0,32},{1,33},{4,36},{5,37},{8,40},{9,41},{12,44},{13,45},{16,48},... | collective-permute-start | bytes 1769480 | tf_op jit(solution)/shard_map/ppermute | solution.py:737
  221.4 59.0 %collective-permute-start.19 = (f32[336,384]{1,0:T(8,128)}, f32[336,384]{1,0:T(8,128)}, u32[]{:S(2)}, u32[]{:S(2)}) collective-permute-start(f32[336,384]{1,0:T(8,128)} %bitcast.21), channel_id=1, source_target_pairs={{0,2},{1,3},{4,6},{5,7},{8,10},{9,11},{12,14},{13,15},{16,18},{17,... | collective-permute-start | bytes 1548296 | tf_op jit(solution)/shard_map/ppermute | solution.py:737
  251.8 28.6 %collective-permute-start.16 = (f32[2,96,384]{2,1,0:T(8,128)}, f32[2,96,384]{2,1,0:T(8,128)}, u32[]{:S(2)}, u32[]{:S(2)}) collective-permute-start(f32[2,96,384]{2,1,0:T(8,128)} %pad_maximum_fusion.9), channel_id=1, source_target_pairs={{0,4},{1,5},{4,0},{5,1},{8,12},{9,13},{12,8},{13,9},{16,20},{17,21... | collective-permute-start | bytes 884744 | tf_op jit(solution)/shard_map/ppermute | solution.py:737
  253.6 26.8 %collective-permute-start.17 = (f32[2,96,384]{2,1,0:T(8,128)}, f32[2,96,384]{2,1,0:T(8,128)}, u32[]{:S(2)}, u32[]{:S(2)}) collective-permute-start(f32[2,96,384]{2,1,0:T(8,128)} %pad_maximum_fusion.10), channel_id=1, source_target_pairs={{0,16},{1,17},{4,20},{5,21},{8,24},{9,25},{12,28},{13,29},{16,0},{... | collective-permute-start | bytes 884744 | tf_op jit(solution)/shard_map/ppermute | solution.py:737
  255.4 25.1 %collective-permute-start.18 = (f32[192,384]{1,0:T(8,128)S(1)}, f32[192,384]{1,0:T(8,128)}, u32[]{:S(2)}, u32[]{:S(2)}) collective-permute-start(f32[192,384]{1,0:T(8,128)S(1)} %copy-done.26), channel_id=1, source_target_pairs={{0,64},{1,65},{4,68},{5,69},{8,72},{9,73},{12,76},{13,77},{16,80},... | collective-permute-start | bytes 884744 | tf_op jit(solution)/shard_map/ppermute | solution.py:737
  282.4 142.9 %all-gather.3.cloned.1.call-start = ((), (), s32[]{:S(2)}) async-start(), calls=%async_computation.2 | async-start | bytes 5013504 | tf_op jit(solution)/shard_map/all_gather | solution.py:907
  282.6 24.0 %collective-permute-start.23 = (f32[672,384]{1,0:T(8,128)S(1)}, f32[672,384]{1,0:T(8,128)}, u32[]{:S(2)}, u32[]{:S(2)}) collective-permute-start(f32[672,384]{1,0:T(8,128)S(1)} %bitcast.111), channel_id=1, source_target_pairs={{0,2},{1,3},{4,6},{5,7},{8,10},{9,11},{12,14},{13,15},{16,18},{17,... | collective-permute-start | bytes 3096584 | tf_op jit(solution)/shard_map/ppermute | solution.py:737
  284.6 25.7 %collective-permute-start.27 = (f32[784,384]{1,0:T(8,128)}, f32[784,384]{1,0:T(8,128)}, u32[]{:S(2)}, u32[]{:S(2)}) collective-permute-start(f32[784,384]{1,0:T(8,128)} %get-tuple-element.217.mine), channel_id=1, source_target_pairs={{0,1},{1,0},{4,5},{5,4},{8,9},{9,8},{12,13},{13,12},{16,17},{17,16... | collective-permute-start | bytes 3612680 | tf_op jit(solution)/shard_map/ppermute | solution.py:737
  284.6 26.5 %collective-permute-start.28 = (f32[784,384]{1,0:T(8,128)}, f32[784,384]{1,0:T(8,128)}, u32[]{:S(2)}, u32[]{:S(2)}) collective-permute-start(f32[784,384]{1,0:T(8,128)} %get-tuple-element.216.mine), channel_id=1, source_target_pairs={{0,1},{1,0},{4,5},{5,4},{8,9},{9,8},{12,13},{13,12},{16,17},{17,16... | collective-permute-start | bytes 3612680 | tf_op jit(solution)/shard_map/ppermute | solution.py:737
  288.5 5.4 %collective-permute-start.20 = (f32[408,384]{1,0:T(8,128)S(1)}, f32[408,384]{1,0:T(8,128)S(1)}, u32[]{:S(2)}, u32[]{:S(2)}) collective-permute-start(f32[408,384]{1,0:T(8,128)S(1)} %pad_maximum_fusion.3), channel_id=1, source_target_pairs={{0,1},{1,0},{4,5},{5,4},{8,9},{9,8},{12,13},{13,12},{16,17},{17,16... | collective-permute-start | bytes 1880072 | tf_op jit(solution)/shard_map/ppermute | solution.py:737
  289.5 17.0 %collective-permute-start.22 = (f32[96,384]{1,0:T(8,128)S(1)}, f32[96,384]{1,0:T(8,128)S(1)}, u32[]{:S(2)}, u32[]{:S(2)}) collective-permute-start(f32[96,384]{1,0:T(8,128)S(1)} %add_bitcast_fusion), channel_id=1, source_target_pairs={{0,32},{1,33},{4,36},{5,37},{8,40},{9,41},{12,44},{13,45},{16,48},... | collective-permute-start | bytes 442376 | tf_op jit(solution)/shard_map/ppermute | solution.py:737
  293.9 12.7 %collective-permute-start.21 = (f32[96,384]{1,0:T(8,128)S(1)}, f32[96,384]{1,0:T(8,128)S(1)}, u32[]{:S(2)}, u32[]{:S(2)}) collective-permute-start(f32[96,384]{1,0:T(8,128)S(1)} %add_bitcast_fusion.1), channel_id=1, source_target_pairs={{0,8},{1,9},{4,12},{5,13},{8,0},{9,1},{12,4},{13,5},{16,24},{17,25... | collective-permute-start | bytes 442376 | tf_op jit(solution)/shard_map/ppermute | solution.py:737
  295.2 23.8 %copy-start.33 = (f32[2352]{0:T(1024)S(1)}, f32[2352]{0:T(1024)}, u32[]{:S(2)}) copy-start(f32[2352]{0:T(1024)} %copy-done.32) | copy-start | bytes 28228
  306.6 3.7 collective-permute-start.29
  308.5 9.7 %collective-permute-start.30 = (f32[192,384]{1,0:T(8,128)S(1)}, f32[192,384]{1,0:T(8,128)S(1)}, u32[]{:S(2)}, u32[]{:S(2)}) collective-permute-start(f32[192,384]{1,0:T(8,128)S(1)} %pad_maximum_fusion.11), channel_id=1, source_target_pairs={{0,64},{1,65},{4,68},{5,69},{8,72},{9,73},{12,76},{13,77},{16,80},... | collective-permute-start | bytes 884744 | tf_op jit(solution)/shard_map/ppermute | solution.py:737
  319.2 14.0 %collective-permute-start.24 = (f32[128,384]{1,0:T(8,128)S(1)}, f32[128,384]{1,0:T(8,128)S(1)}, u32[]{:S(2)}, u32[]{:S(2)}) collective-permute-start(f32[128,384]{1,0:T(8,128)S(1)} %get-tuple-element.329), channel_id=1, source_target_pairs={{0,16},{1,17},{4,20},{5,21},{8,24},{9,25},{12,28},{13,29},{16,32},... | collective-permute-start | bytes 589832 | tf_op jit(solution)/shard_map/ppermute | solution.py:737
  320.6 18.8 %collective-permute-start.26 = (f32[128,384]{1,0:T(8,128)S(1)}, f32[128,384]{1,0:T(8,128)S(1)}, u32[]{:S(2)}, u32[]{:S(2)}) collective-permute-start(f32[128,384]{1,0:T(8,128)S(1)} %get-tuple-element.330), channel_id=1, source_target_pairs={{0,32},{1,33},{4,36},{5,37},{8,40},{9,41},{12,44},{13,45},{16,48},... | collective-permute-start | bytes 589832 | tf_op jit(solution)/shard_map/ppermute | solution.py:737
  321.4 19.7 %collective-permute-start.25 = (f32[128,384]{1,0:T(8,128)S(1)}, f32[128,384]{1,0:T(8,128)S(1)}, u32[]{:S(2)}, u32[]{:S(2)}) collective-permute-start(f32[128,384]{1,0:T(8,128)S(1)} %get-tuple-element.331), channel_id=1, source_target_pairs={{0,48},{1,49},{4,52},{5,53},{8,56},{9,57},{12,60},{13,61},{16,0},{... | collective-permute-start | bytes 589832 | tf_op jit(solution)/shard_map/ppermute | solution.py:737
  325.6 24.1 %copy-start.6 = (f32[672,384]{1,0:T(8,128)}, f32[672,384]{1,0:T(8,128)S(1)}, u32[]{:S(2)}) copy-start(f32[672,384]{1,0:T(8,128)S(1)} %multiply_add_fusion.1.mine) | copy-start | bytes 3096580
  349.6 29.3 %copy-start.3 = (f32[784,384]{1,0:T(8,128)S(1)}, f32[784,384]{1,0:T(8,128)}, u32[]{:S(2)}) copy-start(f32[784,384]{1,0:T(8,128)} %slice.268) | copy-start | bytes 3612676
  349.6 23.1 %collective-permute-start.34 = (f32[672,384]{1,0:T(8,128)S(1)}, f32[672,384]{1,0:T(8,128)S(1)}, u32[]{:S(2)}, u32[]{:S(2)}) collective-permute-start(f32[672,384]{1,0:T(8,128)S(1)} %multiply_add_fusion.1.mine), channel_id=1, source_target_pairs={{0,1},{1,0},{4,5},{5,4},{8,9},{9,8},{12,13},{13,12},{16,17},{17,16... | collective-permute-start | bytes 3096584 | tf_op jit(solution)/shard_map/ppermute | solution.py:737
  349.8 23.0 %collective-permute-start.35 = (f32[560,384]{1,0:T(8,128)S(1)}, f32[560,384]{1,0:T(8,128)S(1)}, u32[]{:S(2)}, u32[]{:S(2)}) collective-permute-start(f32[560,384]{1,0:T(8,128)S(1)} %copy-done.7), channel_id=1, source_target_pairs={{0,2},{1,3},{4,6},{5,7},{8,10},{9,11},{12,14},{13,15},{16,18},{17,... | collective-permute-start | bytes 2580488 | tf_op jit(solution)/shard_map/ppermute | solution.py:737
  351.9 5.8 %collective-permute-start.31 = (f32[32,384]{1,0:T(8,128)S(1)}, f32[32,384]{1,0:T(8,128)S(1)}, u32[]{:S(2)}, u32[]{:S(2)}) collective-permute-start(f32[32,384]{1,0:T(8,128)S(1)} %get-tuple-element.336), channel_id=1, source_target_pairs={{0,4},{1,5},{4,8},{5,9},{8,12},{9,13},{12,0},{13,1},{16,20},{17,21... | collective-permute-start | bytes 147464 | tf_op jit(solution)/shard_map/ppermute | solution.py:737
  352.6 5.6 %collective-permute-start.33 = (f32[32,384]{1,0:T(8,128)S(1)}, f32[32,384]{1,0:T(8,128)S(1)}, u32[]{:S(2)}, u32[]{:S(2)}) collective-permute-start(f32[32,384]{1,0:T(8,128)S(1)} %get-tuple-element.337), channel_id=1, source_target_pairs={{0,8},{1,9},{4,12},{5,13},{8,0},{9,1},{12,4},{13,5},{16,24},{17,25... | collective-permute-start | bytes 147464 | tf_op jit(solution)/shard_map/ppermute | solution.py:737
  353.4 5.2 %collective-permute-start.32 = (f32[32,384]{1,0:T(8,128)S(1)}, f32[32,384]{1,0:T(8,128)S(1)}, u32[]{:S(2)}, u32[]{:S(2)}) collective-permute-start(f32[32,384]{1,0:T(8,128)S(1)} %get-tuple-element.338), channel_id=1, source_target_pairs={{0,12},{1,13},{4,0},{5,1},{8,4},{9,5},{12,8},{13,9},{16,28},{17,29... | collective-permute-start | bytes 147464 | tf_op jit(solution)/shard_map/ppermute | solution.py:737
  372.8 5.1 %collective-permute-start.38 = (f32[784,384]{1,0:T(8,128)}, f32[784,384]{1,0:T(8,128)S(1)}, u32[]{:S(2)}, u32[]{:S(2)}) collective-permute-start(f32[784,384]{1,0:T(8,128)} %get-tuple-element.233.mine), channel_id=1, source_target_pairs={{0,1},{1,0},{4,5},{5,4},{8,9},{9,8},{12,13},{13,12},{16,17},{17,16... | collective-permute-start | bytes 3612680 | tf_op jit(solution)/shard_map/ppermute | solution.py:737
  373.8 4.1 collective-permute-start.36
  378.9 11.9 %collective-permute-start.42 = (f32[560,384]{1,0:T(8,128)S(1)}, f32[560,384]{1,0:T(8,128)S(1)}, u32[]{:S(2)}, u32[]{:S(2)}) collective-permute-start(f32[560,384]{1,0:T(8,128)S(1)} %multiply_add_fusion.2.mine), channel_id=1, source_target_pairs={{0,1},{1,0},{4,5},{5,4},{8,9},{9,8},{12,13},{13,12},{16,17},{17,16... | collective-permute-start | bytes 2580488 | tf_op jit(solution)/shard_map/ppermute | solution.py:737
  378.9 30.5 %collective-permute-start.37 = (f32[784,384]{1,0:T(8,128)S(1)}, f32[784,384]{1,0:T(8,128)}, u32[]{:S(2)}, u32[]{:S(2)}) collective-permute-start(f32[784,384]{1,0:T(8,128)S(1)} %copy-done.3), channel_id=1, source_target_pairs={{0,2},{1,3},{4,6},{5,7},{8,10},{9,11},{12,14},{13,15},{16,18},{17,... | collective-permute-start | bytes 3612680 | tf_op jit(solution)/shard_map/ppermute | solution.py:737
  381.0 9.8 %collective-permute-start.41 = (f32[32,384]{1,0:T(8,128)S(1)}, f32[32,384]{1,0:T(8,128)S(1)}, u32[]{:S(2)}, u32[]{:S(2)}) collective-permute-start(f32[32,384]{1,0:T(8,128)S(1)} %add.521), channel_id=1, source_target_pairs={{0,8},{1,9},{4,12},{5,13},{8,0},{9,1},{12,4},{13,5},{16,24},{17,25... | collective-permute-start | bytes 147464 | tf_op jit(solution)/shard_map/ppermute | solution.py:737
  381.9 8.8 %collective-permute-start.40 = (f32[32,384]{1,0:T(8,128)S(1)}, f32[32,384]{1,0:T(8,128)S(1)}, u32[]{:S(2)}, u32[]{:S(2)}) collective-permute-start(f32[32,384]{1,0:T(8,128)S(1)} %add.521), channel_id=1, source_target_pairs={{0,12},{1,13},{4,0},{5,1},{8,4},{9,5},{12,8},{13,9},{16,28},{17,29... | collective-permute-start | bytes 147464 | tf_op jit(solution)/shard_map/ppermute | solution.py:737
  384.3 6.4 %collective-permute-start.39 = (f32[32,384]{1,0:T(8,128)S(1)}, f32[32,384]{1,0:T(8,128)S(1)}, u32[]{:S(2)}, u32[]{:S(2)}) collective-permute-start(f32[32,384]{1,0:T(8,128)S(1)} %add.521), channel_id=1, source_target_pairs={{0,4},{1,5},{4,8},{5,9},{8,12},{9,13},{12,0},{13,1},{16,20},{17,21... | collective-permute-start | bytes 147464 | tf_op jit(solution)/shard_map/ppermute | solution.py:737
  390.8 14.9 %collective-permute-start.43 = (f32[128,384]{1,0:T(8,128)S(1)}, f32[128,384]{1,0:T(8,128)}, u32[]{:S(2)}, u32[]{:S(2)}) collective-permute-start(f32[128,384]{1,0:T(8,128)S(1)} %constant_dynamic-update-slice_fusion.4), channel_id=1, source_target_pairs={{0,16},{1,17},{4,20},{5,21},{8,24},{9,25},{12,28},{13,29},{16,32},... | collective-permute-start | bytes 589832 | tf_op jit(solution)/shard_map/ppermute | solution.py:737
  393.8 14.8 %collective-permute-start.45 = (f32[128,384]{1,0:T(8,128)S(1)}, f32[128,384]{1,0:T(8,128)S(1)}, u32[]{:S(2)}, u32[]{:S(2)}) collective-permute-start(f32[128,384]{1,0:T(8,128)S(1)} %constant_dynamic-update-slice_fusion.4), channel_id=1, source_target_pairs={{0,32},{1,33},{4,36},{5,37},{8,40},{9,41},{12,44},{13,45},{16,48},... | collective-permute-start | bytes 589832 | tf_op jit(solution)/shard_map/ppermute | solution.py:737
  396.0 12.0 %collective-permute-start.44 = (f32[128,384]{1,0:T(8,128)S(1)}, f32[128,384]{1,0:T(8,128)S(1)}, u32[]{:S(2)}, u32[]{:S(2)}) collective-permute-start(f32[128,384]{1,0:T(8,128)S(1)} %constant_dynamic-update-slice_fusion.4), channel_id=1, source_target_pairs={{0,48},{1,49},{4,52},{5,53},{8,56},{9,57},{12,60},{13,61},{16,0},{... | collective-permute-start | bytes 589832 | tf_op jit(solution)/shard_map/ppermute | solution.py:737
  411.4 10.1 %collective-permute-start.46 = (f32[784,384]{1,0:T(8,128)S(1)}, f32[784,384]{1,0:T(8,128)S(1)}, u32[]{:S(2)}, u32[]{:S(2)}) collective-permute-start(f32[784,384]{1,0:T(8,128)S(1)} %multiply_add_fusion.mine), channel_id=1, source_target_pairs={{0,1},{1,0},{4,5},{5,4},{8,9},{9,8},{12,13},{13,12},{16,17},{17,16... | collective-permute-start | bytes 3612680 | tf_op jit(solution)/shard_map/ppermute | solution.py:737
  (36 other events, 210.8 us)
Sparse Core Ops, SparseCore 0:
  136.7 94.2 reduce-scatter.1
  282.5 61.2 all-gather.4
  346.0 63.6 all-gather.2
